TPU v7x, 32 devices: a whole 2x2x4 slice. The times are simulated.
32 devices in a mesh: row: 2 (over x), col: 16 (over z, y, core).
Axes of the slice: x: 2, y: 2, z: 4, core: 2. Of those that a mesh axis runs over, the one named last changes fastest.
Arguments:
- image: float32 [2048, 1152], P(('row', 'col'))
- text: float32 [2048, 1152], P(('row', 'col'))
- labels: int32 [2048], P(('row', 'col')), may hold values from 0 to 2047, as said below
- log_scale: float32 [1], replicated, may hold values from 2 to 2.7
- bias: float32 [1], replicated, may hold values from -10.5 to -9.5
Outputs:
- loss: float32 [1], replicated
- grad_image: float32 [2048, 1152], P(('row', 'col'))
- grad_text: float32 [2048, 1152], P(('row', 'col'))
- grad_log_scale: float32 [1], replicated
- grad_bias: float32 [1], replicated
Inputs may be any that keep to these rules, and one draw needn't show every extreme that they name: `labels`: each text index 0 to 2047 appears exactly once.
All inputs are finite; a program needn't handle non-finite values.
Results may differ from a plain program's by a relative error of at most 0.0003.
Values sent between devices are 32-bit elements; how exact they have to be, the bound alone decides.
No kernel may reach another device: no remote copies, remote signals or barrier semaphores. Data moves between devices by JAX's collectives and lax.ppermute only.
A program may use at most 64 MiB of HBM per device.

v0:
```python
import jax
import jax.numpy as jnp
from jax import lax
from jax.sharding import PartitionSpec as P

EPSILON = 1e-06


def unit_rows(rows):
    norm = jnp.sqrt(jnp.sum(rows * rows, axis=1, keepdims=True) + EPSILON)
    return (rows / norm, norm)


def full_dot(left, right):
    return jnp.dot(left, right, precision=lax.Precision.HIGHEST, preferred_element_type=jnp.float32)


def per_device(image, text, labels, log_scale, bias):
    rows_dev = image.shape[0]
    n_row = lax.axis_size("row")
    n_col = lax.axis_size("col")
    row_at = lax.axis_index("row")
    pairs = rows_dev * n_row * n_col
    own_image, image_norm = unit_rows(image)
    own_text, text_norm = unit_rows(text)
    offsets = jnp.arange(rows_dev, dtype=jnp.int32)
    image_block, label_block = (
        lax.all_gather(image, "row", axis=0, tiled=True),
        lax.all_gather(labels, "row", axis=0, tiled=True),
    )
    text_block = lax.all_gather(text, "col", axis=0, tiled=True)
    text_ids = (
        (row_at * n_col + jnp.arange(n_col, dtype=jnp.int32)[:, None]) * rows_dev + offsets[None, :]
    ).reshape(-1)
    image_block = unit_rows(image_block)[0]
    text_block = unit_rows(text_block)[0]
    scale = jnp.exp(log_scale[0])
    cosine = full_dot(image_block, text_block.T)
    logit = scale * cosine + bias[0]
    positive = label_block[:, None] == text_ids[None, :]
    term = jnp.where(positive, jax.nn.softplus(-logit), jax.nn.softplus(logit))
    slope = jax.nn.sigmoid(logit) - positive.astype(jnp.float32)
    unit_grad_image = lax.psum_scatter(
        scale * full_dot(slope, text_block), "row", scatter_dimension=0, tiled=True
    )
    unit_grad_text = lax.psum_scatter(
        scale * full_dot(slope.T, image_block), "col", scatter_dimension=0, tiled=True
    )
    summed, slope_sum, product_sum = lax.psum(
        (jnp.sum(term), jnp.sum(slope), jnp.sum(slope * cosine)), ("row", "col")
    )
    grad_image = (
        unit_grad_image - own_image * jnp.sum(own_image * unit_grad_image, axis=1, keepdims=True)
    ) / image_norm
    grad_text = (
        unit_grad_text - own_text * jnp.sum(own_text * unit_grad_text, axis=1, keepdims=True)
    ) / text_norm
    loss = (summed / pairs).reshape(1)
    grad_log_scale = (scale * product_sum / pairs).reshape(1)
    grad_bias = (slope_sum / pairs).reshape(1)
    return (loss, grad_image, grad_text, grad_log_scale, grad_bias)


def solution(mesh):
    return jax.shard_map(
        per_device,
        mesh=mesh,
        in_specs=(P(("row", "col"), None), P(("row", "col"), None), P(("row", "col")), P(), P()),
        out_specs=(P(), P(("row", "col"), None), P(("row", "col"), None), P(), P()),
        check_vma=False,
    )
```

profile of v0, /device:TPU:0, one launch (start us, length us, event | category | flops | bytes accessed | tf_op | source)
XLA Modules:
  0.0 187.0 jit_solution(13610803505322977767)
XLA Ops:
  7.2 0.7 all-gather.2.cloned.1.call-update
  7.9 0.0 reduce-scatter.3.cloned.1.call-start
  8.0 0.1 iota_add_fusion
  8.0 0.1 add.100
  9.5 1.2 dynamic-slice
  11.4 0.9 dynamic-update-slice
  12.2 5.2 %all-reduce = s32[128]{0:T(128)S(1)} all-reduce(s32[128]{0:T(128)S(1)} %dynamic-update-slice), channel_id=1, replica_groups=mesh['row'=2,'col'=16] {'row'}, use_global_device_ids=true, to_apply=%add | all-reduce | flops 128 | bytes 1024
  17.4 8.8 %all_gather.10 = f32[128,1152]{1,0:T(8,128)S(1)} all-gather(f32[64,1152]{1,0:T(8,128)} %param.5), channel_id=1, replica_groups=mesh['row'=2,'col'=16] {'row'}, dimensions={0}, use_global_device_ids=true | all-gather | bytes 884736 | tf_op jit(solution)/shard_map/all_gather | solution.py:28
  26.2 0.1 multiply_reduce_fusion.1
  26.3 40.1 %all-gather.2.cloned.1.call-done = f32[1024,1152]{1,0:T(8,128)} async-done(((f32[64,1152]{1,0:T(8,128)}), f32[1024,1152]{1,0:T(8,128)}) %all-gather.2.cloned.1.call-update) | async-done | bytes 4718608 | tf_op jit(solution)/shard_map/all_gather | solution.py:31
  66.5 2.9 %multiply_reduce_fusion = f32[1024]{0:T(1024)S(1)} fusion(f32[1024,1152]{1,0:T(8,128)} %all-gather.2.cloned.1.call-done), kind=kLoop, calls=%fused_computation.1 | loop fusion | flops 2358272 | bytes 4722688 | tf_op jit(solution)/shard_map/reduce_sum | solution.py:10
  69.3 0.9 copy-done.1
  70.2 5.4 %fusion.3 = (f32[]{:T(128)}, f32[]{:T(128)}, f32[]{:T(128)}, f32[128,1024]{1,0:T(8,128)S(1)}) fusion(s32[1024]{0:T(1024)S(1)} %add.100, s32[128]{0:T(128)S(1)} %all-reduce, f32[]{:T(128)} %bitcast.8, f32[]{:T(128)} %bitcast.1, f32[1024,1152]{1,0:T(8,128)S(1)} %copy-done.1, f32[1024]{0:T(1024)S(1)} %add_sqrt_fusion, f32[128,1152]{1,0:T(8,128)S(1)} %all_gather.10, ...), kind=kOutput, calls=%fused_computation.30 | convolution fusion | flops 1816543232 | bytes 5841940 | tf_op jit(solution)/shard_map/dot_general | solution.py:15
  75.6 4.0 %convolution_multiply_fusion.1 = f32[128,1152]{1,0:T(8,128)} fusion(f32[1024,1152]{1,0:T(8,128)S(1)} %copy-done.1, f32[1024]{0:T(1024)S(1)} %add_sqrt_fusion, f32[]{:T(128)} %bitcast.1, f32[128,1024]{1,0:T(8,128)S(1)} %get-tuple-element.11, f32[]{:T(128)} %bitcast.6, s32[1024]{0:T(1024)S(1)} %add.100, s32[128]{0:T(128)S(1)} %all-reduce), kind=kOutput, calls=%fused_computation.2 | convolution fusion | flops 1814315008 | bytes 5841416 | tf_op jit(solution)/shard_map/dot_general | solution.py:15
  79.7 0.0 reduce-scatter.5.cloned.1.call-start
  79.8 5.7 %convolution_multiply_fusion = f32[1024,1152]{1,0:T(8,128)} fusion(f32[]{:T(128)} %bitcast.1, f32[128,1152]{1,0:T(8,128)S(1)} %all_gather.10, f32[128]{0:T(128)S(1)} %add_sqrt_fusion.3, f32[128,1024]{1,0:T(8,128)S(1)} %get-tuple-element.11, f32[]{:T(128)} %bitcast.7, s32[1024]{0:T(1024)S(1)} %add.100, s32[128]{0:T(128)S(1)} %all-reduce), kind=kOutput, calls=%fused_computation | convolution fusion | flops 1814315008 | bytes 5837832 | tf_op jit(solution)/shard_map/dot_general | solution.py:15
  85.5 0.1 multiply_reduce_fusion.6
  85.6 0.1 multiply_reduce_fusion.4
  85.8 39.6 %all-reduce.1 = (f32[]{:T(128)}, f32[]{:T(128)}, f32[]{:T(128)}) all-reduce(f32[]{:T(128)} %get-tuple-element.7, f32[]{:T(128)} %get-tuple-element.6, f32[]{:T(128)} %get-tuple-element.5), channel_id=1, replica_groups=mesh['row'=2,'col'=16] {'row','col'}, use_global_device_ids=true, to_apply=%region_3.0 | all-reduce | flops 3 | bytes 24 | tf_op jit(solution)/shard_map/psum | solution.py:49
  127.3 1.2 multiply_reduce_fusion.5
  128.5 1.8 subtract_divide_fusion.1
  130.3 43.8 %reduce-scatter.5.cloned.1.call-done = f32[64,1152]{1,0:T(8,128)} async-done(((f32[1024,1152]{1,0:T(8,128)}), f32[64,1152]{1,0:T(8,128)}) %reduce-scatter.5.cloned.1.call-update) | async-done | bytes 294928 | tf_op jit(solution)/shard_map/reduce_scatter | solution.py:46
  174.1 1.2 multiply_reduce_fusion.3
  175.3 1.8 subtract_divide_fusion
  (15 shorter events, 0.1 us)
Async XLA Ops:
  7.2 59.3 %all-gather.2.cloned.1.call-start = ((), (), s32[]{:S(2)}) async-start(), calls=%async_computation.2 | async-start | bytes 5013504 | tf_op jit(solution)/shard_map/all_gather | solution.py:31
  7.9 119.4 %reduce-scatter.3.cloned.1.call-start = ((), (), s32[]{:S(2)}) async-start(), calls=%async_computation.3 | async-start | bytes 884736 | tf_op jit(solution)/shard_map/reduce_scatter | solution.py:43
  66.5 3.8 %copy-start.1 = (f32[1024,1152]{1,0:T(8,128)S(1)}, f32[1024,1152]{1,0:T(8,128)}, u32[]{:S(2)}) copy-start(f32[1024,1152]{1,0:T(8,128)} %all-gather.2.cloned.1.call-done) | copy-start | bytes 14155780
  79.7 94.4 %reduce-scatter.5.cloned.1.call-start = ((), (), s32[]{:S(2)}) async-start(), calls=%async_computation.4 | async-start | bytes 5013504 | tf_op jit(solution)/shard_map/reduce_scatter | solution.py:46
  79.8 5.7 %copy-start = (f32[64,1152]{1,0:T(8,128)S(1)}, f32[64,1152]{1,0:T(8,128)}, u32[]{:S(2)}) copy-start(f32[64,1152]{1,0:T(8,128)} %param.5) | copy-start | bytes 884740
  79.8 5.8 %copy-start.2 = (f32[64,1152]{1,0:T(8,128)S(1)}, f32[64,1152]{1,0:T(8,128)}, u32[]{:S(2)}) copy-start(f32[64,1152]{1,0:T(8,128)} %param.6) | copy-start | bytes 884740
Sparse Core Ops, SparseCore 0:
  10.3 56.1 all-gather.1
  79.8 13.9 reduce-scatter.2
  98.2 75.8 reduce-scatter.4
where the time goes:
time: 187 us
  waiting for transfers between devices  84.7 us (45%)
  blocking collectives  53.6 us (29%)
  between operations  21.2 us (11%)
  matrix products  15.1 us (8%)
  other arithmetic  9.31 us (5%)
  local copies, waits for them, and re-layouts  3.07 us (2%)
    reduce_scatter x1, waiting for transfers between devices, per_device(): lax.psum_scatter(scale * full_dot(slope.T, image_block), 'col', scatter_d...  43.8 us
    all_gather x1, waiting for transfers between devices, per_device(): text_block = lax.all_gather(text, 'col', axis=0, tiled=True)  40.1 us
    psum x1, blocking collectives, per_device(): lax.psum((jnp.sum(term), jnp.sum(slope), jnp.sum(slope * cosine)), ('row'...  39.6 us
    dot_general x3, matrix products, full_dot(): jnp.dot(left, right, precision=lax.Precision.HIGHEST, preferred_element_t...  15.1 us
    all_gather x1, blocking collectives, per_device(): lax.all_gather(image, 'row', axis=0, tiled=True)  8.79 us
    unnamed x1, blocking collectives  5.19 us
  transfers between devices with their start and end apart: 3, of which 2 were waited for; matrix products, arithmetic and copies ran while one was open for 6% of the time, Pallas kernels for 0%

commit v1 on v0

v1 whole, which is shorter than its diff:
```python
import functools

import jax
import jax.numpy as jnp
from jax import lax
from jax.experimental import pallas as pl
from jax.experimental.pallas import tpu as pltpu
from jax.sharding import PartitionSpec as P

EPSILON = 1e-06
AXES = ("row", "col")
VMEM = pl.BlockSpec(memory_space=pltpu.VMEM)
SMEM = pl.BlockSpec(memory_space=pltpu.SMEM)
VMEM_BYTES = 40 << 20


def generators(count):
    steps = []
    for bit in range(count.bit_length() - 1):
        steps.append(12 if bit == 3 else 1 << bit)
    image = steps[2::2] + steps[:1]
    text = steps[3::2] + steps[1:2]
    return image, text


def exchange(value, step, count):
    return lax.ppermute(value, AXES, [(i, i ^ step) for i in range(count)])


def spread(own, steps, count):
    blocks = {0: own}
    for step in steps:
        for mask in list(blocks):
            blocks[mask ^ step] = exchange(blocks[mask], step, count)
    return blocks


def unit_rows(rows):
    norm = jnp.sqrt(jnp.sum(rows * rows, axis=1, keepdims=True) + EPSILON)
    return rows / norm, norm


def halves(value):
    high = value.astype(jnp.bfloat16)
    low = (value - high.astype(jnp.float32)).astype(jnp.bfloat16)
    return high, low


def dot(left, right, dims):
    return lax.dot_general(left, right, (dims, ((), ())), preferred_element_type=jnp.float32)


def image_kernel(count, *refs):
    blocks, (high_ref, low_ref, label_ref) = refs[:count], refs[count:]
    rows = high_ref.shape[0] // count
    for at, block in enumerate(blocks):
        unit, _ = unit_rows(block[:rows, :])
        high, low = halves(unit)
        high_ref[pl.ds(at * rows, rows), :] = high
        low_ref[pl.ds(at * rows, rows), :] = low
    lane = lax.broadcasted_iota(jnp.int32, (8, 2 * rows), 1)
    for at in range(0, count, 2):
        first = blocks[at][pl.ds(rows, 8), pl.ds(0, 2 * rows)]
        second = blocks[at + 1][pl.ds(rows, 8), pl.ds(0, 2 * rows)]
        label_ref[:, pl.ds(at * rows, 2 * rows)] = jnp.where(lane < rows, first, second)


def tile_kernel(count, base_ref, log_scale_ref, bias_ref, high_ref, low_ref, label_ref, *refs):
    texts, outs = refs[:count], refs[count:]
    grads, (slope_ref, unit_ref, sums_ref) = outs[:count], outs[count:]
    rows = texts[0].shape[0]
    total = high_ref.shape[0]
    scale = jnp.exp(jnp.full((1, 1), log_scale_ref[0], jnp.float32))
    term_sum = jnp.zeros((1, total), jnp.float32)
    slope_sum = jnp.zeros((1, total), jnp.float32)
    product_sum = jnp.zeros((1, total), jnp.float32)
    labels = label_ref[0:1, :]
    sub = lax.broadcasted_iota(jnp.int32, (rows, total), 0)
    for at in range(count):
        unit, _ = unit_rows(texts[at][...])
        high, low = halves(unit)
        unit_ref[pl.ds(at * 3 * rows, rows), :] = high
        unit_ref[pl.ds(at * 3 * rows + rows, rows), :] = low
        unit_ref[pl.ds(at * 3 * rows + 2 * rows, rows), :] = high
        both = dot(jnp.concatenate([high, low], axis=0), high_ref[...], ((1,), (1,)))
        cosine = both[:rows] + (both[rows:] + dot(high, low_ref[...], ((1,), (1,))))
        logit = scale * cosine + bias_ref[0]
        positive = (sub + base_ref[at]).astype(jnp.float32) == labels
        decay = jnp.exp(-jnp.abs(logit))
        term = jnp.maximum(jnp.where(positive, -logit, logit), 0.0) + jnp.log1p(decay)
        sigmoid = jnp.where(logit >= 0, 1.0, decay) / (1.0 + decay)
        slope = sigmoid - positive.astype(jnp.float32)
        term_sum += jnp.sum(term, axis=0, keepdims=True)
        slope_sum += jnp.sum(slope, axis=0, keepdims=True)
        product_sum += jnp.sum(slope * cosine, axis=0, keepdims=True)
        slope_high, slope_low = halves(slope)
        both = dot(jnp.concatenate([slope_high, slope_low], axis=0), high_ref[...], ((1,), (0,)))
        grads[at][...] = both[:rows] + (both[rows:] + dot(slope_high, low_ref[...], ((1,), (0,))))
        slope_ref[pl.ds(at * 3 * rows, rows), :] = slope_high
        slope_ref[pl.ds(at * 3 * rows + rows, rows), :] = slope_high
        slope_ref[pl.ds(at * 3 * rows + 2 * rows, rows), :] = slope_low
    parts = []
    for row in (term_sum, slope_sum, product_sum):
        part = row[:, 0:128]
        for at in range(128, total, 128):
            part += row[:, at : at + 128]
        parts.append(part)
    sums_ref[...] = jnp.concatenate(parts + [jnp.zeros((5, 128), jnp.float32)], axis=0)


def tile(bases, log_scale, bias, high, low, labels, texts):
    count = len(texts)
    rows, width = texts[0].shape
    total = high.shape[0]
    out = pl.pallas_call(
        functools.partial(tile_kernel, count),
        out_shape=[jax.ShapeDtypeStruct((rows, width), jnp.float32)] * count
        + [
            jax.ShapeDtypeStruct((3 * count * rows, total), jnp.bfloat16),
            jax.ShapeDtypeStruct((3 * count * rows, width), jnp.bfloat16),
            jax.ShapeDtypeStruct((8, 128), jnp.float32),
        ],
        in_specs=[SMEM] * 3 + [VMEM] * (3 + count),
        out_specs=[VMEM] * (count + 3),
        compiler_params=pltpu.CompilerParams(vmem_limit_bytes=VMEM_BYTES),
    )(bases, log_scale, bias, high, low, labels, *texts)
    return out[:count], out[count], out[count + 1], out[count + 2]


def image_grad_kernel(slope_ref, unit_ref, *refs):
    before, (keep_ref, send_ref) = refs[:-2], refs[-2:]
    total = dot(slope_ref[...], unit_ref[...], ((0,), (0,)))
    half = keep_ref.shape[0]
    if before:
        keep_ref[...] = before[0][...] + total[:half]
        send_ref[...] = before[1][...] + total[half:]
    else:
        keep_ref[...] = total[:half]
        send_ref[...] = total[half:]


def image_grad(slope, unit, before=()):
    half, width = slope.shape[1] // 2, unit.shape[1]
    return pl.pallas_call(
        image_grad_kernel,
        out_shape=[jax.ShapeDtypeStruct((half, width), jnp.float32)] * 2,
        in_specs=[VMEM] * (2 + len(before)),
        out_specs=[VMEM] * 2,
        compiler_params=pltpu.CompilerParams(vmem_limit_bytes=VMEM_BYTES),
    )(slope, unit, *before)


def final_kernel(log_scale_ref, own_ref, *refs):
    parts, out_ref = refs[:-1], refs[-1]
    scale = jnp.exp(jnp.full((1, 1), log_scale_ref[0], jnp.float32))
    total = parts[0][...]
    for part in parts[1:]:
        total = total + part[...]
    grad = scale * total
    unit, norm = unit_rows(own_ref[...])
    out_ref[...] = (grad - unit * jnp.sum(unit * grad, axis=1, keepdims=True)) / norm


def final(log_scale, own, parts):
    return pl.pallas_call(
        final_kernel,
        out_shape=jax.ShapeDtypeStruct(own.shape, jnp.float32),
        in_specs=[SMEM] + [VMEM] * (1 + len(parts)),
        out_specs=VMEM,
        compiler_params=pltpu.CompilerParams(vmem_limit_bytes=VMEM_BYTES),
    )(log_scale, own, *parts)


def gather_back(parts, steps, count):
    parts = {mask: [part] for mask, part in parts.items()}
    for step in reversed(steps):
        masks = sorted((m for m in parts if m ^ step not in parts or m > m ^ step), reverse=True)
        masks = masks[: len(parts) // 2]
        for mask in masks:
            kept = parts.pop(mask)
            parts[mask ^ step].append(exchange(functools.reduce(jnp.add, kept), step, count))
    return parts[0]


def per_device(count, image, text, labels, log_scale, bias):
    rows, width = image.shape
    pairs = rows * count
    me = lax.axis_index("row") * lax.axis_size("col") + lax.axis_index("col")
    image_steps, text_steps = generators(count)
    label_row = jnp.tile(labels.astype(jnp.float32), 2)[None, :]
    carried = jnp.concatenate([image, jnp.pad(label_row, ((0, 7), (0, width - 2 * rows)))], axis=0)
    texts = spread(text, text_steps, count)
    images = spread(carried, image_steps, count)
    masks = list(images)
    total = rows * len(masks)
    high, low, label_lanes = pl.pallas_call(
        functools.partial(image_kernel, len(masks)),
        out_shape=[
            jax.ShapeDtypeStruct((total, width), jnp.bfloat16),
            jax.ShapeDtypeStruct((total, width), jnp.bfloat16),
            jax.ShapeDtypeStruct((8, total), jnp.float32),
        ],
        in_specs=[VMEM] * len(masks),
        out_specs=[VMEM] * 3,
        compiler_params=pltpu.CompilerParams(vmem_limit_bytes=VMEM_BYTES),
    )(*images.values())

    text_masks = list(texts)
    groups = [text_masks[:-1], text_masks[-1:]]
    grads, sums, before = {}, [], ()
    for group in groups:
        bases = jnp.stack([(me ^ mask) * rows for mask in group]).astype(jnp.int32)
        parts, slope, unit, part_sums = tile(
            bases, log_scale, bias, high, low, label_lanes, [texts[mask] for mask in group]
        )
        grads.update(zip(group, parts))
        sums.append(part_sums)
        before = image_grad(slope, unit, before)
    keep, send = before

    unit_grad_text = gather_back(grads, text_steps, count)
    received = exchange(send, image_steps[-1], count)
    kept = keep + received
    near = masks[: len(masks) // 2]
    image_parts = {mask: kept[at * rows : (at + 1) * rows] for at, mask in enumerate(near)}
    unit_grad_image = gather_back(image_parts, image_steps[:-1], count)

    scalars = functools.reduce(jnp.add, sums)
    for step in text_steps[::-1] + image_steps[::-1]:
        scalars = scalars + exchange(scalars, step, count)
    summed, slope_sum, product_sum = jnp.sum(scalars[0]), jnp.sum(scalars[1]), jnp.sum(scalars[2])

    grad_image = final(log_scale, image, unit_grad_image)
    grad_text = final(log_scale, text, unit_grad_text)
    scale = jnp.exp(log_scale[0])
    loss = (summed / pairs).reshape(1)
    grad_log_scale = (scale * product_sum / pairs).reshape(1)
    grad_bias = (slope_sum / pairs).reshape(1)
    return (loss, grad_image, grad_text, grad_log_scale, grad_bias)


def solution(mesh):
    count = mesh.shape["row"] * mesh.shape["col"]
    return jax.shard_map(
        functools.partial(per_device, count),
        mesh=mesh,
        in_specs=(P(AXES, None), P(AXES, None), P(AXES), P(), P()),
        out_specs=(P(), P(AXES, None), P(AXES, None), P(), P()),
        check_vma=False,
    )
```

time: 187 us -> 90.6 us (0.48)
  blocking collectives: 53.6 us -> 0 us
  waiting for transfers between devices: 84.7 us -> 37.6 us
  starting transfers between devices: 0.12 us -> 30.3 us
  matrix products: 15.1 us -> 0 us
  between operations: 21.2 us -> 7.43 us
  Pallas kernels: 0 us -> 11.5 us
  other arithmetic: 9.31 us -> 3.35 us
  local copies, waits for them, and re-layouts: 3.07 us -> 0.12 us
    reduce_scatter x2 -> x0, waiting for transfers between devices: 43.8 us -> none  [the longest x1 43.8 us: per_device(): lax.psum_scatter(scale * full_dot(slope.T, image_block), 'col', scatter_d...]
    all_gather x1 -> x0, waiting for transfers between devices: 40.1 us -> none  [per_device(): text_block = lax.all_gather(text, 'col', axis=0, tiled=True)]
    psum x1 -> x0, blocking collectives: 39.6 us -> none  [per_device(): lax.psum((jnp.sum(term), jnp.sum(slope), jnp.sum(slope * cosine)), ('row'...]
    ppermute x0 -> x22, waiting for transfers between devices: none -> 37.6 us  [exchange(): return lax.ppermute(value, AXES, [(i, i ^ step) for i in range(count)])]
    ppermute x0 -> x22, starting transfers between devices: none -> 30.3 us  [exchange(): return lax.ppermute(value, AXES, [(i, i ^ step) for i in range(count)])]
    dot_general x3 -> x0, matrix products: 15.1 us -> none  [full_dot(): jnp.dot(left, right, precision=lax.Precision.HIGHEST, preferred_element_t...]
    pallas_call x0 -> x7, Pallas kernels: none -> 11.5 us  [the longest x2 7.19 us: tile(): pl.pallas_call(functools.partial(tile_kernel, count), out_shape=[jax.Shap...]
    all_gather x1 -> x0, blocking collectives: 8.79 us -> none  [per_device(): lax.all_gather(image, 'row', axis=0, tiled=True)]
  transfers between devices with their start and end apart: 3 -> 22, of which waited for: 2 -> 11; matrix products, arithmetic and copies ran while one was open for 6% -> 2% of each run, Pallas kernels for 0% -> 8%
where the time goes in v1:
time: 90.6 us; the launch traced here: 90.3 us
  waiting for transfers between devices  37.6 us (42%)
  starting transfers between devices  30.3 us (33%)
  Pallas kernels  11.5 us (13%)
  between operations  7.43 us (8%)
  other arithmetic  3.35 us (4%)
    ppermute x22, waiting for transfers between devices, exchange(): return lax.ppermute(value, AXES, [(i, i ^ step) for i in range(count)])  37.6 us
    ppermute x22, starting transfers between devices, exchange(): return lax.ppermute(value, AXES, [(i, i ^ step) for i in range(count)])  30.3 us
    pallas_call x2, Pallas kernels, tile(): pl.pallas_call(functools.partial(tile_kernel, count), out_shape=[jax.Shap...  7.19 us
    pallas_call x2, Pallas kernels, final(): pl.pallas_call(final_kernel, out_shape=jax.ShapeDtypeStruct(own.shape, jn...  1.89 us
  transfers between devices with their start and end apart: 22, of which 11 were waited for; matrix products, arithmetic and copies ran while one was open for 2% of the time, Pallas kernels for 8%

profile of v1, /device:TPU:0, one launch (start us, length us, event | category | flops | bytes accessed | tf_op | source)
XLA Modules:
  0.0 90.3 jit_solution(15358418267365682625)
XLA Ops:
  2.4 3.1 %collective-permute-start = (f32[72,1152]{1,0:T(8,128)S(1)}, f32[72,1152]{1,0:T(8,128)S(1)}, u32[]{:S(2)}, u32[]{:S(2)}) collective-permute-start(f32[72,1152]{1,0:T(8,128)S(1)} %select_maximum_fusion.refs_0_), channel_id=1, source_target_pairs={{0,4},{1,5},{2,6},{3,7},{4,0},{5,1},{6,2},{7,3},{8,12},{9,13},{10,... | collective-permute-start | bytes 995336 | tf_op jit(solution)/shard_map/ppermute | solution.py:27
  5.5 1.5 %collective-permute-start.1 = (f32[72,1152]{1,0:T(8,128)S(1)}, f32[72,1152]{1,0:T(8,128)S(1)}, u32[]{:S(2)}, u32[]{:S(2)}) collective-permute-start(f32[72,1152]{1,0:T(8,128)S(1)} %select_maximum_fusion.refs_0_), channel_id=1, source_target_pairs={{0,16},{1,17},{2,18},{3,19},{4,20},{5,21},{6,22},{7,23},{8,24},{9,... | collective-permute-start | bytes 995336 | tf_op jit(solution)/shard_map/ppermute | solution.py:27
  6.9 6.3 %collective-permute-done.refs_1_ = f32[72,1152]{1,0:T(8,128)S(1)} collective-permute-done((f32[72,1152]{1,0:T(8,128)S(1)}, f32[72,1152]{1,0:T(8,128)S(1)}, u32[]{:S(2)}, u32[]{:S(2)}) %collective-permute-start) | collective-permute-done | bytes 331808 | tf_op jit(solution)/shard_map/ppermute | solution.py:27
  13.3 1.7 %collective-permute-start.2 = (f32[72,1152]{1,0:T(8,128)S(1)}, f32[72,1152]{1,0:T(8,128)S(1)}, u32[]{:S(2)}, u32[]{:S(2)}) collective-permute-start(f32[72,1152]{1,0:T(8,128)S(1)} %collective-permute-done.refs_1_), channel_id=1, source_target_pairs={{0,16},{1,17},{2,18},{3,19},{4,20},{5,21},{6,22},{7,23},{8,24},{9,... | collective-permute-start | bytes 995336 | tf_op jit(solution)/shard_map/ppermute | solution.py:27
  14.9 3.6 %collective-permute-start.7 = (f32[64,1152]{1,0:T(8,128)}, f32[64,1152]{1,0:T(8,128)S(1)}, u32[]{:S(2)}, u32[]{:S(2)}) collective-permute-start(f32[64,1152]{1,0:T(8,128)} %own_ref.3), channel_id=1, source_target_pairs={{0,12},{1,13},{2,14},{3,15},{4,8},{5,9},{6,10},{7,11},{8,4},{9,5},... | collective-permute-start | bytes 884744 | tf_op jit(solution)/shard_map/ppermute | solution.py:27
  19.0 3.2 %collective-permute-done.2.refs_3_ = f32[72,1152]{1,0:T(8,128)S(1)} collective-permute-done((f32[72,1152]{1,0:T(8,128)S(1)}, f32[72,1152]{1,0:T(8,128)S(1)}, u32[]{:S(2)}, u32[]{:S(2)}) %collective-permute-start.2) | collective-permute-done | bytes 331808 | tf_op jit(solution)/shard_map/ppermute | solution.py:27
  22.2 4.3 %collective-permute-done.7.refs_1_ = f32[64,1152]{1,0:T(8,128)S(1)} collective-permute-done((f32[64,1152]{1,0:T(8,128)}, f32[64,1152]{1,0:T(8,128)S(1)}, u32[]{:S(2)}, u32[]{:S(2)}) %collective-permute-start.7) | collective-permute-done | bytes 294944 | tf_op jit(solution)/shard_map/ppermute | solution.py:27
  26.5 1.5 %collective-permute-start.8 = (f32[64,1152]{1,0:T(8,128)}, f32[64,1152]{1,0:T(8,128)S(1)}, u32[]{:S(2)}, u32[]{:S(2)}) collective-permute-start(f32[64,1152]{1,0:T(8,128)} %own_ref.3), channel_id=1, source_target_pairs={{0,2},{1,3},{2,0},{3,1},{4,6},{5,7},{6,4},{7,5},{8,10},{9,11},{10,... | collective-permute-start | bytes 884744 | tf_op jit(solution)/shard_map/ppermute | solution.py:27
  30.6 6.0 %collective-permute-done.8.refs_2_ = f32[64,1152]{1,0:T(8,128)S(1)} collective-permute-done((f32[64,1152]{1,0:T(8,128)}, f32[64,1152]{1,0:T(8,128)S(1)}, u32[]{:S(2)}, u32[]{:S(2)}) %collective-permute-start.8) | collective-permute-done | bytes 294944 | tf_op jit(solution)/shard_map/ppermute | solution.py:27
  36.6 4.7 %shard_map.93 = (f32[64,1152]{1,0:T(8,128)S(1)}, f32[64,1152]{1,0:T(8,128)S(1)}, f32[64,1152]{1,0:T(8,128)S(1)}, bf16[576,512]{1,0:T(8,128)(2,1)S(1)}, bf16[576,...) custom-call(s32[3]{0:T(128)S(1)} %pad_add_fusion.base_ref, f32[1]{0:T(128)S(6)} %copy.10.log_scale_ref, f32[1]{0:T(128)S(6)} %copy.11.bias_ref, ...), custom_call_target="tpu_custom_call" | custom-call | tf_op jit(solution)/shard_map/pallas_call | solution.py:115
  42.6 2.5 %shard_map.94 = (f32[64,1152]{1,0:T(8,128)S(1)}, bf16[192,512]{1,0:T(8,128)(2,1)S(1)}, bf16[192,1152]{1,0:T(8,128)(2,1)S(1)}, f32[8,128]{1,0:T(8,128)S(1)}) custom-call(s32[1]{0:T(128)} %bitcast.3.base_ref, f32[1]{0:T(128)S(6)} %copy.10.log_scale_ref, f32[1]{0:T(128)S(6)} %copy.11.bias_ref, bf16[512,1152]{1,0:T(8,128)(2,1)S(1)} %get-tuple-element.22.high_ref, ...), custom_call_target="tpu_custom_call" | custom-call | tf_op jit(solution)/shard_map/pallas_call | solution.py:115
  45.7 1.6 %collective-permute-start.20 = (f32[64,1152]{1,0:T(8,128)S(1)}, f32[64,1152]{1,0:T(8,128)S(1)}, u32[]{:S(2)}, u32[]{:S(2)}) collective-permute-start(f32[64,1152]{1,0:T(8,128)S(1)} %get-tuple-element.38), channel_id=1, source_target_pairs={{0,2},{1,3},{2,0},{3,1},{4,6},{5,7},{6,4},{7,5},{8,10},{9,11},{10,... | collective-permute-start | bytes 884744 | tf_op jit(solution)/shard_map/ppermute | solution.py:27
  47.2 1.3 %collective-permute-done.15 = f32[256,1152]{1,0:T(8,128)S(1)} collective-permute-done((f32[256,1152]{1,0:T(8,128)S(1)}, f32[256,1152]{1,0:T(8,128)S(1)}, u32[]{:S(2)}, u32[]{:S(2)}) %collective-permute-start.15) | collective-permute-done | bytes 1179680 | tf_op jit(solution)/shard_map/ppermute | solution.py:27
  49.3 1.5 %collective-permute-start.19 = (f32[64,1152]{1,0:T(8,128)S(1)}, f32[64,1152]{1,0:T(8,128)S(1)}, u32[]{:S(2)}, u32[]{:S(2)}) collective-permute-start(f32[64,1152]{1,0:T(8,128)S(1)} %get-tuple-element.36), channel_id=1, source_target_pairs={{0,2},{1,3},{2,0},{3,1},{4,6},{5,7},{6,4},{7,5},{8,10},{9,11},{10,... | collective-permute-start | bytes 884744 | tf_op jit(solution)/shard_map/ppermute | solution.py:27
  50.8 4.7 %collective-permute-done.20 = f32[64,1152]{1,0:T(8,128)S(1)} collective-permute-done((f32[64,1152]{1,0:T(8,128)S(1)}, f32[64,1152]{1,0:T(8,128)S(1)}, u32[]{:S(2)}, u32[]{:S(2)}) %collective-permute-start.20) | collective-permute-done | bytes 294944 | tf_op jit(solution)/shard_map/ppermute | solution.py:27
  55.6 3.6 %collective-permute-start.21 = (f32[64,1152]{1,0:T(8,128)S(1)}, f32[64,1152]{1,0:T(8,128)S(1)}, u32[]{:S(2)}, u32[]{:S(2)}) collective-permute-start(f32[64,1152]{1,0:T(8,128)S(1)} %add.41), channel_id=1, source_target_pairs={{0,12},{1,13},{2,14},{3,15},{4,8},{5,9},{6,10},{7,11},{8,4},{9,5},... | collective-permute-start | bytes 884744 | tf_op jit(solution)/shard_map/ppermute | solution.py:27
  60.5 4.5 %collective-permute-start.18 = (f32[64,1152]{1,0:T(8,128)S(1)}, f32[64,1152]{1,0:T(8,128)S(1)}, u32[]{:S(2)}, u32[]{:S(2)}) collective-permute-start(f32[64,1152]{1,0:T(8,128)S(1)} %get-tuple-element.42), channel_id=1, source_target_pairs={{0,4},{1,5},{2,6},{3,7},{4,0},{5,1},{6,2},{7,3},{8,12},{9,13},{10,... | collective-permute-start | bytes 884744 | tf_op jit(solution)/shard_map/ppermute | solution.py:27
  65.1 1.5 %collective-permute-start.10 = (f32[8,128]{1,0:T(8,128)S(1)}, f32[8,128]{1,0:T(8,128)S(1)}, u32[]{:S(2)}, u32[]{:S(2)}) collective-permute-start(f32[8,128]{1,0:T(8,128)S(1)} %add.33), channel_id=1, source_target_pairs={{0,2},{1,3},{2,0},{3,1},{4,6},{5,7},{6,4},{7,5},{8,10},{9,11},{10,... | collective-permute-start | bytes 12296 | tf_op jit(solution)/shard_map/ppermute | solution.py:27
  66.6 2.1 %collective-permute-done.10 = f32[8,128]{1,0:T(8,128)S(1)} collective-permute-done((f32[8,128]{1,0:T(8,128)S(1)}, f32[8,128]{1,0:T(8,128)S(1)}, u32[]{:S(2)}, u32[]{:S(2)}) %collective-permute-start.10) | collective-permute-done | bytes 4128 | tf_op jit(solution)/shard_map/ppermute | solution.py:27
  68.7 2.5 %collective-permute-start.11 = (f32[8,128]{1,0:T(8,128)S(1)}, f32[8,128]{1,0:T(8,128)S(1)}, u32[]{:S(2)}, u32[]{:S(2)}) collective-permute-start(f32[8,128]{1,0:T(8,128)S(1)} %add.34), channel_id=1, source_target_pairs={{0,12},{1,13},{2,14},{3,15},{4,8},{5,9},{6,10},{7,11},{8,4},{9,5},... | collective-permute-start | bytes 12296 | tf_op jit(solution)/shard_map/ppermute | solution.py:27
  71.2 2.9 %collective-permute-done.11 = f32[8,128]{1,0:T(8,128)S(1)} collective-permute-done((f32[8,128]{1,0:T(8,128)S(1)}, f32[8,128]{1,0:T(8,128)S(1)}, u32[]{:S(2)}, u32[]{:S(2)}) %collective-permute-start.11) | collective-permute-done | bytes 4128 | tf_op jit(solution)/shard_map/ppermute | solution.py:27
  75.3 1.5 %collective-permute-start.13 = (f32[8,128]{1,0:T(8,128)S(1)}, f32[8,128]{1,0:T(8,128)S(1)}, u32[]{:S(2)}, u32[]{:S(2)}) collective-permute-start(f32[8,128]{1,0:T(8,128)S(1)} %add.36), channel_id=1, source_target_pairs={{0,16},{1,17},{2,18},{3,19},{4,20},{5,21},{6,22},{7,23},{8,24},{9,... | collective-permute-start | bytes 12296 | tf_op jit(solution)/shard_map/ppermute | solution.py:27
  76.8 2.1 %collective-permute-done.13 = f32[8,128]{1,0:T(8,128)S(1)} collective-permute-done((f32[8,128]{1,0:T(8,128)S(1)}, f32[8,128]{1,0:T(8,128)S(1)}, u32[]{:S(2)}, u32[]{:S(2)}) %collective-permute-start.13) | collective-permute-done | bytes 4128 | tf_op jit(solution)/shard_map/ppermute | solution.py:27
  78.9 3.6 %collective-permute-done.14 = f32[8,128]{1,0:T(8,128)S(1)} collective-permute-done((f32[8,128]{1,0:T(8,128)S(1)}, f32[8,128]{1,0:T(8,128)S(1)}, u32[]{:S(2)}, u32[]{:S(2)}) %collective-permute-start.14) | collective-permute-done | bytes 4128 | tf_op jit(solution)/shard_map/ppermute | solution.py:27
  (47 shorter events, 11.1 us)
Async XLA Ops:
  2.4 10.9 %collective-permute-start = (f32[72,1152]{1,0:T(8,128)S(1)}, f32[72,1152]{1,0:T(8,128)S(1)}, u32[]{:S(2)}, u32[]{:S(2)}) collective-permute-start(f32[72,1152]{1,0:T(8,128)S(1)} %select_maximum_fusion.refs_0_), channel_id=1, source_target_pairs={{0,4},{1,5},{2,6},{3,7},{4,0},{5,1},{6,2},{7,3},{8,12},{9,13},{10,... | collective-permute-start | bytes 995336 | tf_op jit(solution)/shard_map/ppermute | solution.py:27
  5.5 13.3 %collective-permute-start.1 = (f32[72,1152]{1,0:T(8,128)S(1)}, f32[72,1152]{1,0:T(8,128)S(1)}, u32[]{:S(2)}, u32[]{:S(2)}) collective-permute-start(f32[72,1152]{1,0:T(8,128)S(1)} %select_maximum_fusion.refs_0_), channel_id=1, source_target_pairs={{0,16},{1,17},{2,18},{3,19},{4,20},{5,21},{6,22},{7,23},{8,24},{9,... | collective-permute-start | bytes 995336 | tf_op jit(solution)/shard_map/ppermute | solution.py:27
  13.3 9.0 %collective-permute-start.2 = (f32[72,1152]{1,0:T(8,128)S(1)}, f32[72,1152]{1,0:T(8,128)S(1)}, u32[]{:S(2)}, u32[]{:S(2)}) collective-permute-start(f32[72,1152]{1,0:T(8,128)S(1)} %collective-permute-done.refs_1_), channel_id=1, source_target_pairs={{0,16},{1,17},{2,18},{3,19},{4,20},{5,21},{6,22},{7,23},{8,24},{9,... | collective-permute-start | bytes 995336 | tf_op jit(solution)/shard_map/ppermute | solution.py:27
  14.9 13.1 %collective-permute-start.3 = (f32[72,1152]{1,0:T(8,128)S(1)}, f32[72,1152]{1,0:T(8,128)S(1)}, u32[]{:S(2)}, u32[]{:S(2)}) collective-permute-start(f32[72,1152]{1,0:T(8,128)S(1)} %select_maximum_fusion.refs_0_), channel_id=1, source_target_pairs={{0,1},{1,0},{2,3},{3,2},{4,5},{5,4},{6,7},{7,6},{8,9},{9,8},{10,11... | collective-permute-start | bytes 995336 | tf_op jit(solution)/shard_map/ppermute | solution.py:27
  14.9 11.6 %collective-permute-start.7 = (f32[64,1152]{1,0:T(8,128)}, f32[64,1152]{1,0:T(8,128)S(1)}, u32[]{:S(2)}, u32[]{:S(2)}) collective-permute-start(f32[64,1152]{1,0:T(8,128)} %own_ref.3), channel_id=1, source_target_pairs={{0,12},{1,13},{2,14},{3,15},{4,8},{5,9},{6,10},{7,11},{8,4},{9,5},... | collective-permute-start | bytes 884744 | tf_op jit(solution)/shard_map/ppermute | solution.py:27
  18.5 11.4 %collective-permute-start.4 = (f32[72,1152]{1,0:T(8,128)S(1)}, f32[72,1152]{1,0:T(8,128)S(1)}, u32[]{:S(2)}, u32[]{:S(2)}) collective-permute-start(f32[72,1152]{1,0:T(8,128)S(1)} %collective-permute-done.refs_1_), channel_id=1, source_target_pairs={{0,1},{1,0},{2,3},{3,2},{4,5},{5,4},{6,7},{7,6},{8,9},{9,8},{10,11... | collective-permute-start | bytes 995336 | tf_op jit(solution)/shard_map/ppermute | solution.py:27
  18.7 11.2 %collective-permute-start.5 = (f32[72,1152]{1,0:T(8,128)S(1)}, f32[72,1152]{1,0:T(8,128)S(1)}, u32[]{:S(2)}, u32[]{:S(2)}) collective-permute-start(f32[72,1152]{1,0:T(8,128)S(1)} %collective-permute-done.1.refs_2_), channel_id=1, source_target_pairs={{0,1},{1,0},{2,3},{3,2},{4,5},{5,4},{6,7},{7,6},{8,9},{9,8},{10,11... | collective-permute-start | bytes 995336 | tf_op jit(solution)/shard_map/ppermute | solution.py:27
  22.2 7.7 %collective-permute-start.6 = (f32[72,1152]{1,0:T(8,128)S(1)}, f32[72,1152]{1,0:T(8,128)S(1)}, u32[]{:S(2)}, u32[]{:S(2)}) collective-permute-start(f32[72,1152]{1,0:T(8,128)S(1)} %collective-permute-done.2.refs_3_), channel_id=1, source_target_pairs={{0,1},{1,0},{2,3},{3,2},{4,5},{5,4},{6,7},{7,6},{8,9},{9,8},{10,11... | collective-permute-start | bytes 995336 | tf_op jit(solution)/shard_map/ppermute | solution.py:27
  26.5 10.1 %collective-permute-start.8 = (f32[64,1152]{1,0:T(8,128)}, f32[64,1152]{1,0:T(8,128)S(1)}, u32[]{:S(2)}, u32[]{:S(2)}) collective-permute-start(f32[64,1152]{1,0:T(8,128)} %own_ref.3), channel_id=1, source_target_pairs={{0,2},{1,3},{2,0},{3,1},{4,6},{5,7},{6,4},{7,5},{8,10},{9,11},{10,... | collective-permute-start | bytes 884744 | tf_op jit(solution)/shard_map/ppermute | solution.py:27
  28.0 14.5 %collective-permute-start.9 = (f32[64,1152]{1,0:T(8,128)S(1)}, f32[64,1152]{1,0:T(8,128)}, u32[]{:S(2)}, u32[]{:S(2)}) collective-permute-start(f32[64,1152]{1,0:T(8,128)S(1)} %collective-permute-done.7.refs_1_), channel_id=1, source_target_pairs={{0,2},{1,3},{2,0},{3,1},{4,6},{5,7},{6,4},{7,5},{8,10},{9,11},{10,... | collective-permute-start | bytes 884744 | tf_op jit(solution)/shard_map/ppermute | solution.py:27
  29.9 6.7 %copy-start = (f32[64,1152]{1,0:T(8,128)S(1)}, f32[64,1152]{1,0:T(8,128)}, u32[]{:S(2)}) copy-start(f32[64,1152]{1,0:T(8,128)} %own_ref.3) | copy-start | bytes 884740
  45.6 2.9 %collective-permute-start.15 = (f32[256,1152]{1,0:T(8,128)S(1)}, f32[256,1152]{1,0:T(8,128)S(1)}, u32[]{:S(2)}, u32[]{:S(2)}) collective-permute-start(f32[256,1152]{1,0:T(8,128)S(1)} %get-tuple-element.34), channel_id=1, source_target_pairs={{0,1},{1,0},{2,3},{3,2},{4,5},{5,4},{6,7},{7,6},{8,9},{9,8},{10,11... | collective-permute-start | bytes 3538952 | tf_op jit(solution)/shard_map/ppermute | solution.py:27
  45.7 9.9 %collective-permute-start.20 = (f32[64,1152]{1,0:T(8,128)S(1)}, f32[64,1152]{1,0:T(8,128)S(1)}, u32[]{:S(2)}, u32[]{:S(2)}) collective-permute-start(f32[64,1152]{1,0:T(8,128)S(1)} %get-tuple-element.38), channel_id=1, source_target_pairs={{0,2},{1,3},{2,0},{3,1},{4,6},{5,7},{6,4},{7,5},{8,10},{9,11},{10,... | collective-permute-start | bytes 884744 | tf_op jit(solution)/shard_map/ppermute | solution.py:27
  48.7 10.5 %collective-permute-start.17 = (f32[64,1152]{1,0:T(8,128)S(1)}, f32[64,1152]{1,0:T(8,128)S(1)}, u32[]{:S(2)}, u32[]{:S(2)}) collective-permute-start(f32[64,1152]{1,0:T(8,128)S(1)} %slice.31), channel_id=1, source_target_pairs={{0,16},{1,17},{2,18},{3,19},{4,20},{5,21},{6,22},{7,23},{8,24},{9,... | collective-permute-start | bytes 884744 | tf_op jit(solution)/shard_map/ppermute | solution.py:27
  49.3 35.8 %collective-permute-start.19 = (f32[64,1152]{1,0:T(8,128)S(1)}, f32[64,1152]{1,0:T(8,128)S(1)}, u32[]{:S(2)}, u32[]{:S(2)}) collective-permute-start(f32[64,1152]{1,0:T(8,128)S(1)} %get-tuple-element.36), channel_id=1, source_target_pairs={{0,2},{1,3},{2,0},{3,1},{4,6},{5,7},{6,4},{7,5},{8,10},{9,11},{10,... | collective-permute-start | bytes 884744 | tf_op jit(solution)/shard_map/ppermute | solution.py:27
  55.6 29.5 %collective-permute-start.21 = (f32[64,1152]{1,0:T(8,128)S(1)}, f32[64,1152]{1,0:T(8,128)S(1)}, u32[]{:S(2)}, u32[]{:S(2)}) collective-permute-start(f32[64,1152]{1,0:T(8,128)S(1)} %add.41), channel_id=1, source_target_pairs={{0,12},{1,13},{2,14},{3,15},{4,8},{5,9},{6,10},{7,11},{8,4},{9,5},... | collective-permute-start | bytes 884744 | tf_op jit(solution)/shard_map/ppermute | solution.py:27
  60.0 26.0 %copy-start.1 = (f32[64,1152]{1,0:T(8,128)S(1)}, f32[64,1152]{1,0:T(8,128)}, u32[]{:S(2)}) copy-start(f32[64,1152]{1,0:T(8,128)} %own_ref.2) | copy-start | bytes 884740
  60.0 26.0 %collective-permute-start.16 = (f32[64,1152]{1,0:T(8,128)}, f32[64,1152]{1,0:T(8,128)S(1)}, u32[]{:S(2)}, u32[]{:S(2)}) collective-permute-start(f32[64,1152]{1,0:T(8,128)} %get-tuple-element.43), channel_id=1, source_target_pairs={{0,16},{1,17},{2,18},{3,19},{4,20},{5,21},{6,22},{7,23},{8,24},{9,... | collective-permute-start | bytes 884744 | tf_op jit(solution)/shard_map/ppermute | solution.py:27
  60.5 25.5 %collective-permute-start.18 = (f32[64,1152]{1,0:T(8,128)S(1)}, f32[64,1152]{1,0:T(8,128)S(1)}, u32[]{:S(2)}, u32[]{:S(2)}) collective-permute-start(f32[64,1152]{1,0:T(8,128)S(1)} %get-tuple-element.42), channel_id=1, source_target_pairs={{0,4},{1,5},{2,6},{3,7},{4,0},{5,1},{6,2},{7,3},{8,12},{9,13},{10,... | collective-permute-start | bytes 884744 | tf_op jit(solution)/shard_map/ppermute | solution.py:27
  65.1 3.6 %collective-permute-start.10 = (f32[8,128]{1,0:T(8,128)S(1)}, f32[8,128]{1,0:T(8,128)S(1)}, u32[]{:S(2)}, u32[]{:S(2)}) collective-permute-start(f32[8,128]{1,0:T(8,128)S(1)} %add.33), channel_id=1, source_target_pairs={{0,2},{1,3},{2,0},{3,1},{4,6},{5,7},{6,4},{7,5},{8,10},{9,11},{10,... | collective-permute-start | bytes 12296 | tf_op jit(solution)/shard_map/ppermute | solution.py:27
  68.7 5.4 %collective-permute-start.11 = (f32[8,128]{1,0:T(8,128)S(1)}, f32[8,128]{1,0:T(8,128)S(1)}, u32[]{:S(2)}, u32[]{:S(2)}) collective-permute-start(f32[8,128]{1,0:T(8,128)S(1)} %add.34), channel_id=1, source_target_pairs={{0,12},{1,13},{2,14},{3,15},{4,8},{5,9},{6,10},{7,11},{8,4},{9,5},... | collective-permute-start | bytes 12296 | tf_op jit(solution)/shard_map/ppermute | solution.py:27
  74.1 1.2 %collective-permute-start.12 = (f32[8,128]{1,0:T(8,128)S(1)}, f32[8,128]{1,0:T(8,128)S(1)}, u32[]{:S(2)}, u32[]{:S(2)}) collective-permute-start(f32[8,128]{1,0:T(8,128)S(1)} %add.35), channel_id=1, source_target_pairs={{0,1},{1,0},{2,3},{3,2},{4,5},{5,4},{6,7},{7,6},{8,9},{9,8},{10,11... | collective-permute-start | bytes 12296 | tf_op jit(solution)/shard_map/ppermute | solution.py:27
  75.3 3.6 %collective-permute-start.13 = (f32[8,128]{1,0:T(8,128)S(1)}, f32[8,128]{1,0:T(8,128)S(1)}, u32[]{:S(2)}, u32[]{:S(2)}) collective-permute-start(f32[8,128]{1,0:T(8,128)S(1)} %add.36), channel_id=1, source_target_pairs={{0,16},{1,17},{2,18},{3,19},{4,20},{5,21},{6,22},{7,23},{8,24},{9,... | collective-permute-start | bytes 12296 | tf_op jit(solution)/shard_map/ppermute | solution.py:27
  78.9 3.6 %collective-permute-start.14 = (f32[8,128]{1,0:T(8,128)S(1)}, f32[8,128]{1,0:T(8,128)S(1)}, u32[]{:S(2)}, u32[]{:S(2)}) collective-permute-start(f32[8,128]{1,0:T(8,128)S(1)} %add.37), channel_id=1, source_target_pairs={{0,4},{1,5},{2,6},{3,7},{4,0},{5,1},{6,2},{7,3},{8,12},{9,13},{10,... | collective-permute-start | bytes 12296 | tf_op jit(solution)/shard_map/ppermute | solution.py:27

commit v2 on v1

v2 whole, which is shorter than its diff:
```python
import functools

import jax
import jax.numpy as jnp
from jax import lax
from jax.experimental import pallas as pl
from jax.experimental.pallas import tpu as pltpu
from jax.sharding import PartitionSpec as P

EPSILON = 1e-06
LANES = 128
AXES = ("row", "col")
VMEM = pl.BlockSpec(memory_space=pltpu.VMEM)
SMEM = pl.BlockSpec(memory_space=pltpu.SMEM)
PARAMS = pltpu.CompilerParams(vmem_limit_bytes=40 << 20)
AHEAD = pl.CostEstimate(flops=10**10, bytes_accessed=10**10, transcendentals=0)


def generators(count):
    image, text = [], []
    for bit in range(1, count.bit_length() - 1):
        (text if bit in (2, 3) or bit > 4 and bit % 2 else image).append(12 if bit == 3 else 1 << bit)
    return image[::-1] + [1], text[::-1]


def exchange(value, step, count):
    return lax.ppermute(value, AXES, [(i, i ^ step) for i in range(count)])


def after(value, *others):
    return lax.optimization_barrier((value, *others))[0]


def unit_rows(rows):
    norm = jnp.sqrt(jnp.sum(rows * rows, axis=1, keepdims=True) + EPSILON)
    return rows / norm, norm


def halves(value):
    high = value.astype(jnp.bfloat16)
    low = (value - high.astype(jnp.float32)).astype(jnp.bfloat16)
    return high, low


def dot(left, right, dims):
    return lax.dot_general(left, right, (dims, ((), ())), preferred_element_type=jnp.float32)


def constants_kernel(masks, rows, me_ref, log_scale_ref, bias_ref, out_ref):
    values = [jnp.exp(jnp.full((1, LANES), log_scale_ref[0], jnp.float32))]
    values.append(jnp.full((1, LANES), bias_ref[0], jnp.float32))
    for mask in masks:
        first = jnp.bitwise_xor(me_ref[0], mask) * rows
        values.append(jnp.full((1, LANES), first, jnp.int32).astype(jnp.float32))
    values.append(jnp.zeros((out_ref.shape[0] - len(values), LANES), jnp.float32))
    out_ref[...] = jnp.concatenate(values, axis=0)


def constants(masks, rows, me, log_scale, bias):
    return pl.pallas_call(
        functools.partial(constants_kernel, masks, rows),
        out_shape=jax.ShapeDtypeStruct((len(masks) // 8 * 8 + 8, LANES), jnp.float32),
        in_specs=[SMEM] * 3,
        out_specs=VMEM,
        compiler_params=PARAMS,
    )(me, log_scale, bias)


def pack_kernel(image_ref, label_ref, out_ref):
    rows, width = image_ref.shape
    for at in range(0, width, LANES):
        out_ref[pl.ds(at // LANES * rows, rows), :] = image_ref[:, pl.ds(at, LANES)]
    label = label_ref[...].astype(jnp.float32)
    tail = jnp.broadcast_to(jnp.concatenate([label, label], axis=1), (8, LANES))
    out_ref[pl.ds(width // LANES * rows, 8), :] = tail


def pack(image, labels):
    rows, width = image.shape
    return pl.pallas_call(
        pack_kernel,
        out_shape=jax.ShapeDtypeStruct((width // LANES * rows + 8, LANES), jnp.float32),
        in_specs=[VMEM] * 2,
        out_specs=VMEM,
        compiler_params=PARAMS,
    )(image, labels.reshape(1, rows))


def image_kernel(count, *refs):
    blocks, (high_ref, low_ref, label_ref) = refs[:count], refs[count:]
    rows = high_ref.shape[0] // count
    width = high_ref.shape[1]
    for at, block in enumerate(blocks):
        squares = jnp.zeros((rows, LANES), jnp.float32)
        for piece in range(width // LANES):
            part = block[pl.ds(piece * rows, rows), :]
            squares += part * part
        norm = jnp.sqrt(jnp.sum(squares, axis=1, keepdims=True) + EPSILON)
        for piece in range(width // LANES):
            high, low = halves(block[pl.ds(piece * rows, rows), :] / norm)
            high_ref[pl.ds(at * rows, rows), pl.ds(piece * LANES, LANES)] = high
            low_ref[pl.ds(at * rows, rows), pl.ds(piece * LANES, LANES)] = low
    lane = lax.broadcasted_iota(jnp.int32, (8, LANES), 1)
    tail = pl.ds(width // LANES * rows, 8)
    for at in range(0, count, 2):
        pair = jnp.where(lane < rows, blocks[at][tail, :], blocks[at + 1][tail, :])
        label_ref[:, pl.ds(at * rows, LANES)] = pair


def image_units(blocks, rows, width):
    total = rows * len(blocks)
    return pl.pallas_call(
        functools.partial(image_kernel, len(blocks)),
        out_shape=[
            jax.ShapeDtypeStruct((total, width), jnp.bfloat16),
            jax.ShapeDtypeStruct((total, width), jnp.bfloat16),
            jax.ShapeDtypeStruct((8, total), jnp.float32),
        ],
        in_specs=[VMEM] * len(blocks),
        out_specs=[VMEM] * 3,
        compiler_params=PARAMS,
    )(*blocks)


def norm_kernel(block_ref, norm_ref):
    block = block_ref[...]
    norm = jnp.sqrt(jnp.sum(block * block, axis=1, keepdims=True) + EPSILON)
    norm_ref[...] = jnp.broadcast_to(norm, norm_ref.shape)


def row_norms(block):
    return pl.pallas_call(
        norm_kernel,
        out_shape=jax.ShapeDtypeStruct((block.shape[0], LANES), jnp.float32),
        in_specs=[VMEM],
        out_specs=VMEM,
        cost_estimate=AHEAD,
        compiler_params=PARAMS,
    )(block)


def tile_kernel(places, normed, fixed_ref, high_ref, low_ref, label_ref, *refs):
    count = len(places)
    texts, refs = refs[:count], refs[count:]
    norms, refs = dict(zip(normed, refs)), refs[len(normed) :]
    before, outs = refs[: -count - 3], refs[-count - 3 :]
    grads, (slope_ref, unit_ref, sums_ref) = outs[:count], outs[count:]
    rows = texts[0].shape[0]
    total = high_ref.shape[0]
    scale, bias = fixed_ref[0:1, 0:1], fixed_ref[1:2, 0:1]
    term_sum = jnp.zeros((1, total), jnp.float32)
    slope_sum = jnp.zeros((1, total), jnp.float32)
    product_sum = jnp.zeros((1, total), jnp.float32)
    labels = label_ref[0:1, :]
    sub = lax.broadcasted_iota(jnp.int32, (rows, total), 0).astype(jnp.float32)
    for at in range(count):
        if at in norms:
            unit = texts[at][...] / norms[at][:, 0:1]
        else:
            unit, _ = unit_rows(texts[at][...])
        high, low = halves(unit)
        unit_ref[pl.ds(at * 3 * rows, rows), :] = high
        unit_ref[pl.ds(at * 3 * rows + rows, rows), :] = low
        unit_ref[pl.ds(at * 3 * rows + 2 * rows, rows), :] = high
        both = dot(jnp.concatenate([high, low], axis=0), high_ref[...], ((1,), (1,)))
        cosine = both[:rows] + (both[rows:] + dot(high, low_ref[...], ((1,), (1,))))
        logit = scale * cosine + bias
        positive = sub + fixed_ref[2 + places[at] : 3 + places[at], 0:1] == labels
        decay = jnp.exp(-jnp.abs(logit))
        term = jnp.maximum(jnp.where(positive, -logit, logit), 0.0) + jnp.log1p(decay)
        sigmoid = jnp.where(logit >= 0, 1.0, decay) / (1.0 + decay)
        slope = sigmoid - positive.astype(jnp.float32)
        term_sum += jnp.sum(term, axis=0, keepdims=True)
        slope_sum += jnp.sum(slope, axis=0, keepdims=True)
        product_sum += jnp.sum(slope * cosine, axis=0, keepdims=True)
        slope_high, slope_low = halves(slope)
        both = dot(jnp.concatenate([slope_high, slope_low], axis=0), high_ref[...], ((1,), (0,)))
        grads[at][...] = both[:rows] + (both[rows:] + dot(slope_high, low_ref[...], ((1,), (0,))))
        slope_ref[pl.ds(at * 3 * rows, rows), :] = slope_high
        slope_ref[pl.ds(at * 3 * rows + rows, rows), :] = slope_high
        slope_ref[pl.ds(at * 3 * rows + 2 * rows, rows), :] = slope_low
    parts = []
    for row in (term_sum, slope_sum, product_sum):
        part = row[:, 0:LANES]
        for at in range(LANES, total, LANES):
            part += row[:, at : at + LANES]
        parts.append(part)
    sums = jnp.concatenate(parts + [jnp.zeros((5, LANES), jnp.float32)], axis=0)
    sums_ref[...] = before[0][...] + sums if before else sums


def tile(places, fixed, images, texts, norms, before=()):
    count = len(texts)
    rows, width = texts[0].shape
    total = images[0].shape[0]
    normed = tuple(at for at, norm in enumerate(norms) if norm is not None)
    extra = [norms[at] for at in normed] + list(before)
    out = pl.pallas_call(
        functools.partial(tile_kernel, places, normed),
        out_shape=[jax.ShapeDtypeStruct((rows, width), jnp.float32)] * count
        + [
            jax.ShapeDtypeStruct((3 * count * rows, total), jnp.bfloat16),
            jax.ShapeDtypeStruct((3 * count * rows, width), jnp.bfloat16),
            jax.ShapeDtypeStruct((8, LANES), jnp.float32),
        ],
        in_specs=[VMEM] * (4 + count + len(extra)),
        out_specs=[VMEM] * (count + 3),
        compiler_params=PARAMS,
    )(fixed, *images, *texts, *extra)
    return out[:count], out[count], out[count + 1], out[count + 2]


def image_grad_kernel(slope_ref, unit_ref, *refs):
    before, (keep_ref, send_ref) = refs[:-2], refs[-2:]
    total = dot(slope_ref[...], unit_ref[...], ((0,), (0,)))
    half = keep_ref.shape[0]
    if before:
        keep_ref[...] = before[0][...] + total[:half]
        send_ref[...] = before[1][...] + total[half:]
    else:
        keep_ref[...] = total[:half]
        send_ref[...] = total[half:]


def image_grad(slope, unit, before=()):
    half, width = slope.shape[1] // 2, unit.shape[1]
    return pl.pallas_call(
        image_grad_kernel,
        out_shape=[jax.ShapeDtypeStruct((half, width), jnp.float32)] * 2,
        in_specs=[VMEM] * (2 + len(before)),
        out_specs=[VMEM] * 2,
        compiler_params=PARAMS,
    )(slope, unit, *before)


def join_kernel(count, *refs):
    parts, others, out_ref = refs[:count], refs[count:-1], refs[-1]
    total = functools.reduce(jnp.add, [part[...] for part in parts])
    if not others:
        out_ref[...] = total
        return
    rows, width = total.shape
    for at in range(0, width, LANES):
        out_ref[pl.ds(at // LANES * rows, rows), :] = total[:, at : at + LANES]
    out_ref[pl.ds(width // LANES * rows, 8), :] = others[0][...]


def join(parts, scalars=None, cost=None):
    rows, width = parts[0].shape
    others = [] if scalars is None else [scalars]
    shape = (rows, width) if scalars is None else (width // LANES * rows + 8, LANES)
    return pl.pallas_call(
        functools.partial(join_kernel, len(parts)),
        out_shape=jax.ShapeDtypeStruct(shape, jnp.float32),
        in_specs=[VMEM] * (len(parts) + len(others)),
        out_specs=VMEM,
        cost_estimate=cost,
        compiler_params=PARAMS,
    )(*parts, *others)


def final_kernel(pairs, counts, fixed_ref, sums_ref, packed_ref, *refs):
    scale = fixed_ref[0:1, 0:1]
    ins, (image_ref, text_ref, loss_ref, scale_ref, bias_ref) = refs[:-5], refs[-5:]
    rows, width = image_ref.shape
    tail = packed_ref[pl.ds(width // LANES * rows, 8), :]
    sums = jnp.sum((sums_ref[...] + tail)[0:3, :], axis=1, keepdims=True) * (1.0 / pairs)
    loss_ref[0] = sums[0, 0]
    bias_ref[0] = sums[1, 0]
    scale_ref[0] = (scale * sums[2:3, :])[0, 0]
    pieces = [packed_ref[pl.ds(at * rows, rows), :] for at in range(width // LANES)]
    more = jnp.concatenate(pieces, axis=1)
    for own_ref, parts, out_ref in (
        (ins[0], ins[1 : 1 + counts[0]], image_ref),
        (ins[1 + counts[0]], ins[2 + counts[0] :], text_ref),
    ):
        total = functools.reduce(jnp.add, [part[...] for part in parts])
        grad = scale * (total + more if out_ref is text_ref else total)
        unit, norm = unit_rows(own_ref[...])
        out_ref[...] = (grad - unit * jnp.sum(unit * grad, axis=1, keepdims=True)) / norm


def final(pairs, fixed, scalars, packed, image, image_parts, text, text_parts):
    counts = (len(image_parts), len(text_parts))
    return pl.pallas_call(
        functools.partial(final_kernel, pairs, counts),
        out_shape=[jax.ShapeDtypeStruct(image.shape, jnp.float32)] * 2
        + [jax.ShapeDtypeStruct((1,), jnp.float32)] * 3,
        in_specs=[VMEM] * (5 + sum(counts)),
        out_specs=[VMEM] * 2 + [SMEM] * 3,
        compiler_params=PARAMS,
    )(fixed, scalars, packed, image, *image_parts, text, *text_parts)


def returns(steps):
    masks, order = [0], []
    for step in steps:
        order.insert(0, (step, [mask ^ step for mask in reversed(masks)]))
        masks += [mask ^ step for mask in masks]
    return order


def send_back(parts, step, masks, send):
    last = None
    for mask in masks:
        value = parts.pop(mask)
        value = value[0] if len(value) == 1 else join(value)
        last = send(value if last is None else after(value, last), step)
        parts[mask ^ step].append(last)


def per_device(count, image, text, labels, log_scale, bias):
    rows, width = image.shape
    pairs = rows * count
    me = lax.axis_index("row") * lax.axis_size("col") + lax.axis_index("col")
    image_steps, text_steps = generators(count)
    core = image_steps[-1]
    send = functools.partial(exchange, count=count)

    masks = [0]
    for step in text_steps:
        masks += [mask ^ step for mask in masks]
    fixed = constants(masks, rows, me.astype(jnp.int32).reshape(1), log_scale, bias)

    texts, norms = {0: text}, {}
    for step in text_steps:
        far = list(texts)[1:]
        texts[step] = send(text, step)
        for mask in far:
            norms[mask] = row_norms(texts[mask])
            texts[mask ^ step] = send(after(texts[mask], texts[step], norms[mask]), step)
    images = {0: pack(image, labels)}
    for step in image_steps[:-1]:
        far = list(images)[1:]
        images[step] = send(images[0], step)
        for mask in far:
            images[mask ^ step] = send(after(images[mask], images[step], fixed), step)
    near = list(images)
    for mask in near:
        block = images[mask]
        if mask == near[-1]:
            block = after(block, *norms.values())
        images[mask ^ core] = send(block, core)
    units = image_units(list(images.values()), rows, width)

    text_masks = list(texts)
    grads, scalars, sums = {}, (), ()
    for group in (text_masks[:-1], text_masks[-1:]):
        places = [masks.index(mask) for mask in group]
        blocks, known = [texts[mask] for mask in group], [norms.get(mask) for mask in group]
        parts, slope, unit, part = tile(places, fixed, units, blocks, known, scalars)
        grads.update(zip(group, parts))
        scalars = (part,)
        sums = image_grad(slope, unit, sums)
    keep, away = sums
    (scalars,) = scalars

    for step in [core] + image_steps[:-1]:
        scalars = scalars + send(scalars, step)
    text_parts = {mask: [part] for mask, part in grads.items()}
    for step, masks in returns(text_steps)[:-1]:
        send_back(text_parts, step, masks, send)
        scalars = after(scalars, text_parts[masks[0] ^ step][-1])
        scalars = scalars + send(scalars, step)
    packed = send(join(text_parts.pop(text_steps[0]), scalars, AHEAD), text_steps[0])
    kept = keep + send(away, core)
    image_parts = {mask: [kept[at * rows : (at + 1) * rows]] for at, mask in enumerate(near)}
    for step, masks in returns(image_steps[:-1]):
        send_back(image_parts, step, masks, send)

    grad_image, grad_text, loss, grad_log_scale, grad_bias = final(
        pairs, fixed, scalars, packed, image, image_parts[0], text, text_parts[0]
    )
    return (loss, grad_image, grad_text, grad_log_scale, grad_bias)


def solution(mesh):
    count = mesh.shape["row"] * mesh.shape["col"]
    return jax.shard_map(
        functools.partial(per_device, count),
        mesh=mesh,
        in_specs=(P(AXES, None), P(AXES, None), P(AXES), P(), P()),
        out_specs=(P(), P(AXES, None), P(AXES, None), P(), P()),
        check_vma=False,
    )
```

time: 90.6 us -> 65.3 us (0.72)
  starting transfers between devices: 30.3 us -> 17.8 us
  between operations: 7.43 us -> 2.06 us
  waiting for transfers between devices: 37.6 us -> 33.8 us
  other arithmetic: 3.35 us -> 0.18 us
  Pallas kernels: 11.5 us -> 9.52 us
  local copies, waits for them, and re-layouts: 0.12 us -> 1.7 us
    ppermute x22 -> x21, starting transfers between devices: 30.3 us -> 17.8 us  [exchange(): return lax.ppermute(value, AXES, [(i, i ^ step) for i in range(count)])]
    ppermute x22 -> x21, waiting for transfers between devices: 37.6 us -> 33.8 us  [exchange(): return lax.ppermute(value, AXES, [(i, i ^ step) for i in range(count)])]
    pallas_call x5 -> x9, Pallas kernels: 9.74 us -> 7.77 us  [the longest x2 5.67 us: tile(): pl.pallas_call(functools.partial(tile_kernel, places, normed), out_shape=...]
    unnamed x4 -> x8, local copies, waits for them, and re-layouts: 0.01 us -> 1.62 us
    concatenate x1 -> x0, other arithmetic: 0.98 us -> none  [per_device(): jnp.concatenate([image, jnp.pad(label_row, ((0, 7), (0, width - 2 * rows)...]
  transfers between devices with their start and end apart: 22 -> 21, of which waited for: 11 -> 12; matrix products, arithmetic and copies ran while one was open for 2% -> 0% of each run, Pallas kernels for 8% -> 10%
where the time goes in v2:
time: 65.3 us; the launch traced here: 65.1 us
  waiting for transfers between devices  33.8 us (52%)
  starting transfers between devices  17.8 us (27%)
  Pallas kernels  9.52 us (15%)
  between operations  2.06 us (3%)
  local copies, waits for them, and re-layouts  1.7 us (3%)
    ppermute x21, waiting for transfers between devices, exchange(): return lax.ppermute(value, AXES, [(i, i ^ step) for i in range(count)])  33.8 us
    ppermute x21, starting transfers between devices, exchange(): return lax.ppermute(value, AXES, [(i, i ^ step) for i in range(count)])  17.8 us
    pallas_call x2, Pallas kernels, tile(): pl.pallas_call(functools.partial(tile_kernel, places, normed), out_shape=...  5.67 us
    pallas_call x2, Pallas kernels, image_grad(): pl.pallas_call(image_grad_kernel, out_shape=[jax.ShapeDtypeStruct((half,...  1.75 us
    unnamed x8, local copies, waits for them, and re-layouts  1.62 us
  transfers between devices with their start and end apart: 21, of which 12 were waited for; matrix products, arithmetic and copies ran while one was open for 0% of the time, Pallas kernels for 10%

profile of v2, /device:TPU:0, one launch (start us, length us, event | category | flops | bytes accessed | tf_op | source)
XLA Modules:
  0.0 65.1 jit_solution(11520796575848219429)
XLA Ops:
  0.6 1.0 %copy-done.1 = f32[64,1152]{1,0:T(8,128)S(1)} copy-done((f32[64,1152]{1,0:T(8,128)S(1)}, f32[64,1152]{1,0:T(8,128)}, u32[]{:S(2)}) %copy-start.1) | copy-done | bytes 294936
  2.3 3.0 %collective-permute-start.1 = (f32[584,128]{1,0:T(8,128)S(1)}, f32[584,128]{1,0:T(8,128)S(1)}, u32[]{:S(2)}, u32[]{:S(2)}) collective-permute-start(f32[584,128]{1,0:T(8,128)S(1)} %shard_map.93.refs_0_), channel_id=1, source_target_pairs={{0,2},{1,3},{2,0},{3,1},{4,6},{5,7},{6,4},{7,5},{8,10},{9,11},{10,... | collective-permute-start | bytes 897032 | tf_op jit(solution)/shard_map/ppermute | solution.py:27
  5.3 1.5 %collective-permute-start = (f32[584,128]{1,0:T(8,128)S(1)}, f32[584,128]{1,0:T(8,128)S(1)}, u32[]{:S(2)}, u32[]{:S(2)}) collective-permute-start(f32[584,128]{1,0:T(8,128)S(1)} %shard_map.93.refs_0_), channel_id=1, source_target_pairs={{0,16},{1,17},{2,18},{3,19},{4,20},{5,21},{6,22},{7,23},{8,24},{9,... | collective-permute-start | bytes 897032 | tf_op jit(solution)/shard_map/ppermute | solution.py:27
  6.8 3.6 %collective-permute-start.6 = (f32[64,1152]{1,0:T(8,128)}, f32[64,1152]{1,0:T(8,128)S(1)}, u32[]{:S(2)}, u32[]{:S(2)}) collective-permute-start(f32[64,1152]{1,0:T(8,128)} %refs_4_.1), channel_id=1, source_target_pairs={{0,12},{1,13},{2,14},{3,15},{4,8},{5,9},{6,10},{7,11},{8,4},{9,5},... | collective-permute-start | bytes 884744 | tf_op jit(solution)/shard_map/ppermute | solution.py:27
  12.4 1.5 %collective-permute-done.refs_1_ = f32[584,128]{1,0:T(8,128)S(1)} collective-permute-done((f32[584,128]{1,0:T(8,128)S(1)}, f32[584,128]{1,0:T(8,128)S(1)}, u32[]{:S(2)}, u32[]{:S(2)}) %collective-permute-start) | collective-permute-done | bytes 299040 | tf_op jit(solution)/shard_map/ppermute | solution.py:27
  14.2 4.6 %collective-permute-done.6.block_ref.refs_1_ = f32[64,1152]{1,0:T(8,128)S(1)} collective-permute-done((f32[64,1152]{1,0:T(8,128)}, f32[64,1152]{1,0:T(8,128)S(1)}, u32[]{:S(2)}, u32[]{:S(2)}) %collective-permute-start.6) | collective-permute-done | bytes 294944 | tf_op jit(solution)/shard_map/ppermute | solution.py:27
  19.5 2.0 %collective-permute-done.2.refs_3_ = f32[584,128]{1,0:T(8,128)S(1)} collective-permute-done((f32[584,128]{1,0:T(8,128)S(1)}, f32[584,128]{1,0:T(8,128)S(1)}, u32[]{:S(2)}, u32[]{:S(2)}) %collective-permute-start.2) | collective-permute-done | bytes 299040 | tf_op jit(solution)/shard_map/ppermute | solution.py:27
  21.5 2.0 %collective-permute-done.8.refs_2_ = f32[64,1152]{1,0:T(8,128)S(1)} collective-permute-done((f32[64,1152]{1,0:T(8,128)}, f32[64,1152]{1,0:T(8,128)S(1)}, u32[]{:S(2)}, u32[]{:S(2)}) %collective-permute-start.8) | collective-permute-done | bytes 294944 | tf_op jit(solution)/shard_map/ppermute | solution.py:27
  23.5 1.7 %collective-permute-start.9 = (f32[64,1152]{1,0:T(8,128)S(1)}, f32[64,1152]{1,0:T(8,128)S(1)}, u32[]{:S(2)}, u32[]{:S(2)}) collective-permute-start(f32[64,1152]{1,0:T(8,128)S(1)} %collective-permute-done.6.block_ref.refs_1_), channel_id=1, source_target_pairs={{0,4},{1,5},{2,6},{3,7},{4,0},{5,1},{6,2},{7,3},{8,12},{9,13},{10,... | collective-permute-start | bytes 884744 | tf_op jit(solution)/shard_map/ppermute | solution.py:27
  25.2 0.7 %shard_map.95 = (bf16[512,1152]{1,0:T(8,128)(2,1)S(1)}, bf16[512,1152]{1,0:T(8,128)(2,1)S(1)}, f32[8,512]{1,0:T(8,128)S(1)}) custom-call(f32[584,128]{1,0:T(8,128)S(1)} %shard_map.93.refs_0_, f32[584,128]{1,0:T(8,128)S(1)} %collective-permute-done.refs_1_, f32[584,128]{1,0:T(8,128)S(1)} %collective-permute-done.1.refs_2_, ...), custom_call_target="tpu_custom_call" | custom-call | tf_op jit(solution)/shard_map/pallas_call | solution.py:112
  25.9 4.2 %shard_map.96 = (f32[64,1152]{1,0:T(8,128)S(1)}, f32[64,1152]{1,0:T(8,128)S(1)}, f32[64,1152]{1,0:T(8,128)S(1)}, bf16[576,512]{1,0:T(8,128)(2,1)S(1)}, bf16[576,...) custom-call(f32[8,128]{1,0:T(8,128)S(1)} %shard_map.92.fixed_ref, bf16[512,1152]{1,0:T(8,128)(2,1)S(1)} %get-tuple-element.35.high_ref, ...), custom_call_target="tpu_custom_call" | custom-call | tf_op jit(solution)/shard_map/pallas_call | solution.py:198
  30.1 1.2 %shard_map.99 = (f32[256,1152]{1,0:T(8,128)S(1)}, f32[256,1152]{1,0:T(8,128)S(1)}) custom-call(bf16[576,512]{1,0:T(8,128)(2,1)S(1)} %get-tuple-element.46.slope_ref, bf16[576,1152]{1,0:T(8,128)(2,1)S(1)} %get-tuple-element.47.unit_ref), custom_call_target="tpu_custom_call" | custom-call | tf_op jit(solution)/shard_map/pallas_call | solution.py:227
  31.3 1.1 %collective-permute-done.9.refs_0_ = f32[64,1152]{1,0:T(8,128)S(1)} collective-permute-done((f32[64,1152]{1,0:T(8,128)S(1)}, f32[64,1152]{1,0:T(8,128)S(1)}, u32[]{:S(2)}, u32[]{:S(2)}) %collective-permute-start.9) | collective-permute-done | bytes 294944 | tf_op jit(solution)/shard_map/ppermute | solution.py:27
  32.4 1.5 %shard_map.97 = (f32[64,1152]{1,0:T(8,128)S(1)}, bf16[192,512]{1,0:T(8,128)(2,1)S(1)}, bf16[192,1152]{1,0:T(8,128)(2,1)S(1)}, f32[8,128]{1,0:T(8,128)S(1)}) custom-call(f32[8,128]{1,0:T(8,128)S(1)} %shard_map.92.fixed_ref, bf16[512,1152]{1,0:T(8,128)(2,1)S(1)} %get-tuple-element.35.high_ref, bf16[512,1152]{1,0:T(8,128)(2,1)S(1)} %get-tuple-element.36.low_ref, ...), custom_call_target="tpu_custom_call" | custom-call | tf_op jit(solution)/shard_map/pallas_call | solution.py:198
  34.5 0.9 %collective-permute-start.13 = (f32[64,1152]{1,0:T(8,128)S(1)}, f32[64,1152]{1,0:T(8,128)S(1)}, u32[]{:S(2)}, u32[]{:S(2)}) collective-permute-start(f32[64,1152]{1,0:T(8,128)S(1)} %get-tuple-element.41), channel_id=1, source_target_pairs={{0,4},{1,5},{2,6},{3,7},{4,0},{5,1},{6,2},{7,3},{8,12},{9,13},{10,... | collective-permute-start | bytes 884744 | tf_op jit(solution)/shard_map/ppermute | solution.py:27
  35.6 1.8 %collective-permute-done.10 = f32[8,128]{1,0:T(8,128)S(1)} collective-permute-done((f32[8,128]{1,0:T(8,128)S(1)}, f32[8,128]{1,0:T(8,128)S(1)}, u32[]{:S(2)}, u32[]{:S(2)}) %collective-permute-start.10) | collective-permute-done | bytes 4128 | tf_op jit(solution)/shard_map/ppermute | solution.py:27
  37.9 3.1 %collective-permute-done.11 = f32[8,128]{1,0:T(8,128)S(1)} collective-permute-done((f32[8,128]{1,0:T(8,128)S(1)}, f32[8,128]{1,0:T(8,128)S(1)}, u32[]{:S(2)}, u32[]{:S(2)}) %collective-permute-start.11) | collective-permute-done | bytes 4128 | tf_op jit(solution)/shard_map/ppermute | solution.py:27
  41.5 3.1 %collective-permute-done.12 = f32[8,128]{1,0:T(8,128)S(1)} collective-permute-done((f32[8,128]{1,0:T(8,128)S(1)}, f32[8,128]{1,0:T(8,128)S(1)}, u32[]{:S(2)}, u32[]{:S(2)}) %collective-permute-start.12) | collective-permute-done | bytes 4128 | tf_op jit(solution)/shard_map/ppermute | solution.py:27
  44.6 0.8 %collective-permute-start.14 = (f32[8,128]{1,0:T(8,128)S(1)}, f32[8,128]{1,0:T(8,128)S(1)}, u32[]{:S(2)}, u32[]{:S(2)}) collective-permute-start(f32[8,128]{1,0:T(8,128)S(1)} %add.21), channel_id=1, source_target_pairs={{0,4},{1,5},{2,6},{3,7},{4,0},{5,1},{6,2},{7,3},{8,12},{9,13},{10,... | collective-permute-start | bytes 12296 | tf_op jit(solution)/shard_map/ppermute | solution.py:27
  45.4 2.8 %collective-permute-done.14 = f32[8,128]{1,0:T(8,128)S(1)} collective-permute-done((f32[8,128]{1,0:T(8,128)S(1)}, f32[8,128]{1,0:T(8,128)S(1)}, u32[]{:S(2)}, u32[]{:S(2)}) %collective-permute-start.14) | collective-permute-done | bytes 4128 | tf_op jit(solution)/shard_map/ppermute | solution.py:27
  49.1 2.3 %collective-permute-start.15 = (f32[584,128]{1,0:T(8,128)S(1)}, f32[584,128]{1,0:T(8,128)S(1)}, u32[]{:S(2)}, u32[]{:S(2)}) collective-permute-start(f32[584,128]{1,0:T(8,128)S(1)} %shard_map.98), channel_id=1, source_target_pairs={{0,12},{1,13},{2,14},{3,15},{4,8},{5,9},{6,10},{7,11},{8,4},{9,5},... | collective-permute-start | bytes 897032 | tf_op jit(solution)/shard_map/ppermute | solution.py:27
  51.6 4.4 %collective-permute-done.17.refs_1_ = f32[64,1152]{1,0:T(8,128)S(1)} collective-permute-done((f32[64,1152]{1,0:T(8,128)S(1)}, f32[64,1152]{1,0:T(8,128)S(1)}, u32[]{:S(2)}, u32[]{:S(2)}) %collective-permute-start.17) | collective-permute-done | bytes 294944 | tf_op jit(solution)/shard_map/ppermute | solution.py:27
  57.1 6.8 %collective-permute-done.20.refs_6_ = f32[64,1152]{1,0:T(8,128)S(1)} collective-permute-done((f32[64,1152]{1,0:T(8,128)S(1)}, f32[64,1152]{1,0:T(8,128)S(1)}, u32[]{:S(2)}, u32[]{:S(2)}) %collective-permute-start.20) | collective-permute-done | bytes 294944 | tf_op jit(solution)/shard_map/ppermute | solution.py:27
  64.0 1.1 %shard_map.102 = (f32[64,1152]{1,0:T(8,128)}, f32[64,1152]{1,0:T(8,128)}, f32[1]{0:T(128)}, f32[1]{0:T(128)}, f32[1]{0:T(128)}) custom-call(f32[8,128]{1,0:T(8,128)S(1)} %shard_map.92.fixed_ref, f32[8,128]{1,0:T(8,128)S(1)} %add.22.refs_2_.sums_ref, f32[584,128]{1,0:T(8,128)S(1)} %collective-permute-done.15.packed_ref, f32[64,1152]{1,0:T(8,128)S(1)} %copy-done.2, ...), custom_call_target="tpu_custom_call" | custom-call | tf_op jit(solution)/shard_map/pallas_call | solution.py:285
  (43 shorter events, 6.5 us)
Async XLA Ops:
  0.6 1.0 %copy-start.1 = (f32[64,1152]{1,0:T(8,128)S(1)}, f32[64,1152]{1,0:T(8,128)}, u32[]{:S(2)}) copy-start(f32[64,1152]{1,0:T(8,128)} %refs_0_.3) | copy-start | bytes 884740
  2.3 10.1 %collective-permute-start.1 = (f32[584,128]{1,0:T(8,128)S(1)}, f32[584,128]{1,0:T(8,128)S(1)}, u32[]{:S(2)}, u32[]{:S(2)}) collective-permute-start(f32[584,128]{1,0:T(8,128)S(1)} %shard_map.93.refs_0_), channel_id=1, source_target_pairs={{0,2},{1,3},{2,0},{3,1},{4,6},{5,7},{6,4},{7,5},{8,10},{9,11},{10,... | collective-permute-start | bytes 897032 | tf_op jit(solution)/shard_map/ppermute | solution.py:27
  5.3 8.6 %collective-permute-start = (f32[584,128]{1,0:T(8,128)S(1)}, f32[584,128]{1,0:T(8,128)S(1)}, u32[]{:S(2)}, u32[]{:S(2)}) collective-permute-start(f32[584,128]{1,0:T(8,128)S(1)} %shard_map.93.refs_0_), channel_id=1, source_target_pairs={{0,16},{1,17},{2,18},{3,19},{4,20},{5,21},{6,22},{7,23},{8,24},{9,... | collective-permute-start | bytes 897032 | tf_op jit(solution)/shard_map/ppermute | solution.py:27
  6.8 12.0 %collective-permute-start.6 = (f32[64,1152]{1,0:T(8,128)}, f32[64,1152]{1,0:T(8,128)S(1)}, u32[]{:S(2)}, u32[]{:S(2)}) collective-permute-start(f32[64,1152]{1,0:T(8,128)} %refs_4_.1), channel_id=1, source_target_pairs={{0,12},{1,13},{2,14},{3,15},{4,8},{5,9},{6,10},{7,11},{8,4},{9,5},... | collective-permute-start | bytes 884744 | tf_op jit(solution)/shard_map/ppermute | solution.py:27
  10.4 13.1 %collective-permute-start.8 = (f32[64,1152]{1,0:T(8,128)}, f32[64,1152]{1,0:T(8,128)S(1)}, u32[]{:S(2)}, u32[]{:S(2)}) collective-permute-start(f32[64,1152]{1,0:T(8,128)} %refs_4_.1), channel_id=1, source_target_pairs={{0,4},{1,5},{2,6},{3,7},{4,0},{5,1},{6,2},{7,3},{8,12},{9,13},{10,... | collective-permute-start | bytes 884744 | tf_op jit(solution)/shard_map/ppermute | solution.py:27
  10.4 14.8 %collective-permute-start.3 = (f32[584,128]{1,0:T(8,128)S(1)}, f32[584,128]{1,0:T(8,128)S(1)}, u32[]{:S(2)}, u32[]{:S(2)}) collective-permute-start(f32[584,128]{1,0:T(8,128)S(1)} %shard_map.93.refs_0_), channel_id=1, source_target_pairs={{0,1},{1,0},{2,3},{3,2},{4,5},{5,4},{6,7},{7,6},{8,9},{9,8},{10,11... | collective-permute-start | bytes 897032 | tf_op jit(solution)/shard_map/ppermute | solution.py:27
  13.9 7.6 %collective-permute-start.2 = (f32[584,128]{1,0:T(8,128)S(1)}, f32[584,128]{1,0:T(8,128)S(1)}, u32[]{:S(2)}, u32[]{:S(2)}) collective-permute-start(f32[584,128]{1,0:T(8,128)S(1)} %collective-permute-done.refs_1_), channel_id=1, source_target_pairs={{0,2},{1,3},{2,0},{3,1},{4,6},{5,7},{6,4},{7,5},{8,10},{9,11},{10,... | collective-permute-start | bytes 897032 | tf_op jit(solution)/shard_map/ppermute | solution.py:27
  18.9 7.0 %copy-start = (f32[64,1152]{1,0:T(8,128)S(1)}, f32[64,1152]{1,0:T(8,128)}, u32[]{:S(2)}) copy-start(f32[64,1152]{1,0:T(8,128)} %refs_4_.1) | copy-start | bytes 884740
  18.9 6.2 %collective-permute-start.5 = (f32[584,128]{1,0:T(8,128)S(1)}, f32[584,128]{1,0:T(8,128)S(1)}, u32[]{:S(2)}, u32[]{:S(2)}) collective-permute-start(f32[584,128]{1,0:T(8,128)S(1)} %collective-permute-done.1.refs_2_), channel_id=1, source_target_pairs={{0,1},{1,0},{2,3},{3,2},{4,5},{5,4},{6,7},{7,6},{8,9},{9,8},{10,11... | collective-permute-start | bytes 897032 | tf_op jit(solution)/shard_map/ppermute | solution.py:27
  19.0 6.2 %collective-permute-start.4 = (f32[584,128]{1,0:T(8,128)S(1)}, f32[584,128]{1,0:T(8,128)S(1)}, u32[]{:S(2)}, u32[]{:S(2)}) collective-permute-start(f32[584,128]{1,0:T(8,128)S(1)} %collective-permute-done.refs_1_), channel_id=1, source_target_pairs={{0,1},{1,0},{2,3},{3,2},{4,5},{5,4},{6,7},{7,6},{8,9},{9,8},{10,11... | collective-permute-start | bytes 897032 | tf_op jit(solution)/shard_map/ppermute | solution.py:27
  21.5 3.7 %collective-permute-start.7 = (f32[584,128]{1,0:T(8,128)S(1)}, f32[584,128]{1,0:T(8,128)S(1)}, u32[]{:S(2)}, u32[]{:S(2)}) collective-permute-start(f32[584,128]{1,0:T(8,128)S(1)} %collective-permute-done.2.refs_3_), channel_id=1, source_target_pairs={{0,1},{1,0},{2,3},{3,2},{4,5},{5,4},{6,7},{7,6},{8,9},{9,8},{10,11... | collective-permute-start | bytes 897032 | tf_op jit(solution)/shard_map/ppermute | solution.py:27
  23.5 8.9 %collective-permute-start.9 = (f32[64,1152]{1,0:T(8,128)S(1)}, f32[64,1152]{1,0:T(8,128)S(1)}, u32[]{:S(2)}, u32[]{:S(2)}) collective-permute-start(f32[64,1152]{1,0:T(8,128)S(1)} %collective-permute-done.6.block_ref.refs_1_), channel_id=1, source_target_pairs={{0,4},{1,5},{2,6},{3,7},{4,0},{5,1},{6,2},{7,3},{8,12},{9,13},{10,... | collective-permute-start | bytes 884744 | tf_op jit(solution)/shard_map/ppermute | solution.py:27
  34.5 13.8 %collective-permute-start.16 = (f32[256,1152]{1,0:T(8,128)S(1)}, f32[256,1152]{1,0:T(8,128)S(1)}, u32[]{:S(2)}, u32[]{:S(2)}) collective-permute-start(f32[256,1152]{1,0:T(8,128)S(1)} %get-tuple-element.51), channel_id=1, source_target_pairs={{0,1},{1,0},{2,3},{3,2},{4,5},{5,4},{6,7},{7,6},{8,9},{9,8},{10,11... | collective-permute-start | bytes 3538952 | tf_op jit(solution)/shard_map/ppermute | solution.py:27
  34.5 10.1 %collective-permute-start.13 = (f32[64,1152]{1,0:T(8,128)S(1)}, f32[64,1152]{1,0:T(8,128)S(1)}, u32[]{:S(2)}, u32[]{:S(2)}) collective-permute-start(f32[64,1152]{1,0:T(8,128)S(1)} %get-tuple-element.41), channel_id=1, source_target_pairs={{0,4},{1,5},{2,6},{3,7},{4,0},{5,1},{6,2},{7,3},{8,12},{9,13},{10,... | collective-permute-start | bytes 884744 | tf_op jit(solution)/shard_map/ppermute | solution.py:27
  35.4 2.0 %collective-permute-start.10 = (f32[8,128]{1,0:T(8,128)S(1)}, f32[8,128]{1,0:T(8,128)S(1)}, u32[]{:S(2)}, u32[]{:S(2)}) collective-permute-start(f32[8,128]{1,0:T(8,128)S(1)} %get-tuple-element.40), channel_id=1, source_target_pairs={{0,1},{1,0},{2,3},{3,2},{4,5},{5,4},{6,7},{7,6},{8,9},{9,8},{10,11... | collective-permute-start | bytes 12296 | tf_op jit(solution)/shard_map/ppermute | solution.py:27
  37.4 3.6 %collective-permute-start.11 = (f32[8,128]{1,0:T(8,128)S(1)}, f32[8,128]{1,0:T(8,128)S(1)}, u32[]{:S(2)}, u32[]{:S(2)}) collective-permute-start(f32[8,128]{1,0:T(8,128)S(1)} %add.19), channel_id=1, source_target_pairs={{0,16},{1,17},{2,18},{3,19},{4,20},{5,21},{6,22},{7,23},{8,24},{9,... | collective-permute-start | bytes 12296 | tf_op jit(solution)/shard_map/ppermute | solution.py:27
  41.0 3.6 %collective-permute-start.12 = (f32[8,128]{1,0:T(8,128)S(1)}, f32[8,128]{1,0:T(8,128)S(1)}, u32[]{:S(2)}, u32[]{:S(2)}) collective-permute-start(f32[8,128]{1,0:T(8,128)S(1)} %add.20), channel_id=1, source_target_pairs={{0,2},{1,3},{2,0},{3,1},{4,6},{5,7},{6,4},{7,5},{8,10},{9,11},{10,... | collective-permute-start | bytes 12296 | tf_op jit(solution)/shard_map/ppermute | solution.py:27
  44.6 3.6 %collective-permute-start.14 = (f32[8,128]{1,0:T(8,128)S(1)}, f32[8,128]{1,0:T(8,128)S(1)}, u32[]{:S(2)}, u32[]{:S(2)}) collective-permute-start(f32[8,128]{1,0:T(8,128)S(1)} %add.21), channel_id=1, source_target_pairs={{0,4},{1,5},{2,6},{3,7},{4,0},{5,1},{6,2},{7,3},{8,12},{9,13},{10,... | collective-permute-start | bytes 12296 | tf_op jit(solution)/shard_map/ppermute | solution.py:27
  48.5 7.5 %collective-permute-start.17 = (f32[64,1152]{1,0:T(8,128)S(1)}, f32[64,1152]{1,0:T(8,128)S(1)}, u32[]{:S(2)}, u32[]{:S(2)}) collective-permute-start(f32[64,1152]{1,0:T(8,128)S(1)} %get-tuple-element.62), channel_id=1, source_target_pairs={{0,2},{1,3},{2,0},{3,1},{4,6},{5,7},{6,4},{7,5},{8,10},{9,11},{10,... | collective-permute-start | bytes 884744 | tf_op jit(solution)/shard_map/ppermute | solution.py:27
  49.0 14.9 %copy-start.2 = (f32[64,1152]{1,0:T(8,128)S(1)}, f32[64,1152]{1,0:T(8,128)}, u32[]{:S(2)}) copy-start(f32[64,1152]{1,0:T(8,128)} %refs_0_.3) | copy-start | bytes 884740
  49.1 14.9 %collective-permute-start.15 = (f32[584,128]{1,0:T(8,128)S(1)}, f32[584,128]{1,0:T(8,128)S(1)}, u32[]{:S(2)}, u32[]{:S(2)}) collective-permute-start(f32[584,128]{1,0:T(8,128)S(1)} %shard_map.98), channel_id=1, source_target_pairs={{0,12},{1,13},{2,14},{3,15},{4,8},{5,9},{6,10},{7,11},{8,4},{9,5},... | collective-permute-start | bytes 897032 | tf_op jit(solution)/shard_map/ppermute | solution.py:27
  51.4 12.6 %collective-permute-start.20 = (f32[64,1152]{1,0:T(8,128)S(1)}, f32[64,1152]{1,0:T(8,128)S(1)}, u32[]{:S(2)}, u32[]{:S(2)}) collective-permute-start(f32[64,1152]{1,0:T(8,128)S(1)} %get-tuple-element.55), channel_id=1, source_target_pairs={{0,4},{1,5},{2,6},{3,7},{4,0},{5,1},{6,2},{7,3},{8,12},{9,13},{10,... | collective-permute-start | bytes 884744 | tf_op jit(solution)/shard_map/ppermute | solution.py:27
  56.0 8.0 %collective-permute-start.18 = (f32[64,1152]{1,0:T(8,128)S(1)}, f32[64,1152]{1,0:T(8,128)S(1)}, u32[]{:S(2)}, u32[]{:S(2)}) collective-permute-start(f32[64,1152]{1,0:T(8,128)S(1)} %get-tuple-element.52), channel_id=1, source_target_pairs={{0,2},{1,3},{2,0},{3,1},{4,6},{5,7},{6,4},{7,5},{8,10},{9,11},{10,... | collective-permute-start | bytes 884744 | tf_op jit(solution)/shard_map/ppermute | solution.py:27
  56.5 7.4 %collective-permute-start.19 = (f32[64,1152]{1,0:T(8,128)S(1)}, f32[64,1152]{1,0:T(8,128)S(1)}, u32[]{:S(2)}, u32[]{:S(2)}) collective-permute-start(f32[64,1152]{1,0:T(8,128)S(1)} %shard_map.101), channel_id=1, source_target_pairs={{0,16},{1,17},{2,18},{3,19},{4,20},{5,21},{6,22},{7,23},{8,24},{9,... | collective-permute-start | bytes 884744 | tf_op jit(solution)/shard_map/ppermute | solution.py:27
  (1 other events, 0.7 us)

commit v3 on v2

--- a/solution.py
+++ b/solution.py
@@ -9,6 +9,7 @@
 
 EPSILON = 1e-06
 LANES = 128
+PAD = 8
 AXES = ("row", "col")
 VMEM = pl.BlockSpec(memory_space=pltpu.VMEM)
 SMEM = pl.BlockSpec(memory_space=pltpu.SMEM)
@@ -71,19 +72,41 @@
     for at in range(0, width, LANES):
         out_ref[pl.ds(at // LANES * rows, rows), :] = image_ref[:, pl.ds(at, LANES)]
     label = label_ref[...].astype(jnp.float32)
-    tail = jnp.broadcast_to(jnp.concatenate([label, label], axis=1), (8, LANES))
-    out_ref[pl.ds(width // LANES * rows, 8), :] = tail
+    out_ref[pl.ds(width // LANES * rows, 1), :] = jnp.concatenate([label, label], axis=1)
 
 
 def pack(image, labels):
     rows, width = image.shape
     return pl.pallas_call(
         pack_kernel,
-        out_shape=jax.ShapeDtypeStruct((width // LANES * rows + 8, LANES), jnp.float32),
+        out_shape=jax.ShapeDtypeStruct((width // LANES * rows + 1, LANES), jnp.float32),
         in_specs=[VMEM] * 2,
         out_specs=VMEM,
         compiler_params=PARAMS,
     )(image, labels.reshape(1, rows))
+
+
+def pack_text_kernel(text_ref, out_ref):
+    rows, width = text_ref.shape
+    for at in range(0, width, LANES):
+        out_ref[pl.ds(at // LANES * rows, rows), :] = text_ref[:, pl.ds(at, LANES)]
+    rest = out_ref.shape[0] - width // LANES * rows
+    out_ref[pl.ds(width // LANES * rows, rest), :] = jnp.zeros((rest, LANES), jnp.float32)
+
+
+def pack_text(text):
+    rows, width = text.shape
+    return pl.pallas_call(
+        pack_text_kernel,
+        out_shape=jax.ShapeDtypeStruct((width // LANES * rows + PAD, LANES), jnp.float32),
+        in_specs=[VMEM],
+        out_specs=VMEM,
+        compiler_params=PARAMS,
+    )(text)
+
+
+def unpack(ref, rows):
+    return jnp.concatenate([ref[pl.ds(at, rows), :] for at in range(0, ref.shape[0] // rows * rows, rows)], axis=1)
 
 
 def image_kernel(count, *refs):
@@ -100,11 +123,11 @@
             high, low = halves(block[pl.ds(piece * rows, rows), :] / norm)
             high_ref[pl.ds(at * rows, rows), pl.ds(piece * LANES, LANES)] = high
             low_ref[pl.ds(at * rows, rows), pl.ds(piece * LANES, LANES)] = low
-    lane = lax.broadcasted_iota(jnp.int32, (8, LANES), 1)
-    tail = pl.ds(width // LANES * rows, 8)
+    lane = lax.broadcasted_iota(jnp.int32, (1, LANES), 1)
+    tail = pl.ds(width // LANES * rows, 1)
     for at in range(0, count, 2):
         pair = jnp.where(lane < rows, blocks[at][tail, :], blocks[at + 1][tail, :])
-        label_ref[:, pl.ds(at * rows, LANES)] = pair
+        label_ref[0:1, pl.ds(at * rows, LANES)] = pair
 
 
 def image_units(blocks, rows, width):
@@ -123,15 +146,15 @@
 
 
 def norm_kernel(block_ref, norm_ref):
-    block = block_ref[...]
+    block = unpack(block_ref, norm_ref.shape[0])
     norm = jnp.sqrt(jnp.sum(block * block, axis=1, keepdims=True) + EPSILON)
     norm_ref[...] = jnp.broadcast_to(norm, norm_ref.shape)
 
 
-def row_norms(block):
+def row_norms(block, rows):
     return pl.pallas_call(
         norm_kernel,
-        out_shape=jax.ShapeDtypeStruct((block.shape[0], LANES), jnp.float32),
+        out_shape=jax.ShapeDtypeStruct((rows, LANES), jnp.float32),
         in_specs=[VMEM],
         out_specs=VMEM,
         cost_estimate=AHEAD,
@@ -145,40 +168,43 @@
     norms, refs = dict(zip(normed, refs)), refs[len(normed) :]
     before, outs = refs[: -count - 3], refs[-count - 3 :]
     grads, (slope_ref, unit_ref, sums_ref) = outs[:count], outs[count:]
-    rows = texts[0].shape[0]
+    rows = grads[0].shape[0]
     total = high_ref.shape[0]
     scale, bias = fixed_ref[0:1, 0:1], fixed_ref[1:2, 0:1]
-    term_sum = jnp.zeros((1, total), jnp.float32)
-    slope_sum = jnp.zeros((1, total), jnp.float32)
-    product_sum = jnp.zeros((1, total), jnp.float32)
     labels = label_ref[0:1, :]
-    sub = lax.broadcasted_iota(jnp.int32, (rows, total), 0).astype(jnp.float32)
+    sub = lax.rem(lax.broadcasted_iota(jnp.int32, (count * rows, total), 0), rows).astype(jnp.float32)
+    wide = count * rows
+    units = []
     for at in range(count):
         if at in norms:
-            unit = texts[at][...] / norms[at][:, 0:1]
+            units.append(halves(unpack(texts[at], rows) / norms[at][:, 0:1]))
         else:
-            unit, _ = unit_rows(texts[at][...])
-        high, low = halves(unit)
-        unit_ref[pl.ds(at * 3 * rows, rows), :] = high
-        unit_ref[pl.ds(at * 3 * rows + rows, rows), :] = low
-        unit_ref[pl.ds(at * 3 * rows + 2 * rows, rows), :] = high
-        both = dot(jnp.concatenate([high, low], axis=0), high_ref[...], ((1,), (1,)))
-        cosine = both[:rows] + (both[rows:] + dot(high, low_ref[...], ((1,), (1,))))
-        logit = scale * cosine + bias
-        positive = sub + fixed_ref[2 + places[at] : 3 + places[at], 0:1] == labels
-        decay = jnp.exp(-jnp.abs(logit))
-        term = jnp.maximum(jnp.where(positive, -logit, logit), 0.0) + jnp.log1p(decay)
-        sigmoid = jnp.where(logit >= 0, 1.0, decay) / (1.0 + decay)
-        slope = sigmoid - positive.astype(jnp.float32)
-        term_sum += jnp.sum(term, axis=0, keepdims=True)
-        slope_sum += jnp.sum(slope, axis=0, keepdims=True)
-        product_sum += jnp.sum(slope * cosine, axis=0, keepdims=True)
-        slope_high, slope_low = halves(slope)
-        both = dot(jnp.concatenate([slope_high, slope_low], axis=0), high_ref[...], ((1,), (0,)))
-        grads[at][...] = both[:rows] + (both[rows:] + dot(slope_high, low_ref[...], ((1,), (0,))))
-        slope_ref[pl.ds(at * 3 * rows, rows), :] = slope_high
-        slope_ref[pl.ds(at * 3 * rows + rows, rows), :] = slope_high
-        slope_ref[pl.ds(at * 3 * rows + 2 * rows, rows), :] = slope_low
+            units.append(halves(unit_rows(unpack(texts[at], rows))[0]))
+    high = jnp.concatenate([unit[0] for unit in units], axis=0)
+    low = jnp.concatenate([unit[1] for unit in units], axis=0)
+    unit_ref[pl.ds(0, wide), :] = high
+    unit_ref[pl.ds(wide, wide), :] = low
+    unit_ref[pl.ds(2 * wide, wide), :] = high
+    both = dot(jnp.concatenate([high, low], axis=0), high_ref[...], ((1,), (1,)))
+    cosine = both[:wide] + (both[wide:] + dot(high, low_ref[...], ((1,), (1,))))
+    logit = scale * cosine + bias
+    first = [jnp.broadcast_to(fixed_ref[2 + place : 3 + place, 0:1], (rows, 1)) for place in places]
+    positive = sub + jnp.concatenate(first, axis=0) == labels
+    decay = jnp.exp(-jnp.abs(logit))
+    term = jnp.maximum(jnp.where(positive, -logit, logit), 0.0) + jnp.log1p(decay)
+    sigmoid = jnp.where(logit >= 0, 1.0, decay) / (1.0 + decay)
+    slope = sigmoid - positive.astype(jnp.float32)
+    term_sum = jnp.sum(term, axis=0, keepdims=True)
+    slope_sum = jnp.sum(slope, axis=0, keepdims=True)
+    product_sum = jnp.sum(slope * cosine, axis=0, keepdims=True)
+    slope_high, slope_low = halves(slope)
+    both = dot(jnp.concatenate([slope_high, slope_low], axis=0), high_ref[...], ((1,), (0,)))
+    both = both[:wide] + (both[wide:] + dot(slope_high, low_ref[...], ((1,), (0,))))
+    for at in range(count):
+        grads[at][...] = both[at * rows : (at + 1) * rows]
+    slope_ref[pl.ds(0, wide), :] = slope_high
+    slope_ref[pl.ds(wide, wide), :] = slope_high
+    slope_ref[pl.ds(2 * wide, wide), :] = slope_low
     parts = []
     for row in (term_sum, slope_sum, product_sum):
         part = row[:, 0:LANES]
@@ -189,9 +215,8 @@
     sums_ref[...] = before[0][...] + sums if before else sums
 
 
-def tile(places, fixed, images, texts, norms, before=()):
+def tile(rows, width, places, fixed, images, texts, norms, before=()):
     count = len(texts)
-    rows, width = texts[0].shape
     total = images[0].shape[0]
     normed = tuple(at for at, norm in enumerate(norms) if norm is not None)
     extra = [norms[at] for at in normed] + list(before)
@@ -259,37 +284,33 @@
     )(*parts, *others)
 
 
-def final_kernel(pairs, counts, fixed_ref, sums_ref, packed_ref, *refs):
+def final_kernel(pairs, counts, fixed_ref, sums_ref, *refs):
     scale = fixed_ref[0:1, 0:1]
     ins, (image_ref, text_ref, loss_ref, scale_ref, bias_ref) = refs[:-5], refs[-5:]
-    rows, width = image_ref.shape
-    tail = packed_ref[pl.ds(width // LANES * rows, 8), :]
-    sums = jnp.sum((sums_ref[...] + tail)[0:3, :], axis=1, keepdims=True) * (1.0 / pairs)
+    sums = jnp.sum(sums_ref[0:3, :], axis=1, keepdims=True) * (1.0 / pairs)
     loss_ref[0] = sums[0, 0]
     bias_ref[0] = sums[1, 0]
     scale_ref[0] = (scale * sums[2:3, :])[0, 0]
-    pieces = [packed_ref[pl.ds(at * rows, rows), :] for at in range(width // LANES)]
-    more = jnp.concatenate(pieces, axis=1)
     for own_ref, parts, out_ref in (
         (ins[0], ins[1 : 1 + counts[0]], image_ref),
         (ins[1 + counts[0]], ins[2 + counts[0] :], text_ref),
     ):
         total = functools.reduce(jnp.add, [part[...] for part in parts])
-        grad = scale * (total + more if out_ref is text_ref else total)
+        grad = scale * total
         unit, norm = unit_rows(own_ref[...])
         out_ref[...] = (grad - unit * jnp.sum(unit * grad, axis=1, keepdims=True)) / norm
 
 
-def final(pairs, fixed, scalars, packed, image, image_parts, text, text_parts):
+def final(pairs, fixed, scalars, image, image_parts, text, text_parts):
     counts = (len(image_parts), len(text_parts))
     return pl.pallas_call(
         functools.partial(final_kernel, pairs, counts),
         out_shape=[jax.ShapeDtypeStruct(image.shape, jnp.float32)] * 2
         + [jax.ShapeDtypeStruct((1,), jnp.float32)] * 3,
-        in_specs=[VMEM] * (5 + sum(counts)),
+        in_specs=[VMEM] * (4 + sum(counts)),
         out_specs=[VMEM] * 2 + [SMEM] * 3,
         compiler_params=PARAMS,
-    )(fixed, scalars, packed, image, *image_parts, text, *text_parts)
+    )(fixed, scalars, image, *image_parts, text, *text_parts)
 
 
 def returns(steps):
@@ -322,12 +343,12 @@
         masks += [mask ^ step for mask in masks]
     fixed = constants(masks, rows, me.astype(jnp.int32).reshape(1), log_scale, bias)
 
-    texts, norms = {0: text}, {}
+    texts, norms = {0: pack_text(text)}, {}
     for step in text_steps:
         far = list(texts)[1:]
-        texts[step] = send(text, step)
+        texts[step] = send(texts[0], step)
         for mask in far:
-            norms[mask] = row_norms(texts[mask])
+            norms[mask] = row_norms(texts[mask], rows)
             texts[mask ^ step] = send(after(texts[mask], texts[step], norms[mask]), step)
     images = {0: pack(image, labels)}
     for step in image_steps[:-1]:
@@ -348,28 +369,31 @@
     for group in (text_masks[:-1], text_masks[-1:]):
         places = [masks.index(mask) for mask in group]
         blocks, known = [texts[mask] for mask in group], [norms.get(mask) for mask in group]
-        parts, slope, unit, part = tile(places, fixed, units, blocks, known, scalars)
+        parts, slope, unit, part = tile(rows, width, places, fixed, units, blocks, known, scalars)
         grads.update(zip(group, parts))
         scalars = (part,)
         sums = image_grad(slope, unit, sums)
     keep, away = sums
     (scalars,) = scalars
 
-    for step in [core] + image_steps[:-1]:
-        scalars = scalars + send(scalars, step)
+    for step in text_steps[::-1]:
+        scalars = join([scalars, send(scalars, step)], cost=AHEAD)
     text_parts = {mask: [part] for mask, part in grads.items()}
-    for step, masks in returns(text_steps)[:-1]:
+    order = returns(text_steps)
+    for step, masks in order[:-1]:
         send_back(text_parts, step, masks, send)
-        scalars = after(scalars, text_parts[masks[0] ^ step][-1])
-        scalars = scalars + send(scalars, step)
-    packed = send(join(text_parts.pop(text_steps[0]), scalars, AHEAD), text_steps[0])
+    far = join(text_parts.pop(text_steps[0]))
+    scalars = after(scalars, far)
+    text_parts[0].append(send(far, text_steps[0]))
     kept = keep + send(away, core)
     image_parts = {mask: [kept[at * rows : (at + 1) * rows]] for at, mask in enumerate(near)}
     for step, masks in returns(image_steps[:-1]):
         send_back(image_parts, step, masks, send)
+    for step in image_steps[::-1]:
+        scalars = scalars + send(scalars, step)
 
     grad_image, grad_text, loss, grad_log_scale, grad_bias = final(
-        pairs, fixed, scalars, packed, image, image_parts[0], text, text_parts[0]
+        pairs, fixed, scalars, image, image_parts[0], text, text_parts[0]
     )
     return (loss, grad_image, grad_text, grad_log_scale, grad_bias)
 

time: 65.3 us -> 60.2 us (0.922)
  waiting for transfers between devices: 33.8 us -> 23.1 us
  starting transfers between devices: 17.8 us -> 24.2 us
  Pallas kernels: 9.52 us -> 7.78 us
  local copies, waits for them, and re-layouts: 1.7 us -> 2.66 us
    ppermute x21 -> x22, waiting for transfers between devices: 33.8 us -> 23.1 us  [exchange(): return lax.ppermute(value, AXES, [(i, i ^ step) for i in range(count)])]
    ppermute x21 -> x22, starting transfers between devices: 17.8 us -> 24.2 us  [exchange(): return lax.ppermute(value, AXES, [(i, i ^ step) for i in range(count)])]
    pallas_call x2, Pallas kernels: 5.67 us -> 3.94 us  [tile(): pl.pallas_call(functools.partial(tile_kernel, places, normed), out_shape=...]
    unnamed x8 -> x10, local copies, waits for them, and re-layouts: 1.62 us -> 2.59 us
  transfers between devices with their start and end apart: 21 -> 22, of which waited for: 12 -> 11; matrix products, arithmetic and copies ran while one was open for 0% -> 0% of each run, Pallas kernels for 10% -> 8%
where the time goes in v3:
time: 60.2 us; the launch traced here: 60 us
  starting transfers between devices  24.2 us (40%)
  waiting for transfers between devices  23.1 us (38%)
  Pallas kernels  7.78 us (13%)
  local copies, waits for them, and re-layouts  2.66 us (4%)
  between operations  2.07 us (3%)
    ppermute x22, starting transfers between devices, exchange(): return lax.ppermute(value, AXES, [(i, i ^ step) for i in range(count)])  24.2 us
    ppermute x22, waiting for transfers between devices, exchange(): return lax.ppermute(value, AXES, [(i, i ^ step) for i in range(count)])  23.1 us
    pallas_call x2, Pallas kernels, tile(): pl.pallas_call(functools.partial(tile_kernel, places, normed), out_shape=...  3.94 us
    unnamed x10, local copies, waits for them, and re-layouts  2.59 us
    pallas_call x2, Pallas kernels, image_grad(): pl.pallas_call(image_grad_kernel, out_shape=[jax.ShapeDtypeStruct((half,...  1.73 us
  transfers between devices with their start and end apart: 22, of which 11 were waited for; matrix products, arithmetic and copies ran while one was open for 0% of the time, Pallas kernels for 8%

profile of v3, /device:TPU:0, one launch (start us, length us, event | category | flops | bytes accessed | tf_op | source)
XLA Modules:
  0.0 60.0 jit_solution(17653910719421285762)
XLA Ops:
  1.6 5.1 %collective-permute-start.6 = (f32[584,128]{1,0:T(8,128)S(1)}, f32[584,128]{1,0:T(8,128)S(1)}, u32[]{:S(2)}, u32[]{:S(2)}) collective-permute-start(f32[584,128]{1,0:T(8,128)S(1)} %shard_map.94.refs_0_), channel_id=1, source_target_pairs={{0,12},{1,13},{2,14},{3,15},{4,8},{5,9},{6,10},{7,11},{8,4},{9,5},... | collective-permute-start | bytes 897032 | tf_op jit(solution)/shard_map/ppermute | solution.py:28
  8.4 1.5 %collective-permute-start.1 = (f32[577,128]{1,0:T(8,128)S(1)}, f32[577,128]{1,0:T(8,128)S(1)}, u32[]{:S(2)}, u32[]{:S(2)}) collective-permute-start(f32[577,128]{1,0:T(8,128)S(1)} %shard_map.93.refs_0_), channel_id=1, source_target_pairs={{0,2},{1,3},{2,0},{3,1},{4,6},{5,7},{6,4},{7,5},{8,10},{9,11},{10,... | collective-permute-start | bytes 886280 | tf_op jit(solution)/shard_map/ppermute | solution.py:28
  10.0 1.5 %collective-permute-start = (f32[577,128]{1,0:T(8,128)S(1)}, f32[577,128]{1,0:T(8,128)S(1)}, u32[]{:S(2)}, u32[]{:S(2)}) collective-permute-start(f32[577,128]{1,0:T(8,128)S(1)} %shard_map.93.refs_0_), channel_id=1, source_target_pairs={{0,16},{1,17},{2,18},{3,19},{4,20},{5,21},{6,22},{7,23},{8,24},{9,... | collective-permute-start | bytes 886280 | tf_op jit(solution)/shard_map/ppermute | solution.py:28
  12.8 4.2 %collective-permute-done.1.refs_2_ = f32[577,128]{1,0:T(8,128)S(1)} collective-permute-done((f32[577,128]{1,0:T(8,128)S(1)}, f32[577,128]{1,0:T(8,128)S(1)}, u32[]{:S(2)}, u32[]{:S(2)}) %collective-permute-start.1) | collective-permute-done | bytes 295456 | tf_op jit(solution)/shard_map/ppermute | solution.py:28
  17.0 1.2 %collective-permute-done.refs_1_ = f32[577,128]{1,0:T(8,128)S(1)} collective-permute-done((f32[577,128]{1,0:T(8,128)S(1)}, f32[577,128]{1,0:T(8,128)S(1)}, u32[]{:S(2)}, u32[]{:S(2)}) %collective-permute-start) | collective-permute-done | bytes 295456 | tf_op jit(solution)/shard_map/ppermute | solution.py:28
  18.9 1.5 %collective-permute-done.8.refs_2_ = f32[584,128]{1,0:T(8,128)S(1)} collective-permute-done((f32[584,128]{1,0:T(8,128)S(1)}, f32[584,128]{1,0:T(8,128)S(1)}, u32[]{:S(2)}, u32[]{:S(2)}) %collective-permute-start.8) | collective-permute-done | bytes 299040 | tf_op jit(solution)/shard_map/ppermute | solution.py:28
  20.3 1.7 %collective-permute-start.9 = (f32[584,128]{1,0:T(8,128)S(1)}, f32[584,128]{1,0:T(8,128)S(1)}, u32[]{:S(2)}, u32[]{:S(2)}) collective-permute-start(f32[584,128]{1,0:T(8,128)S(1)} %collective-permute-done.6.block_ref.refs_1_), channel_id=1, source_target_pairs={{0,4},{1,5},{2,6},{3,7},{4,0},{5,1},{6,2},{7,3},{8,12},{9,13},{10,... | collective-permute-start | bytes 897032 | tf_op jit(solution)/shard_map/ppermute | solution.py:28
  22.6 3.0 %collective-permute-done.2.refs_3_ = f32[577,128]{1,0:T(8,128)S(1)} collective-permute-done((f32[577,128]{1,0:T(8,128)S(1)}, f32[577,128]{1,0:T(8,128)S(1)}, u32[]{:S(2)}, u32[]{:S(2)}) %collective-permute-start.2) | collective-permute-done | bytes 295456 | tf_op jit(solution)/shard_map/ppermute | solution.py:28
  25.6 1.6 %collective-permute-done.7.refs_7_ = f32[577,128]{1,0:T(8,128)S(1)} collective-permute-done((f32[577,128]{1,0:T(8,128)S(1)}, f32[577,128]{1,0:T(8,128)S(1)}, u32[]{:S(2)}, u32[]{:S(2)}) %collective-permute-start.7) | collective-permute-done | bytes 295456 | tf_op jit(solution)/shard_map/ppermute | solution.py:28
  27.9 2.4 %shard_map.97 = (f32[64,1152]{1,0:T(8,128)S(1)}, f32[64,1152]{1,0:T(8,128)S(1)}, f32[64,1152]{1,0:T(8,128)S(1)}, bf16[576,512]{1,0:T(8,128)(2,1)S(1)}, bf16[576,...) custom-call(f32[8,128]{1,0:T(8,128)S(1)} %shard_map.92.fixed_ref, bf16[512,1152]{1,0:T(8,128)(2,1)S(1)} %get-tuple-element.35.high_ref, ...), custom_call_target="tpu_custom_call" | custom-call | tf_op jit(solution)/shard_map/pallas_call | solution.py:223
  30.3 1.2 %shard_map.102 = (f32[256,1152]{1,0:T(8,128)S(1)}, f32[256,1152]{1,0:T(8,128)S(1)}) custom-call(bf16[576,512]{1,0:T(8,128)(2,1)S(1)} %get-tuple-element.46.slope_ref, bf16[576,1152]{1,0:T(8,128)(2,1)S(1)} %get-tuple-element.47.unit_ref), custom_call_target="tpu_custom_call" | custom-call | tf_op jit(solution)/shard_map/pallas_call | solution.py:252
  31.5 1.5 %shard_map.98 = (f32[64,1152]{1,0:T(8,128)S(1)}, bf16[192,512]{1,0:T(8,128)(2,1)S(1)}, bf16[192,1152]{1,0:T(8,128)(2,1)S(1)}, f32[8,128]{1,0:T(8,128)S(1)}) custom-call(f32[8,128]{1,0:T(8,128)S(1)} %shard_map.92.fixed_ref, bf16[512,1152]{1,0:T(8,128)(2,1)S(1)} %get-tuple-element.35.high_ref, bf16[512,1152]{1,0:T(8,128)(2,1)S(1)} %get-tuple-element.36.low_ref, ...), custom_call_target="tpu_custom_call" | custom-call | tf_op jit(solution)/shard_map/pallas_call | solution.py:223
  33.8 2.0 %collective-permute-start.12 = (f32[64,1152]{1,0:T(8,128)S(1)}, f32[64,1152]{1,0:T(8,128)S(1)}, u32[]{:S(2)}, u32[]{:S(2)}) collective-permute-start(f32[64,1152]{1,0:T(8,128)S(1)} %get-tuple-element.42), channel_id=1, source_target_pairs={{0,4},{1,5},{2,6},{3,7},{4,0},{5,1},{6,2},{7,3},{8,12},{9,13},{10,... | collective-permute-start | bytes 884744 | tf_op jit(solution)/shard_map/ppermute | solution.py:28
  37.4 2.3 %collective-permute-start.11 = (f32[8,128]{1,0:T(8,128)S(1)}, f32[8,128]{1,0:T(8,128)S(1)}, u32[]{:S(2)}, u32[]{:S(2)}) collective-permute-start(f32[8,128]{1,0:T(8,128)S(1)} %shard_map.99.refs_0_), channel_id=1, source_target_pairs={{0,12},{1,13},{2,14},{3,15},{4,8},{5,9},{6,10},{7,11},{8,4},{9,5},... | collective-permute-start | bytes 12296 | tf_op jit(solution)/shard_map/ppermute | solution.py:28
  39.7 3.5 %collective-permute-done.12.refs_1_ = f32[64,1152]{1,0:T(8,128)S(1)} collective-permute-done((f32[64,1152]{1,0:T(8,128)S(1)}, f32[64,1152]{1,0:T(8,128)S(1)}, u32[]{:S(2)}, u32[]{:S(2)}) %collective-permute-start.12) | collective-permute-done | bytes 294944 | tf_op jit(solution)/shard_map/ppermute | solution.py:28
  43.2 1.7 %collective-permute-start.20 = (f32[64,1152]{1,0:T(8,128)S(1)}, f32[64,1152]{1,0:T(8,128)S(1)}, u32[]{:S(2)}, u32[]{:S(2)}) collective-permute-start(f32[64,1152]{1,0:T(8,128)S(1)} %get-tuple-element.55), channel_id=1, source_target_pairs={{0,4},{1,5},{2,6},{3,7},{4,0},{5,1},{6,2},{7,3},{8,12},{9,13},{10,... | collective-permute-start | bytes 884744 | tf_op jit(solution)/shard_map/ppermute | solution.py:28
  44.9 1.4 %collective-permute-start.21 = (f32[64,1152]{1,0:T(8,128)S(1)}, f32[64,1152]{1,0:T(8,128)S(1)}, u32[]{:S(2)}, u32[]{:S(2)}) collective-permute-start(f32[64,1152]{1,0:T(8,128)S(1)} %shard_map.101), channel_id=1, source_target_pairs={{0,12},{1,13},{2,14},{3,15},{4,8},{5,9},{6,10},{7,11},{8,4},{9,5},... | collective-permute-start | bytes 884744 | tf_op jit(solution)/shard_map/ppermute | solution.py:28
  46.3 1.5 %collective-permute-start.18 = (f32[64,1152]{1,0:T(8,128)S(1)}, f32[64,1152]{1,0:T(8,128)S(1)}, u32[]{:S(2)}, u32[]{:S(2)}) collective-permute-start(f32[64,1152]{1,0:T(8,128)S(1)} %get-tuple-element.52), channel_id=1, source_target_pairs={{0,2},{1,3},{2,0},{3,1},{4,6},{5,7},{6,4},{7,5},{8,10},{9,11},{10,... | collective-permute-start | bytes 884744 | tf_op jit(solution)/shard_map/ppermute | solution.py:28
  47.9 1.6 %collective-permute-start.19 = (f32[64,1152]{1,0:T(8,128)S(1)}, f32[64,1152]{1,0:T(8,128)S(1)}, u32[]{:S(2)}, u32[]{:S(2)}) collective-permute-start(f32[64,1152]{1,0:T(8,128)S(1)} %shard_map.104), channel_id=1, source_target_pairs={{0,16},{1,17},{2,18},{3,19},{4,20},{5,21},{6,22},{7,23},{8,24},{9,... | collective-permute-start | bytes 884744 | tf_op jit(solution)/shard_map/ppermute | solution.py:28
  49.5 1.2 %collective-permute-done.13 = f32[8,128]{1,0:T(8,128)S(1)} collective-permute-done((f32[8,128]{1,0:T(8,128)S(1)}, f32[8,128]{1,0:T(8,128)S(1)}, u32[]{:S(2)}, u32[]{:S(2)}) %collective-permute-start.13) | collective-permute-done | bytes 4128 | tf_op jit(solution)/shard_map/ppermute | solution.py:28
  51.2 3.1 %collective-permute-done.14 = f32[8,128]{1,0:T(8,128)S(1)} collective-permute-done((f32[8,128]{1,0:T(8,128)S(1)}, f32[8,128]{1,0:T(8,128)S(1)}, u32[]{:S(2)}, u32[]{:S(2)}) %collective-permute-start.14) | collective-permute-done | bytes 4128 | tf_op jit(solution)/shard_map/ppermute | solution.py:28
  54.3 1.4 %collective-permute-start.15 = (f32[8,128]{1,0:T(8,128)S(1)}, f32[8,128]{1,0:T(8,128)S(1)}, u32[]{:S(2)}, u32[]{:S(2)}) collective-permute-start(f32[8,128]{1,0:T(8,128)S(1)} %add.17), channel_id=1, source_target_pairs={{0,16},{1,17},{2,18},{3,19},{4,20},{5,21},{6,22},{7,23},{8,24},{9,... | collective-permute-start | bytes 12296 | tf_op jit(solution)/shard_map/ppermute | solution.py:28
  55.7 2.2 %collective-permute-done.15 = f32[8,128]{1,0:T(8,128)S(1)} collective-permute-done((f32[8,128]{1,0:T(8,128)S(1)}, f32[8,128]{1,0:T(8,128)S(1)}, u32[]{:S(2)}, u32[]{:S(2)}) %collective-permute-start.15) | collective-permute-done | bytes 4128 | tf_op jit(solution)/shard_map/ppermute | solution.py:28
  58.9 1.1 %shard_map.105 = (f32[64,1152]{1,0:T(8,128)}, f32[64,1152]{1,0:T(8,128)}, f32[1]{0:T(128)}, f32[1]{0:T(128)}, f32[1]{0:T(128)}) custom-call(f32[8,128]{1,0:T(8,128)S(1)} %shard_map.92.fixed_ref, f32[8,128]{1,0:T(8,128)S(1)} %add.18.sums_ref, f32[64,1152]{1,0:T(8,128)S(1)} %copy-done.3, f32[64,1152]{1,0:T(8,128)S(1)} %get-tuple-element.64.refs_1_, ...), custom_call_target="tpu_custom_call" | custom-call | tf_op jit(solution)/shard_map/pallas_call | solution.py:306
  (49 shorter events, 8.4 us)
Async XLA Ops:
  1.6 17.1 %collective-permute-start.6 = (f32[584,128]{1,0:T(8,128)S(1)}, f32[584,128]{1,0:T(8,128)S(1)}, u32[]{:S(2)}, u32[]{:S(2)}) collective-permute-start(f32[584,128]{1,0:T(8,128)S(1)} %shard_map.94.refs_0_), channel_id=1, source_target_pairs={{0,12},{1,13},{2,14},{3,15},{4,8},{5,9},{6,10},{7,11},{8,4},{9,5},... | collective-permute-start | bytes 897032 | tf_op jit(solution)/shard_map/ppermute | solution.py:28
  8.4 8.6 %collective-permute-start.1 = (f32[577,128]{1,0:T(8,128)S(1)}, f32[577,128]{1,0:T(8,128)S(1)}, u32[]{:S(2)}, u32[]{:S(2)}) collective-permute-start(f32[577,128]{1,0:T(8,128)S(1)} %shard_map.93.refs_0_), channel_id=1, source_target_pairs={{0,2},{1,3},{2,0},{3,1},{4,6},{5,7},{6,4},{7,5},{8,10},{9,11},{10,... | collective-permute-start | bytes 886280 | tf_op jit(solution)/shard_map/ppermute | solution.py:28
  10.0 8.3 %collective-permute-start = (f32[577,128]{1,0:T(8,128)S(1)}, f32[577,128]{1,0:T(8,128)S(1)}, u32[]{:S(2)}, u32[]{:S(2)}) collective-permute-start(f32[577,128]{1,0:T(8,128)S(1)} %shard_map.93.refs_0_), channel_id=1, source_target_pairs={{0,16},{1,17},{2,18},{3,19},{4,20},{5,21},{6,22},{7,23},{8,24},{9,... | collective-permute-start | bytes 886280 | tf_op jit(solution)/shard_map/ppermute | solution.py:28
  11.5 8.9 %collective-permute-start.8 = (f32[584,128]{1,0:T(8,128)S(1)}, f32[584,128]{1,0:T(8,128)S(1)}, u32[]{:S(2)}, u32[]{:S(2)}) collective-permute-start(f32[584,128]{1,0:T(8,128)S(1)} %shard_map.94.refs_0_), channel_id=1, source_target_pairs={{0,4},{1,5},{2,6},{3,7},{4,0},{5,1},{6,2},{7,3},{8,12},{9,13},{10,... | collective-permute-start | bytes 897032 | tf_op jit(solution)/shard_map/ppermute | solution.py:28
  18.2 7.3 %collective-permute-start.2 = (f32[577,128]{1,0:T(8,128)S(1)}, f32[577,128]{1,0:T(8,128)S(1)}, u32[]{:S(2)}, u32[]{:S(2)}) collective-permute-start(f32[577,128]{1,0:T(8,128)S(1)} %collective-permute-done.refs_1_), channel_id=1, source_target_pairs={{0,2},{1,3},{2,0},{3,1},{4,6},{5,7},{6,4},{7,5},{8,10},{9,11},{10,... | collective-permute-start | bytes 886280 | tf_op jit(solution)/shard_map/ppermute | solution.py:28
  20.3 11.2 %collective-permute-start.9 = (f32[584,128]{1,0:T(8,128)S(1)}, f32[584,128]{1,0:T(8,128)S(1)}, u32[]{:S(2)}, u32[]{:S(2)}) collective-permute-start(f32[584,128]{1,0:T(8,128)S(1)} %collective-permute-done.6.block_ref.refs_1_), channel_id=1, source_target_pairs={{0,4},{1,5},{2,6},{3,7},{4,0},{5,1},{6,2},{7,3},{8,12},{9,13},{10,... | collective-permute-start | bytes 897032 | tf_op jit(solution)/shard_map/ppermute | solution.py:28
  22.1 3.5 %collective-permute-start.3 = (f32[577,128]{1,0:T(8,128)S(1)}, f32[577,128]{1,0:T(8,128)S(1)}, u32[]{:S(2)}, u32[]{:S(2)}) collective-permute-start(f32[577,128]{1,0:T(8,128)S(1)} %shard_map.93.refs_0_), channel_id=1, source_target_pairs={{0,1},{1,0},{2,3},{3,2},{4,5},{5,4},{6,7},{7,6},{8,9},{9,8},{10,11... | collective-permute-start | bytes 886280 | tf_op jit(solution)/shard_map/ppermute | solution.py:28
  22.1 3.5 %collective-permute-start.5 = (f32[577,128]{1,0:T(8,128)S(1)}, f32[577,128]{1,0:T(8,128)S(1)}, u32[]{:S(2)}, u32[]{:S(2)}) collective-permute-start(f32[577,128]{1,0:T(8,128)S(1)} %collective-permute-done.1.refs_2_), channel_id=1, source_target_pairs={{0,1},{1,0},{2,3},{3,2},{4,5},{5,4},{6,7},{7,6},{8,9},{9,8},{10,11... | collective-permute-start | bytes 886280 | tf_op jit(solution)/shard_map/ppermute | solution.py:28
  22.6 3.0 %collective-permute-start.4 = (f32[577,128]{1,0:T(8,128)S(1)}, f32[577,128]{1,0:T(8,128)S(1)}, u32[]{:S(2)}, u32[]{:S(2)}) collective-permute-start(f32[577,128]{1,0:T(8,128)S(1)} %collective-permute-done.refs_1_), channel_id=1, source_target_pairs={{0,1},{1,0},{2,3},{3,2},{4,5},{5,4},{6,7},{7,6},{8,9},{9,8},{10,11... | collective-permute-start | bytes 886280 | tf_op jit(solution)/shard_map/ppermute | solution.py:28
  25.6 1.6 %collective-permute-start.7 = (f32[577,128]{1,0:T(8,128)S(1)}, f32[577,128]{1,0:T(8,128)S(1)}, u32[]{:S(2)}, u32[]{:S(2)}) collective-permute-start(f32[577,128]{1,0:T(8,128)S(1)} %collective-permute-done.2.refs_3_), channel_id=1, source_target_pairs={{0,1},{1,0},{2,3},{3,2},{4,5},{5,4},{6,7},{7,6},{8,9},{9,8},{10,11... | collective-permute-start | bytes 886280 | tf_op jit(solution)/shard_map/ppermute | solution.py:28
  33.6 2.9 %collective-permute-start.16 = (f32[256,1152]{1,0:T(8,128)S(1)}, f32[256,1152]{1,0:T(8,128)S(1)}, u32[]{:S(2)}, u32[]{:S(2)}) collective-permute-start(f32[256,1152]{1,0:T(8,128)S(1)} %get-tuple-element.51), channel_id=1, source_target_pairs={{0,1},{1,0},{2,3},{3,2},{4,5},{5,4},{6,7},{7,6},{8,9},{9,8},{10,11... | collective-permute-start | bytes 3538952 | tf_op jit(solution)/shard_map/ppermute | solution.py:28
  33.8 3.6 %collective-permute-start.10 = (f32[8,128]{1,0:T(8,128)S(1)}, f32[8,128]{1,0:T(8,128)S(1)}, u32[]{:S(2)}, u32[]{:S(2)}) collective-permute-start(f32[8,128]{1,0:T(8,128)S(1)} %get-tuple-element.40.refs_0_), channel_id=1, source_target_pairs={{0,4},{1,5},{2,6},{3,7},{4,0},{5,1},{6,2},{7,3},{8,12},{9,13},{10,... | collective-permute-start | bytes 12296 | tf_op jit(solution)/shard_map/ppermute | solution.py:28
  33.8 9.4 %collective-permute-start.12 = (f32[64,1152]{1,0:T(8,128)S(1)}, f32[64,1152]{1,0:T(8,128)S(1)}, u32[]{:S(2)}, u32[]{:S(2)}) collective-permute-start(f32[64,1152]{1,0:T(8,128)S(1)} %get-tuple-element.42), channel_id=1, source_target_pairs={{0,4},{1,5},{2,6},{3,7},{4,0},{5,1},{6,2},{7,3},{8,12},{9,13},{10,... | collective-permute-start | bytes 884744 | tf_op jit(solution)/shard_map/ppermute | solution.py:28
  36.7 9.6 %collective-permute-start.17 = (f32[64,1152]{1,0:T(8,128)S(1)}, f32[64,1152]{1,0:T(8,128)S(1)}, u32[]{:S(2)}, u32[]{:S(2)}) collective-permute-start(f32[64,1152]{1,0:T(8,128)S(1)} %get-tuple-element.62), channel_id=1, source_target_pairs={{0,2},{1,3},{2,0},{3,1},{4,6},{5,7},{6,4},{7,5},{8,10},{9,11},{10,... | collective-permute-start | bytes 884744 | tf_op jit(solution)/shard_map/ppermute | solution.py:28
  37.4 12.1 %collective-permute-start.11 = (f32[8,128]{1,0:T(8,128)S(1)}, f32[8,128]{1,0:T(8,128)S(1)}, u32[]{:S(2)}, u32[]{:S(2)}) collective-permute-start(f32[8,128]{1,0:T(8,128)S(1)} %shard_map.99.refs_0_), channel_id=1, source_target_pairs={{0,12},{1,13},{2,14},{3,15},{4,8},{5,9},{6,10},{7,11},{8,4},{9,5},... | collective-permute-start | bytes 12296 | tf_op jit(solution)/shard_map/ppermute | solution.py:28
  43.2 14.7 %collective-permute-start.20 = (f32[64,1152]{1,0:T(8,128)S(1)}, f32[64,1152]{1,0:T(8,128)S(1)}, u32[]{:S(2)}, u32[]{:S(2)}) collective-permute-start(f32[64,1152]{1,0:T(8,128)S(1)} %get-tuple-element.55), channel_id=1, source_target_pairs={{0,4},{1,5},{2,6},{3,7},{4,0},{5,1},{6,2},{7,3},{8,12},{9,13},{10,... | collective-permute-start | bytes 884744 | tf_op jit(solution)/shard_map/ppermute | solution.py:28
  44.9 13.9 %collective-permute-start.21 = (f32[64,1152]{1,0:T(8,128)S(1)}, f32[64,1152]{1,0:T(8,128)S(1)}, u32[]{:S(2)}, u32[]{:S(2)}) collective-permute-start(f32[64,1152]{1,0:T(8,128)S(1)} %shard_map.101), channel_id=1, source_target_pairs={{0,12},{1,13},{2,14},{3,15},{4,8},{5,9},{6,10},{7,11},{8,4},{9,5},... | collective-permute-start | bytes 884744 | tf_op jit(solution)/shard_map/ppermute | solution.py:28
  46.3 12.5 %collective-permute-start.18 = (f32[64,1152]{1,0:T(8,128)S(1)}, f32[64,1152]{1,0:T(8,128)S(1)}, u32[]{:S(2)}, u32[]{:S(2)}) collective-permute-start(f32[64,1152]{1,0:T(8,128)S(1)} %get-tuple-element.52), channel_id=1, source_target_pairs={{0,2},{1,3},{2,0},{3,1},{4,6},{5,7},{6,4},{7,5},{8,10},{9,11},{10,... | collective-permute-start | bytes 884744 | tf_op jit(solution)/shard_map/ppermute | solution.py:28
  47.9 11.0 %copy-start.1 = (f32[64,1152]{1,0:T(8,128)S(1)}, f32[64,1152]{1,0:T(8,128)}, u32[]{:S(2)}) copy-start(f32[64,1152]{1,0:T(8,128)} %refs_4_.1) | copy-start | bytes 884740
  47.9 11.0 %copy-start.3 = (f32[64,1152]{1,0:T(8,128)S(1)}, f32[64,1152]{1,0:T(8,128)}, u32[]{:S(2)}) copy-start(f32[64,1152]{1,0:T(8,128)} %refs_0_.1) | copy-start | bytes 884740
  47.9 10.9 %collective-permute-start.19 = (f32[64,1152]{1,0:T(8,128)S(1)}, f32[64,1152]{1,0:T(8,128)S(1)}, u32[]{:S(2)}, u32[]{:S(2)}) collective-permute-start(f32[64,1152]{1,0:T(8,128)S(1)} %shard_map.104), channel_id=1, source_target_pairs={{0,16},{1,17},{2,18},{3,19},{4,20},{5,21},{6,22},{7,23},{8,24},{9,... | collective-permute-start | bytes 884744 | tf_op jit(solution)/shard_map/ppermute | solution.py:28
  49.5 1.2 %collective-permute-start.13 = (f32[8,128]{1,0:T(8,128)S(1)}, f32[8,128]{1,0:T(8,128)S(1)}, u32[]{:S(2)}, u32[]{:S(2)}) collective-permute-start(f32[8,128]{1,0:T(8,128)S(1)} %shard_map.100), channel_id=1, source_target_pairs={{0,1},{1,0},{2,3},{3,2},{4,5},{5,4},{6,7},{7,6},{8,9},{9,8},{10,11... | collective-permute-start | bytes 12296 | tf_op jit(solution)/shard_map/ppermute | solution.py:28
  50.7 3.6 %collective-permute-start.14 = (f32[8,128]{1,0:T(8,128)S(1)}, f32[8,128]{1,0:T(8,128)S(1)}, u32[]{:S(2)}, u32[]{:S(2)}) collective-permute-start(f32[8,128]{1,0:T(8,128)S(1)} %add.16), channel_id=1, source_target_pairs={{0,2},{1,3},{2,0},{3,1},{4,6},{5,7},{6,4},{7,5},{8,10},{9,11},{10,... | collective-permute-start | bytes 12296 | tf_op jit(solution)/shard_map/ppermute | solution.py:28
  54.3 3.6 %collective-permute-start.15 = (f32[8,128]{1,0:T(8,128)S(1)}, f32[8,128]{1,0:T(8,128)S(1)}, u32[]{:S(2)}, u32[]{:S(2)}) collective-permute-start(f32[8,128]{1,0:T(8,128)S(1)} %add.17), channel_id=1, source_target_pairs={{0,16},{1,17},{2,18},{3,19},{4,20},{5,21},{6,22},{7,23},{8,24},{9,... | collective-permute-start | bytes 12296 | tf_op jit(solution)/shard_map/ppermute | solution.py:28
  (3 other events, 2.6 us)

commit v4 on v3

--- a/solution.py
+++ b/solution.py
@@ -20,8 +20,8 @@
 def generators(count):
     image, text = [], []
     for bit in range(1, count.bit_length() - 1):
-        (text if bit in (2, 3) or bit > 4 and bit % 2 else image).append(12 if bit == 3 else 1 << bit)
-    return image[::-1] + [1], text[::-1]
+        (text if bit in (2, 3) or bit > 4 and bit % 2 else image).append(1 << bit)
+    return image + [1], text[::-1]
 
 
 def exchange(value, step, count):
@@ -67,42 +67,38 @@
     )(me, log_scale, bias)
 
 
-def pack_kernel(image_ref, label_ref, out_ref):
+def pack_kernel(image_ref, text_ref, label_ref, image_out, text_out, image, text, labels, sems):
     rows, width = image_ref.shape
-    for at in range(0, width, LANES):
-        out_ref[pl.ds(at // LANES * rows, rows), :] = image_ref[:, pl.ds(at, LANES)]
-    label = label_ref[...].astype(jnp.float32)
-    out_ref[pl.ds(width // LANES * rows, 1), :] = jnp.concatenate([label, label], axis=1)
-
-
-def pack(image, labels):
+    moves = [(text_ref, text), (image_ref, image), (label_ref, labels)]
+    copies = [pltpu.make_async_copy(*move, sems.at[at]) for at, move in enumerate(moves)]
+    for copy in copies:
+        copy.start()
+    text_out[pl.ds(width // LANES * rows, PAD), :] = jnp.zeros((PAD, LANES), jnp.float32)
+    for copy, held, out in zip(copies, (text, image), (text_out, image_out)):
+        copy.wait()
+        for at in range(0, width, LANES):
+            out[pl.ds(at // LANES * rows, rows), :] = held[:, pl.ds(at, LANES)]
+    copies[2].wait()
+    label = labels[...].astype(jnp.float32)
+    image_out[pl.ds(width // LANES * rows, 1), :] = jnp.concatenate([label, label], axis=1)
+
+
+def pack(image, text, labels):
     rows, width = image.shape
+    pieces = width // LANES * rows
     return pl.pallas_call(
         pack_kernel,
-        out_shape=jax.ShapeDtypeStruct((width // LANES * rows + 1, LANES), jnp.float32),
-        in_specs=[VMEM] * 2,
-        out_specs=VMEM,
-        compiler_params=PARAMS,
-    )(image, labels.reshape(1, rows))
-
-
-def pack_text_kernel(text_ref, out_ref):
-    rows, width = text_ref.shape
-    for at in range(0, width, LANES):
-        out_ref[pl.ds(at // LANES * rows, rows), :] = text_ref[:, pl.ds(at, LANES)]
-    rest = out_ref.shape[0] - width // LANES * rows
-    out_ref[pl.ds(width // LANES * rows, rest), :] = jnp.zeros((rest, LANES), jnp.float32)
-
-
-def pack_text(text):
-    rows, width = text.shape
-    return pl.pallas_call(
-        pack_text_kernel,
-        out_shape=jax.ShapeDtypeStruct((width // LANES * rows + PAD, LANES), jnp.float32),
-        in_specs=[VMEM],
-        out_specs=VMEM,
-        compiler_params=PARAMS,
-    )(text)
+        out_shape=[jax.ShapeDtypeStruct((pieces + more, LANES), jnp.float32) for more in (1, PAD)],
+        in_specs=[pl.BlockSpec(memory_space=pltpu.HBM)] * 3,
+        out_specs=[VMEM] * 2,
+        scratch_shapes=[
+            pltpu.VMEM((rows, width), jnp.float32),
+            pltpu.VMEM((rows, width), jnp.float32),
+            pltpu.VMEM((1, rows), jnp.int32),
+            pltpu.SemaphoreType.DMA((3,)),
+        ],
+        compiler_params=pltpu.CompilerParams(vmem_limit_bytes=60 << 20),
+    )(image, text, labels.reshape(1, rows))
 
 
 def unpack(ref, rows):
@@ -343,24 +339,25 @@
         masks += [mask ^ step for mask in masks]
     fixed = constants(masks, rows, me.astype(jnp.int32).reshape(1), log_scale, bias)
 
-    texts, norms = {0: pack_text(text)}, {}
+    packed_image, packed_text = pack(image, text, labels)
+    texts, norms = {0: packed_text}, {}
     for step in text_steps:
         far = list(texts)[1:]
         texts[step] = send(texts[0], step)
         for mask in far:
             norms[mask] = row_norms(texts[mask], rows)
-            texts[mask ^ step] = send(after(texts[mask], texts[step], norms[mask]), step)
-    images = {0: pack(image, labels)}
+            texts[mask ^ step] = send(after(texts[mask], norms[mask]), step)
+    images = {0: packed_image}
     for step in image_steps[:-1]:
         far = list(images)[1:]
         images[step] = send(images[0], step)
         for mask in far:
-            images[mask ^ step] = send(after(images[mask], images[step], fixed), step)
+            images[mask ^ step] = send(after(images[mask], fixed), step)
     near = list(images)
     for mask in near:
         block = images[mask]
         if mask == near[-1]:
-            block = after(block, *norms.values())
+            block = after(block, *norms.values(), *(texts[step] for step in text_steps))
         images[mask ^ core] = send(block, core)
     units = image_units(list(images.values()), rows, width)
 
@@ -376,8 +373,11 @@
     keep, away = sums
     (scalars,) = scalars
 
-    for step in text_steps[::-1]:
+    for step in text_steps[:0:-1]:
         scalars = join([scalars, send(scalars, step)], cost=AHEAD)
+    scalars = scalars + send(scalars, core)
+    scalars = join([scalars, send(scalars, text_steps[0])], cost=AHEAD)
+
     text_parts = {mask: [part] for mask, part in grads.items()}
     order = returns(text_steps)
     for step, masks in order[:-1]:
@@ -389,7 +389,7 @@
     image_parts = {mask: [kept[at * rows : (at + 1) * rows]] for at, mask in enumerate(near)}
     for step, masks in returns(image_steps[:-1]):
         send_back(image_parts, step, masks, send)
-    for step in image_steps[::-1]:
+    for step in image_steps[-2::-1]:
         scalars = scalars + send(scalars, step)
 
     grad_image, grad_text, loss, grad_log_scale, grad_bias = final(

time: 60.2 us -> 58.2 us (0.967)
  waiting for transfers between devices: 23.1 us -> 20.5 us
  local copies, waits for them, and re-layouts: 2.66 us -> 0.1 us
  Pallas kernels: 7.78 us -> 9.61 us
  starting transfers between devices: 24.2 us -> 25.5 us
    ppermute x22, waiting for transfers between devices: 23.1 us -> 20.5 us  [exchange(): return lax.ppermute(value, AXES, [(i, i ^ step) for i in range(count)])]
    unnamed x10 -> x8, local copies, waits for them, and re-layouts: 2.59 us -> 0.02 us
    pallas_call x2 -> x1, Pallas kernels: 0.11 us -> 1.92 us  [pack(): pl.pallas_call(pack_kernel, out_shape=[jax.ShapeDtypeStruct((pieces + mor...]
    ppermute x22, starting transfers between devices: 24.2 us -> 25.5 us  [exchange(): return lax.ppermute(value, AXES, [(i, i ^ step) for i in range(count)])]
  transfers between devices with their start and end apart: 22 -> 22, of which waited for: 11 -> 9; matrix products, arithmetic and copies ran while one was open for 0% -> 0% of each run, Pallas kernels for 8% -> 8%
where the time goes in v4:
time: 58.2 us; the launch traced here: 58 us
  starting transfers between devices  25.5 us (44%)
  waiting for transfers between devices  20.5 us (35%)
  Pallas kernels  9.61 us (17%)
  between operations  2.11 us (4%)
    ppermute x22, starting transfers between devices, exchange(): return lax.ppermute(value, AXES, [(i, i ^ step) for i in range(count)])  25.5 us
    ppermute x22, waiting for transfers between devices, exchange(): return lax.ppermute(value, AXES, [(i, i ^ step) for i in range(count)])  20.5 us
    pallas_call x2, Pallas kernels, tile(): pl.pallas_call(functools.partial(tile_kernel, places, normed), out_shape=...  3.95 us
    pallas_call x1, Pallas kernels, pack(): pl.pallas_call(pack_kernel, out_shape=[jax.ShapeDtypeStruct((pieces + mor...  1.92 us
    pallas_call x2, Pallas kernels, image_grad(): pl.pallas_call(image_grad_kernel, out_shape=[jax.ShapeDtypeStruct((half,...  1.73 us
  transfers between devices with their start and end apart: 22, of which 9 were waited for; matrix products, arithmetic and copies ran while one was open for 0% of the time, Pallas kernels for 8%

profile of v4, /device:TPU:0, one launch (start us, length us, event | category | flops | bytes accessed | tf_op | source)
XLA Modules:
  0.0 58.0 jit_solution(6668261468696434690)
XLA Ops:
  0.6 1.9 %shard_map.93 = (f32[577,128]{1,0:T(8,128)}, f32[584,128]{1,0:T(8,128)}) custom-call(f32[64,1152]{1,0:T(8,128)} %refs_0_.1, f32[64,1152]{1,0:T(8,128)} %refs_4_.1, s32[1,64]{1,0:T(1,128)} %bitcast.2), custom_call_target="tpu_custom_call" | custom-call | tf_op jit(solution)/shard_map/pallas_call | solution.py:89
  2.6 4.1 %collective-permute-start.6 = (f32[584,128]{1,0:T(8,128)}, f32[584,128]{1,0:T(8,128)S(1)}, u32[]{:S(2)}, u32[]{:S(2)}) collective-permute-start(f32[584,128]{1,0:T(8,128)} %get-tuple-element.37.refs_0_), channel_id=1, source_target_pairs={{0,8},{1,9},{2,10},{3,11},{4,12},{5,13},{6,14},{7,15},{8,0},{9,1},... | collective-permute-start | bytes 897032 | tf_op jit(solution)/shard_map/ppermute | solution.py:28
  6.7 1.5 %collective-permute-start = (f32[577,128]{1,0:T(8,128)}, f32[577,128]{1,0:T(8,128)S(1)}, u32[]{:S(2)}, u32[]{:S(2)}) collective-permute-start(f32[577,128]{1,0:T(8,128)} %get-tuple-element.35.refs_0_), channel_id=1, source_target_pairs={{0,2},{1,3},{2,0},{3,1},{4,6},{5,7},{6,4},{7,5},{8,10},{9,11},{10,... | collective-permute-start | bytes 886280 | tf_op jit(solution)/shard_map/ppermute | solution.py:28
  8.2 1.6 %collective-permute-start.7 = (f32[584,128]{1,0:T(8,128)}, f32[584,128]{1,0:T(8,128)S(1)}, u32[]{:S(2)}, u32[]{:S(2)}) collective-permute-start(f32[584,128]{1,0:T(8,128)} %get-tuple-element.37.refs_0_), channel_id=1, source_target_pairs={{0,4},{1,5},{2,6},{3,7},{4,0},{5,1},{6,2},{7,3},{8,12},{9,13},{10,... | collective-permute-start | bytes 897032 | tf_op jit(solution)/shard_map/ppermute | solution.py:28
  9.8 1.5 %collective-permute-start.1 = (f32[577,128]{1,0:T(8,128)}, f32[577,128]{1,0:T(8,128)S(1)}, u32[]{:S(2)}, u32[]{:S(2)}) collective-permute-start(f32[577,128]{1,0:T(8,128)} %get-tuple-element.35.refs_0_), channel_id=1, source_target_pairs={{0,16},{1,17},{2,18},{3,19},{4,20},{5,21},{6,22},{7,23},{8,24},{9,... | collective-permute-start | bytes 886280 | tf_op jit(solution)/shard_map/ppermute | solution.py:28
  12.6 2.9 %collective-permute-done.refs_1_ = f32[577,128]{1,0:T(8,128)S(1)} collective-permute-done((f32[577,128]{1,0:T(8,128)}, f32[577,128]{1,0:T(8,128)S(1)}, u32[]{:S(2)}, u32[]{:S(2)}) %collective-permute-start) | collective-permute-done | bytes 295456 | tf_op jit(solution)/shard_map/ppermute | solution.py:28
  15.4 1.5 %collective-permute-start.2 = (f32[577,128]{1,0:T(8,128)S(1)}, f32[577,128]{1,0:T(8,128)S(1)}, u32[]{:S(2)}, u32[]{:S(2)}) collective-permute-start(f32[577,128]{1,0:T(8,128)S(1)} %collective-permute-done.refs_1_), channel_id=1, source_target_pairs={{0,16},{1,17},{2,18},{3,19},{4,20},{5,21},{6,22},{7,23},{8,24},{9,... | collective-permute-start | bytes 886280 | tf_op jit(solution)/shard_map/ppermute | solution.py:28
  16.9 3.6 %collective-permute-done.6.block_ref.refs_1_ = f32[584,128]{1,0:T(8,128)S(1)} collective-permute-done((f32[584,128]{1,0:T(8,128)}, f32[584,128]{1,0:T(8,128)S(1)}, u32[]{:S(2)}, u32[]{:S(2)}) %collective-permute-start.6) | collective-permute-done | bytes 299040 | tf_op jit(solution)/shard_map/ppermute | solution.py:28
  22.0 2.3 %collective-permute-done.2.refs_3_ = f32[577,128]{1,0:T(8,128)S(1)} collective-permute-done((f32[577,128]{1,0:T(8,128)S(1)}, f32[577,128]{1,0:T(8,128)S(1)}, u32[]{:S(2)}, u32[]{:S(2)}) %collective-permute-start.2) | collective-permute-done | bytes 295456 | tf_op jit(solution)/shard_map/ppermute | solution.py:28
  24.4 1.6 %collective-permute-done.8.refs_7_ = f32[577,128]{1,0:T(8,128)S(1)} collective-permute-done((f32[577,128]{1,0:T(8,128)S(1)}, f32[577,128]{1,0:T(8,128)S(1)}, u32[]{:S(2)}, u32[]{:S(2)}) %collective-permute-start.8) | collective-permute-done | bytes 295456 | tf_op jit(solution)/shard_map/ppermute | solution.py:28
  26.7 2.4 %shard_map.96 = (f32[64,1152]{1,0:T(8,128)S(1)}, f32[64,1152]{1,0:T(8,128)S(1)}, f32[64,1152]{1,0:T(8,128)S(1)}, bf16[576,512]{1,0:T(8,128)(2,1)S(1)}, bf16[576,...) custom-call(f32[8,128]{1,0:T(8,128)S(1)} %shard_map.92.fixed_ref, bf16[512,1152]{1,0:T(8,128)(2,1)S(1)} %get-tuple-element.39.high_ref, ...), custom_call_target="tpu_custom_call" | custom-call | tf_op jit(solution)/shard_map/pallas_call | solution.py:219
  29.1 1.2 %shard_map.101 = (f32[256,1152]{1,0:T(8,128)S(1)}, f32[256,1152]{1,0:T(8,128)S(1)}) custom-call(bf16[576,512]{1,0:T(8,128)(2,1)S(1)} %get-tuple-element.50.slope_ref, bf16[576,1152]{1,0:T(8,128)(2,1)S(1)} %get-tuple-element.51.unit_ref), custom_call_target="tpu_custom_call" | custom-call | tf_op jit(solution)/shard_map/pallas_call | solution.py:248
  30.3 1.5 %shard_map.97 = (f32[64,1152]{1,0:T(8,128)S(1)}, bf16[192,512]{1,0:T(8,128)(2,1)S(1)}, bf16[192,1152]{1,0:T(8,128)(2,1)S(1)}, f32[8,128]{1,0:T(8,128)S(1)}) custom-call(f32[8,128]{1,0:T(8,128)S(1)} %shard_map.92.fixed_ref, bf16[512,1152]{1,0:T(8,128)(2,1)S(1)} %get-tuple-element.39.high_ref, bf16[512,1152]{1,0:T(8,128)(2,1)S(1)} %get-tuple-element.40.low_ref, ...), custom_call_target="tpu_custom_call" | custom-call | tf_op jit(solution)/shard_map/pallas_call | solution.py:219
  33.1 1.6 %collective-permute-start.13 = (f32[64,1152]{1,0:T(8,128)S(1)}, f32[64,1152]{1,0:T(8,128)S(1)}, u32[]{:S(2)}, u32[]{:S(2)}) collective-permute-start(f32[64,1152]{1,0:T(8,128)S(1)} %get-tuple-element.46), channel_id=1, source_target_pairs={{0,4},{1,5},{2,6},{3,7},{4,0},{5,1},{6,2},{7,3},{8,12},{9,13},{10,... | collective-permute-start | bytes 884744 | tf_op jit(solution)/shard_map/ppermute | solution.py:28
  35.6 1.5 %collective-permute-start.17 = (f32[64,1152]{1,0:T(8,128)S(1)}, f32[64,1152]{1,0:T(8,128)S(1)}, u32[]{:S(2)}, u32[]{:S(2)}) collective-permute-start(f32[64,1152]{1,0:T(8,128)S(1)} %get-tuple-element.66), channel_id=1, source_target_pairs={{0,16},{1,17},{2,18},{3,19},{4,20},{5,21},{6,22},{7,23},{8,24},{9,... | collective-permute-start | bytes 884744 | tf_op jit(solution)/shard_map/ppermute | solution.py:28
  38.3 1.7 %collective-permute-start.12 = (f32[8,128]{1,0:T(8,128)S(1)}, f32[8,128]{1,0:T(8,128)S(1)}, u32[]{:S(2)}, u32[]{:S(2)}) collective-permute-start(f32[8,128]{1,0:T(8,128)S(1)} %add.16.refs_0_), channel_id=1, source_target_pairs={{0,8},{1,9},{2,10},{3,11},{4,12},{5,13},{6,14},{7,15},{8,0},{9,1},... | collective-permute-start | bytes 12296 | tf_op jit(solution)/shard_map/ppermute | solution.py:28
  40.0 2.2 %collective-permute-done.13.refs_1_ = f32[64,1152]{1,0:T(8,128)S(1)} collective-permute-done((f32[64,1152]{1,0:T(8,128)S(1)}, f32[64,1152]{1,0:T(8,128)S(1)}, u32[]{:S(2)}, u32[]{:S(2)}) %collective-permute-start.13) | collective-permute-done | bytes 294944 | tf_op jit(solution)/shard_map/ppermute | solution.py:28
  42.1 1.5 %collective-permute-start.20 = (f32[64,1152]{1,0:T(8,128)S(1)}, f32[64,1152]{1,0:T(8,128)S(1)}, u32[]{:S(2)}, u32[]{:S(2)}) collective-permute-start(f32[64,1152]{1,0:T(8,128)S(1)} %get-tuple-element.59), channel_id=1, source_target_pairs={{0,4},{1,5},{2,6},{3,7},{4,0},{5,1},{6,2},{7,3},{8,12},{9,13},{10,... | collective-permute-start | bytes 884744 | tf_op jit(solution)/shard_map/ppermute | solution.py:28
  43.7 1.8 %collective-permute-start.21 = (f32[64,1152]{1,0:T(8,128)S(1)}, f32[64,1152]{1,0:T(8,128)S(1)}, u32[]{:S(2)}, u32[]{:S(2)}) collective-permute-start(f32[64,1152]{1,0:T(8,128)S(1)} %shard_map.100), channel_id=1, source_target_pairs={{0,8},{1,9},{2,10},{3,11},{4,12},{5,13},{6,14},{7,15},{8,0},{9,1},... | collective-permute-start | bytes 884744 | tf_op jit(solution)/shard_map/ppermute | solution.py:28
  45.5 1.6 %collective-permute-start.18 = (f32[64,1152]{1,0:T(8,128)S(1)}, f32[64,1152]{1,0:T(8,128)S(1)}, u32[]{:S(2)}, u32[]{:S(2)}) collective-permute-start(f32[64,1152]{1,0:T(8,128)S(1)} %get-tuple-element.56), channel_id=1, source_target_pairs={{0,16},{1,17},{2,18},{3,19},{4,20},{5,21},{6,22},{7,23},{8,24},{9,... | collective-permute-start | bytes 884744 | tf_op jit(solution)/shard_map/ppermute | solution.py:28
  47.1 1.5 %collective-permute-start.19 = (f32[64,1152]{1,0:T(8,128)S(1)}, f32[64,1152]{1,0:T(8,128)S(1)}, u32[]{:S(2)}, u32[]{:S(2)}) collective-permute-start(f32[64,1152]{1,0:T(8,128)S(1)} %shard_map.103), channel_id=1, source_target_pairs={{0,2},{1,3},{2,0},{3,1},{4,6},{5,7},{6,4},{7,5},{8,10},{9,11},{10,... | collective-permute-start | bytes 884744 | tf_op jit(solution)/shard_map/ppermute | solution.py:28
  49.1 4.1 %collective-permute-done.14 = f32[8,128]{1,0:T(8,128)S(1)} collective-permute-done((f32[8,128]{1,0:T(8,128)S(1)}, f32[8,128]{1,0:T(8,128)S(1)}, u32[]{:S(2)}, u32[]{:S(2)}) %collective-permute-start.14) | collective-permute-done | bytes 4128 | tf_op jit(solution)/shard_map/ppermute | solution.py:28
  53.2 1.5 %collective-permute-start.15 = (f32[8,128]{1,0:T(8,128)S(1)}, f32[8,128]{1,0:T(8,128)S(1)}, u32[]{:S(2)}, u32[]{:S(2)}) collective-permute-start(f32[8,128]{1,0:T(8,128)S(1)} %add.17), channel_id=1, source_target_pairs={{0,2},{1,3},{2,0},{3,1},{4,6},{5,7},{6,4},{7,5},{8,10},{9,11},{10,... | collective-permute-start | bytes 12296 | tf_op jit(solution)/shard_map/ppermute | solution.py:28
  54.7 2.1 %collective-permute-done.15 = f32[8,128]{1,0:T(8,128)S(1)} collective-permute-done((f32[8,128]{1,0:T(8,128)S(1)}, f32[8,128]{1,0:T(8,128)S(1)}, u32[]{:S(2)}, u32[]{:S(2)}) %collective-permute-start.15) | collective-permute-done | bytes 4128 | tf_op jit(solution)/shard_map/ppermute | solution.py:28
  (46 shorter events, 7.2 us)
Async XLA Ops:
  2.6 17.9 %collective-permute-start.6 = (f32[584,128]{1,0:T(8,128)}, f32[584,128]{1,0:T(8,128)S(1)}, u32[]{:S(2)}, u32[]{:S(2)}) collective-permute-start(f32[584,128]{1,0:T(8,128)} %get-tuple-element.37.refs_0_), channel_id=1, source_target_pairs={{0,8},{1,9},{2,10},{3,11},{4,12},{5,13},{6,14},{7,15},{8,0},{9,1},... | collective-permute-start | bytes 897032 | tf_op jit(solution)/shard_map/ppermute | solution.py:28
  6.7 8.8 %collective-permute-start = (f32[577,128]{1,0:T(8,128)}, f32[577,128]{1,0:T(8,128)S(1)}, u32[]{:S(2)}, u32[]{:S(2)}) collective-permute-start(f32[577,128]{1,0:T(8,128)} %get-tuple-element.35.refs_0_), channel_id=1, source_target_pairs={{0,2},{1,3},{2,0},{3,1},{4,6},{5,7},{6,4},{7,5},{8,10},{9,11},{10,... | collective-permute-start | bytes 886280 | tf_op jit(solution)/shard_map/ppermute | solution.py:28
  8.2 13.8 %collective-permute-start.7 = (f32[584,128]{1,0:T(8,128)}, f32[584,128]{1,0:T(8,128)S(1)}, u32[]{:S(2)}, u32[]{:S(2)}) collective-permute-start(f32[584,128]{1,0:T(8,128)} %get-tuple-element.37.refs_0_), channel_id=1, source_target_pairs={{0,4},{1,5},{2,6},{3,7},{4,0},{5,1},{6,2},{7,3},{8,12},{9,13},{10,... | collective-permute-start | bytes 897032 | tf_op jit(solution)/shard_map/ppermute | solution.py:28
  9.8 11.7 %collective-permute-start.1 = (f32[577,128]{1,0:T(8,128)}, f32[577,128]{1,0:T(8,128)S(1)}, u32[]{:S(2)}, u32[]{:S(2)}) collective-permute-start(f32[577,128]{1,0:T(8,128)} %get-tuple-element.35.refs_0_), channel_id=1, source_target_pairs={{0,16},{1,17},{2,18},{3,19},{4,20},{5,21},{6,22},{7,23},{8,24},{9,... | collective-permute-start | bytes 886280 | tf_op jit(solution)/shard_map/ppermute | solution.py:28
  15.4 8.9 %collective-permute-start.2 = (f32[577,128]{1,0:T(8,128)S(1)}, f32[577,128]{1,0:T(8,128)S(1)}, u32[]{:S(2)}, u32[]{:S(2)}) collective-permute-start(f32[577,128]{1,0:T(8,128)S(1)} %collective-permute-done.refs_1_), channel_id=1, source_target_pairs={{0,16},{1,17},{2,18},{3,19},{4,20},{5,21},{6,22},{7,23},{8,24},{9,... | collective-permute-start | bytes 886280 | tf_op jit(solution)/shard_map/ppermute | solution.py:28
  20.6 9.7 %collective-permute-start.9 = (f32[584,128]{1,0:T(8,128)S(1)}, f32[584,128]{1,0:T(8,128)S(1)}, u32[]{:S(2)}, u32[]{:S(2)}) collective-permute-start(f32[584,128]{1,0:T(8,128)S(1)} %collective-permute-done.6.block_ref.refs_1_), channel_id=1, source_target_pairs={{0,4},{1,5},{2,6},{3,7},{4,0},{5,1},{6,2},{7,3},{8,12},{9,13},{10,... | collective-permute-start | bytes 897032 | tf_op jit(solution)/shard_map/ppermute | solution.py:28
  21.4 2.9 %collective-permute-start.3 = (f32[577,128]{1,0:T(8,128)S(1)}, f32[577,128]{1,0:T(8,128)S(1)}, u32[]{:S(2)}, u32[]{:S(2)}) collective-permute-start(f32[577,128]{1,0:T(8,128)S(1)} %copy-done.3), channel_id=1, source_target_pairs={{0,1},{1,0},{2,3},{3,2},{4,5},{5,4},{6,7},{7,6},{8,9},{9,8},{10,11... | collective-permute-start | bytes 886280 | tf_op jit(solution)/shard_map/ppermute | solution.py:28
  21.4 2.9 %collective-permute-start.4 = (f32[577,128]{1,0:T(8,128)S(1)}, f32[577,128]{1,0:T(8,128)S(1)}, u32[]{:S(2)}, u32[]{:S(2)}) collective-permute-start(f32[577,128]{1,0:T(8,128)S(1)} %collective-permute-done.refs_1_), channel_id=1, source_target_pairs={{0,1},{1,0},{2,3},{3,2},{4,5},{5,4},{6,7},{7,6},{8,9},{9,8},{10,11... | collective-permute-start | bytes 886280 | tf_op jit(solution)/shard_map/ppermute | solution.py:28
  22.0 2.4 %collective-permute-start.5 = (f32[577,128]{1,0:T(8,128)S(1)}, f32[577,128]{1,0:T(8,128)S(1)}, u32[]{:S(2)}, u32[]{:S(2)}) collective-permute-start(f32[577,128]{1,0:T(8,128)S(1)} %collective-permute-done.1.refs_2_), channel_id=1, source_target_pairs={{0,1},{1,0},{2,3},{3,2},{4,5},{5,4},{6,7},{7,6},{8,9},{9,8},{10,11... | collective-permute-start | bytes 886280 | tf_op jit(solution)/shard_map/ppermute | solution.py:28
  24.4 1.6 %collective-permute-start.8 = (f32[577,128]{1,0:T(8,128)S(1)}, f32[577,128]{1,0:T(8,128)S(1)}, u32[]{:S(2)}, u32[]{:S(2)}) collective-permute-start(f32[577,128]{1,0:T(8,128)S(1)} %collective-permute-done.2.refs_3_), channel_id=1, source_target_pairs={{0,1},{1,0},{2,3},{3,2},{4,5},{5,4},{6,7},{7,6},{8,9},{9,8},{10,11... | collective-permute-start | bytes 886280 | tf_op jit(solution)/shard_map/ppermute | solution.py:28
  32.4 2.9 %collective-permute-start.16 = (f32[256,1152]{1,0:T(8,128)S(1)}, f32[256,1152]{1,0:T(8,128)S(1)}, u32[]{:S(2)}, u32[]{:S(2)}) collective-permute-start(f32[256,1152]{1,0:T(8,128)S(1)} %get-tuple-element.55), channel_id=1, source_target_pairs={{0,1},{1,0},{2,3},{3,2},{4,5},{5,4},{6,7},{7,6},{8,9},{9,8},{10,11... | collective-permute-start | bytes 3538952 | tf_op jit(solution)/shard_map/ppermute | solution.py:28
  32.6 4.5 %collective-permute-start.10 = (f32[8,128]{1,0:T(8,128)S(1)}, f32[8,128]{1,0:T(8,128)S(1)}, u32[]{:S(2)}, u32[]{:S(2)}) collective-permute-start(f32[8,128]{1,0:T(8,128)S(1)} %get-tuple-element.44.refs_0_), channel_id=1, source_target_pairs={{0,4},{1,5},{2,6},{3,7},{4,0},{5,1},{6,2},{7,3},{8,12},{9,13},{10,... | collective-permute-start | bytes 12296 | tf_op jit(solution)/shard_map/ppermute | solution.py:28
  33.1 9.1 %collective-permute-start.13 = (f32[64,1152]{1,0:T(8,128)S(1)}, f32[64,1152]{1,0:T(8,128)S(1)}, u32[]{:S(2)}, u32[]{:S(2)}) collective-permute-start(f32[64,1152]{1,0:T(8,128)S(1)} %get-tuple-element.46), channel_id=1, source_target_pairs={{0,4},{1,5},{2,6},{3,7},{4,0},{5,1},{6,2},{7,3},{8,12},{9,13},{10,... | collective-permute-start | bytes 884744 | tf_op jit(solution)/shard_map/ppermute | solution.py:28
  35.6 9.9 %collective-permute-start.17 = (f32[64,1152]{1,0:T(8,128)S(1)}, f32[64,1152]{1,0:T(8,128)S(1)}, u32[]{:S(2)}, u32[]{:S(2)}) collective-permute-start(f32[64,1152]{1,0:T(8,128)S(1)} %get-tuple-element.66), channel_id=1, source_target_pairs={{0,16},{1,17},{2,18},{3,19},{4,20},{5,21},{6,22},{7,23},{8,24},{9,... | collective-permute-start | bytes 884744 | tf_op jit(solution)/shard_map/ppermute | solution.py:28
  37.1 1.2 %collective-permute-start.11 = (f32[8,128]{1,0:T(8,128)S(1)}, f32[8,128]{1,0:T(8,128)S(1)}, u32[]{:S(2)}, u32[]{:S(2)}) collective-permute-start(f32[8,128]{1,0:T(8,128)S(1)} %shard_map.98), channel_id=1, source_target_pairs={{0,1},{1,0},{2,3},{3,2},{4,5},{5,4},{6,7},{7,6},{8,9},{9,8},{10,11... | collective-permute-start | bytes 12296 | tf_op jit(solution)/shard_map/ppermute | solution.py:28
  38.3 10.4 %collective-permute-start.12 = (f32[8,128]{1,0:T(8,128)S(1)}, f32[8,128]{1,0:T(8,128)S(1)}, u32[]{:S(2)}, u32[]{:S(2)}) collective-permute-start(f32[8,128]{1,0:T(8,128)S(1)} %add.16.refs_0_), channel_id=1, source_target_pairs={{0,8},{1,9},{2,10},{3,11},{4,12},{5,13},{6,14},{7,15},{8,0},{9,1},... | collective-permute-start | bytes 12296 | tf_op jit(solution)/shard_map/ppermute | solution.py:28
  42.1 14.7 %collective-permute-start.20 = (f32[64,1152]{1,0:T(8,128)S(1)}, f32[64,1152]{1,0:T(8,128)S(1)}, u32[]{:S(2)}, u32[]{:S(2)}) collective-permute-start(f32[64,1152]{1,0:T(8,128)S(1)} %get-tuple-element.59), channel_id=1, source_target_pairs={{0,4},{1,5},{2,6},{3,7},{4,0},{5,1},{6,2},{7,3},{8,12},{9,13},{10,... | collective-permute-start | bytes 884744 | tf_op jit(solution)/shard_map/ppermute | solution.py:28
  43.7 13.1 %collective-permute-start.21 = (f32[64,1152]{1,0:T(8,128)S(1)}, f32[64,1152]{1,0:T(8,128)S(1)}, u32[]{:S(2)}, u32[]{:S(2)}) collective-permute-start(f32[64,1152]{1,0:T(8,128)S(1)} %shard_map.100), channel_id=1, source_target_pairs={{0,8},{1,9},{2,10},{3,11},{4,12},{5,13},{6,14},{7,15},{8,0},{9,1},... | collective-permute-start | bytes 884744 | tf_op jit(solution)/shard_map/ppermute | solution.py:28
  45.5 11.3 %collective-permute-start.18 = (f32[64,1152]{1,0:T(8,128)S(1)}, f32[64,1152]{1,0:T(8,128)S(1)}, u32[]{:S(2)}, u32[]{:S(2)}) collective-permute-start(f32[64,1152]{1,0:T(8,128)S(1)} %get-tuple-element.56), channel_id=1, source_target_pairs={{0,16},{1,17},{2,18},{3,19},{4,20},{5,21},{6,22},{7,23},{8,24},{9,... | collective-permute-start | bytes 884744 | tf_op jit(solution)/shard_map/ppermute | solution.py:28
  47.1 9.8 %copy-start = (f32[64,1152]{1,0:T(8,128)S(1)}, f32[64,1152]{1,0:T(8,128)}, u32[]{:S(2)}) copy-start(f32[64,1152]{1,0:T(8,128)} %refs_0_.1) | copy-start | bytes 884740
  47.1 9.8 %copy-start.1 = (f32[64,1152]{1,0:T(8,128)S(1)}, f32[64,1152]{1,0:T(8,128)}, u32[]{:S(2)}) copy-start(f32[64,1152]{1,0:T(8,128)} %refs_4_.1) | copy-start | bytes 884740
  47.1 9.7 %collective-permute-start.19 = (f32[64,1152]{1,0:T(8,128)S(1)}, f32[64,1152]{1,0:T(8,128)S(1)}, u32[]{:S(2)}, u32[]{:S(2)}) collective-permute-start(f32[64,1152]{1,0:T(8,128)S(1)} %shard_map.103), channel_id=1, source_target_pairs={{0,2},{1,3},{2,0},{3,1},{4,6},{5,7},{6,4},{7,5},{8,10},{9,11},{10,... | collective-permute-start | bytes 884744 | tf_op jit(solution)/shard_map/ppermute | solution.py:28
  48.7 4.5 %collective-permute-start.14 = (f32[8,128]{1,0:T(8,128)S(1)}, f32[8,128]{1,0:T(8,128)S(1)}, u32[]{:S(2)}, u32[]{:S(2)}) collective-permute-start(f32[8,128]{1,0:T(8,128)S(1)} %shard_map.99), channel_id=1, source_target_pairs={{0,16},{1,17},{2,18},{3,19},{4,20},{5,21},{6,22},{7,23},{8,24},{9,... | collective-permute-start | bytes 12296 | tf_op jit(solution)/shard_map/ppermute | solution.py:28
  53.2 3.6 %collective-permute-start.15 = (f32[8,128]{1,0:T(8,128)S(1)}, f32[8,128]{1,0:T(8,128)S(1)}, u32[]{:S(2)}, u32[]{:S(2)}) collective-permute-start(f32[8,128]{1,0:T(8,128)S(1)} %add.17), channel_id=1, source_target_pairs={{0,2},{1,3},{2,0},{3,1},{4,6},{5,7},{6,4},{7,5},{8,10},{9,11},{10,... | collective-permute-start | bytes 12296 | tf_op jit(solution)/shard_map/ppermute | solution.py:28
  (2 other events, 15.0 us)

commit v5 on v4

--- a/solution.py
+++ b/solution.py
@@ -105,8 +105,8 @@
     return jnp.concatenate([ref[pl.ds(at, rows), :] for at in range(0, ref.shape[0] // rows * rows, rows)], axis=1)
 
 
-def image_kernel(count, *refs):
-    blocks, (high_ref, low_ref, label_ref) = refs[:count], refs[count:]
+def image_units(blocks, high_ref, low_ref, label_ref):
+    count = len(blocks)
     rows = high_ref.shape[0] // count
     width = high_ref.shape[1]
     for at, block in enumerate(blocks):
@@ -126,21 +126,6 @@
         label_ref[0:1, pl.ds(at * rows, LANES)] = pair
 
 
-def image_units(blocks, rows, width):
-    total = rows * len(blocks)
-    return pl.pallas_call(
-        functools.partial(image_kernel, len(blocks)),
-        out_shape=[
-            jax.ShapeDtypeStruct((total, width), jnp.bfloat16),
-            jax.ShapeDtypeStruct((total, width), jnp.bfloat16),
-            jax.ShapeDtypeStruct((8, total), jnp.float32),
-        ],
-        in_specs=[VMEM] * len(blocks),
-        out_specs=[VMEM] * 3,
-        compiler_params=PARAMS,
-    )(*blocks)
-
-
 def norm_kernel(block_ref, norm_ref):
     block = unpack(block_ref, norm_ref.shape[0])
     norm = jnp.sqrt(jnp.sum(block * block, axis=1, keepdims=True) + EPSILON)
@@ -158,12 +143,18 @@
     )(block)
 
 
-def tile_kernel(places, normed, fixed_ref, high_ref, low_ref, label_ref, *refs):
+def tile_kernel(places, normed, blocks, first, fixed_ref, *refs):
     count = len(places)
     texts, refs = refs[:count], refs[count:]
     norms, refs = dict(zip(normed, refs)), refs[len(normed) :]
-    before, outs = refs[: -count - 3], refs[-count - 3 :]
-    grads, (slope_ref, unit_ref, sums_ref) = outs[:count], outs[count:]
+    sums_ref, away_ref, keep_ref = refs[-1], refs[-2], refs[-3]
+    grads, refs = refs[-3 - count : -3], refs[: -3 - count]
+    if first:
+        high_ref, low_ref, label_ref = refs[blocks:]
+        image_units(refs[:blocks], high_ref, low_ref, label_ref)
+        before = ()
+    else:
+        high_ref, low_ref, label_ref, *before = refs
     rows = grads[0].shape[0]
     total = high_ref.shape[0]
     scale, bias = fixed_ref[0:1, 0:1], fixed_ref[1:2, 0:1]
@@ -178,80 +169,57 @@
             units.append(halves(unit_rows(unpack(texts[at], rows))[0]))
     high = jnp.concatenate([unit[0] for unit in units], axis=0)
     low = jnp.concatenate([unit[1] for unit in units], axis=0)
-    unit_ref[pl.ds(0, wide), :] = high
-    unit_ref[pl.ds(wide, wide), :] = low
-    unit_ref[pl.ds(2 * wide, wide), :] = high
     both = dot(jnp.concatenate([high, low], axis=0), high_ref[...], ((1,), (1,)))
     cosine = both[:wide] + (both[wide:] + dot(high, low_ref[...], ((1,), (1,))))
     logit = scale * cosine + bias
-    first = [jnp.broadcast_to(fixed_ref[2 + place : 3 + place, 0:1], (rows, 1)) for place in places]
-    positive = sub + jnp.concatenate(first, axis=0) == labels
+    starts = [jnp.broadcast_to(fixed_ref[2 + place : 3 + place, 0:1], (rows, 1)) for place in places]
+    positive = sub + jnp.concatenate(starts, axis=0) == labels
     decay = jnp.exp(-jnp.abs(logit))
     term = jnp.maximum(jnp.where(positive, -logit, logit), 0.0) + jnp.log1p(decay)
     sigmoid = jnp.where(logit >= 0, 1.0, decay) / (1.0 + decay)
     slope = sigmoid - positive.astype(jnp.float32)
-    term_sum = jnp.sum(term, axis=0, keepdims=True)
-    slope_sum = jnp.sum(slope, axis=0, keepdims=True)
-    product_sum = jnp.sum(slope * cosine, axis=0, keepdims=True)
+    parts = []
+    for value in (term, slope, slope * cosine):
+        row = jnp.sum(value, axis=0, keepdims=True)
+        parts.append(functools.reduce(jnp.add, [row[:, at : at + LANES] for at in range(0, total, LANES)]))
+    sums = jnp.concatenate(parts + [jnp.zeros((5, LANES), jnp.float32)], axis=0)
     slope_high, slope_low = halves(slope)
     both = dot(jnp.concatenate([slope_high, slope_low], axis=0), high_ref[...], ((1,), (0,)))
     both = both[:wide] + (both[wide:] + dot(slope_high, low_ref[...], ((1,), (0,))))
     for at in range(count):
         grads[at][...] = both[at * rows : (at + 1) * rows]
-    slope_ref[pl.ds(0, wide), :] = slope_high
-    slope_ref[pl.ds(wide, wide), :] = slope_high
-    slope_ref[pl.ds(2 * wide, wide), :] = slope_low
-    parts = []
-    for row in (term_sum, slope_sum, product_sum):
-        part = row[:, 0:LANES]
-        for at in range(LANES, total, LANES):
-            part += row[:, at : at + LANES]
-        parts.append(part)
-    sums = jnp.concatenate(parts + [jnp.zeros((5, LANES), jnp.float32)], axis=0)
-    sums_ref[...] = before[0][...] + sums if before else sums
-
-
-def tile(rows, width, places, fixed, images, texts, norms, before=()):
+    slopes = jnp.concatenate([slope_high, slope_high, slope_low], axis=0)
+    image = dot(slopes, jnp.concatenate([high, low, high], axis=0), ((0,), (0,)))
+    half = total // 2
+    if before:
+        keep_ref[...] = before[0][...] + image[:half]
+        away_ref[...] = before[1][...] + image[half:]
+        sums_ref[...] = before[2][...] + sums
+    else:
+        keep_ref[...] = image[:half]
+        away_ref[...] = image[half:]
+        sums_ref[...] = sums
+
+
+def tile(rows, width, places, fixed, texts, norms, blocks=(), before=()):
     count = len(texts)
-    total = images[0].shape[0]
+    total = rows * len(blocks) if blocks else before[0].shape[0]
     normed = tuple(at for at, norm in enumerate(norms) if norm is not None)
-    extra = [norms[at] for at in normed] + list(before)
+    inputs = [fixed, *texts, *(norms[at] for at in normed), *blocks, *before]
+    shapes = [jax.ShapeDtypeStruct((total, width), jnp.bfloat16)] * 2 if blocks else []
+    shapes += [jax.ShapeDtypeStruct((8, total), jnp.float32)] if blocks else []
+    units = len(shapes)
+    shapes += [jax.ShapeDtypeStruct((rows, width), jnp.float32)] * count
+    shapes += [jax.ShapeDtypeStruct((total // 2, width), jnp.float32)] * 2
+    shapes += [jax.ShapeDtypeStruct((8, LANES), jnp.float32)]
     out = pl.pallas_call(
-        functools.partial(tile_kernel, places, normed),
-        out_shape=[jax.ShapeDtypeStruct((rows, width), jnp.float32)] * count
-        + [
-            jax.ShapeDtypeStruct((3 * count * rows, total), jnp.bfloat16),
-            jax.ShapeDtypeStruct((3 * count * rows, width), jnp.bfloat16),
-            jax.ShapeDtypeStruct((8, LANES), jnp.float32),
-        ],
-        in_specs=[VMEM] * (4 + count + len(extra)),
-        out_specs=[VMEM] * (count + 3),
-        compiler_params=PARAMS,
-    )(fixed, *images, *texts, *extra)
-    return out[:count], out[count], out[count + 1], out[count + 2]
-
-
-def image_grad_kernel(slope_ref, unit_ref, *refs):
-    before, (keep_ref, send_ref) = refs[:-2], refs[-2:]
-    total = dot(slope_ref[...], unit_ref[...], ((0,), (0,)))
-    half = keep_ref.shape[0]
-    if before:
-        keep_ref[...] = before[0][...] + total[:half]
-        send_ref[...] = before[1][...] + total[half:]
-    else:
-        keep_ref[...] = total[:half]
-        send_ref[...] = total[half:]
-
-
-def image_grad(slope, unit, before=()):
-    half, width = slope.shape[1] // 2, unit.shape[1]
-    return pl.pallas_call(
-        image_grad_kernel,
-        out_shape=[jax.ShapeDtypeStruct((half, width), jnp.float32)] * 2,
-        in_specs=[VMEM] * (2 + len(before)),
-        out_specs=[VMEM] * 2,
-        compiler_params=PARAMS,
-    )(slope, unit, *before)
+        functools.partial(tile_kernel, places, normed, len(blocks), bool(blocks)),
+        out_shape=shapes,
+        in_specs=[VMEM] * len(inputs),
+        out_specs=[VMEM] * len(shapes),
+        compiler_params=PARAMS,
+    )(*inputs)
+    return out[:units], out[units : units + count], out[-3:]
 
 
 def join_kernel(count, *refs):
@@ -359,22 +327,21 @@
         if mask == near[-1]:
             block = after(block, *norms.values(), *(texts[step] for step in text_steps))
         images[mask ^ core] = send(block, core)
-    units = image_units(list(images.values()), rows, width)
 
     text_masks = list(texts)
-    grads, scalars, sums = {}, (), ()
+    grads, units, sums = {}, (), ()
     for group in (text_masks[:-1], text_masks[-1:]):
         places = [masks.index(mask) for mask in group]
-        blocks, known = [texts[mask] for mask in group], [norms.get(mask) for mask in group]
-        parts, slope, unit, part = tile(rows, width, places, fixed, units, blocks, known, scalars)
+        arrays, known = [texts[mask] for mask in group], [norms.get(mask) for mask in group]
+        blocks = () if units else list(images.values())
+        made, parts, sums = tile(rows, width, places, fixed, arrays, known, blocks, [*units, *sums])
+        units = units or made
         grads.update(zip(group, parts))
-        scalars = (part,)
-        sums = image_grad(slope, unit, sums)
-    keep, away = sums
-    (scalars,) = scalars
+    keep, away, scalars = sums
 
     for step in text_steps[:0:-1]:
         scalars = join([scalars, send(scalars, step)], cost=AHEAD)
+    near_sums = scalars
     scalars = scalars + send(scalars, core)
     scalars = join([scalars, send(scalars, text_steps[0])], cost=AHEAD)
 
@@ -385,11 +352,11 @@
     far = join(text_parts.pop(text_steps[0]))
     scalars = after(scalars, far)
     text_parts[0].append(send(far, text_steps[0]))
-    kept = keep + send(away, core)
+    kept = keep + after(send(away, core), near_sums)
     image_parts = {mask: [kept[at * rows : (at + 1) * rows]] for at, mask in enumerate(near)}
     for step, masks in returns(image_steps[:-1]):
         send_back(image_parts, step, masks, send)
-    for step in image_steps[-2::-1]:
+    for step in image_steps[:-1]:
         scalars = scalars + send(scalars, step)
 
     grad_image, grad_text, loss, grad_log_scale, grad_bias = final(

time: 58.2 us -> 58.2 us (level)
  Pallas kernels: 9.61 us -> 8.91 us
  starting transfers between devices: 25.5 us -> 26.2 us
    ppermute x22, starting transfers between devices: 25.5 us -> 26.2 us  [exchange(): return lax.ppermute(value, AXES, [(i, i ^ step) for i in range(count)])]
    pallas_call x5 -> x2, Pallas kernels: 6.39 us -> 5.67 us  [tile(): pl.pallas_call(functools.partial(tile_kernel, places, normed, len(blocks)...]
  transfers between devices with their start and end apart: 22 -> 22, of which waited for: 9 -> 9; matrix products, arithmetic and copies ran while one was open for 0% -> 0% of each run, Pallas kernels for 8% -> 7%
where the time goes in v5:
time: 58.2 us; the launch traced here: 58 us
  starting transfers between devices  26.2 us (45%)
  waiting for transfers between devices  20.6 us (35%)
  Pallas kernels  8.91 us (15%)
  between operations  2.07 us (4%)
    ppermute x22, starting transfers between devices, exchange(): return lax.ppermute(value, AXES, [(i, i ^ step) for i in range(count)])  26.2 us
    ppermute x22, waiting for transfers between devices, exchange(): return lax.ppermute(value, AXES, [(i, i ^ step) for i in range(count)])  20.6 us
    pallas_call x2, Pallas kernels, tile(): pl.pallas_call(functools.partial(tile_kernel, places, normed, len(blocks)...  5.67 us
    pallas_call x1, Pallas kernels, pack(): pl.pallas_call(pack_kernel, out_shape=[jax.ShapeDtypeStruct((pieces + mor...  1.93 us
  transfers between devices with their start and end apart: 22, of which 9 were waited for; matrix products, arithmetic and copies ran while one was open for 0% of the time, Pallas kernels for 7%

profile of v5, /device:TPU:0, one launch (start us, length us, event | category | flops | bytes accessed | tf_op | source)
XLA Modules:
  0.0 58.0 jit_solution(662650102733856867)
XLA Ops:
  0.6 1.9 %shard_map.93 = (f32[577,128]{1,0:T(8,128)}, f32[584,128]{1,0:T(8,128)}) custom-call(f32[64,1152]{1,0:T(8,128)} %refs_0_.1, f32[64,1152]{1,0:T(8,128)} %refs_4_.1, s32[1,64]{1,0:T(1,128)} %bitcast.2), custom_call_target="tpu_custom_call" | custom-call | tf_op jit(solution)/shard_map/pallas_call | solution.py:89
  2.6 4.1 %collective-permute-start = (f32[584,128]{1,0:T(8,128)}, f32[584,128]{1,0:T(8,128)S(1)}, u32[]{:S(2)}, u32[]{:S(2)}) collective-permute-start(f32[584,128]{1,0:T(8,128)} %get-tuple-element.32.refs_0_), channel_id=1, source_target_pairs={{0,8},{1,9},{2,10},{3,11},{4,12},{5,13},{6,14},{7,15},{8,0},{9,1},... | collective-permute-start | bytes 897032 | tf_op jit(solution)/shard_map/ppermute | solution.py:28
  6.7 1.5 %collective-permute-start.3 = (f32[577,128]{1,0:T(8,128)}, f32[577,128]{1,0:T(8,128)S(1)}, u32[]{:S(2)}, u32[]{:S(2)}) collective-permute-start(f32[577,128]{1,0:T(8,128)} %get-tuple-element.34.refs_4_), channel_id=1, source_target_pairs={{0,2},{1,3},{2,0},{3,1},{4,6},{5,7},{6,4},{7,5},{8,10},{9,11},{10,... | collective-permute-start | bytes 886280 | tf_op jit(solution)/shard_map/ppermute | solution.py:28
  8.2 1.6 %collective-permute-start.2 = (f32[584,128]{1,0:T(8,128)}, f32[584,128]{1,0:T(8,128)S(1)}, u32[]{:S(2)}, u32[]{:S(2)}) collective-permute-start(f32[584,128]{1,0:T(8,128)} %get-tuple-element.32.refs_0_), channel_id=1, source_target_pairs={{0,4},{1,5},{2,6},{3,7},{4,0},{5,1},{6,2},{7,3},{8,12},{9,13},{10,... | collective-permute-start | bytes 897032 | tf_op jit(solution)/shard_map/ppermute | solution.py:28
  9.8 1.5 %collective-permute-start.4 = (f32[577,128]{1,0:T(8,128)}, f32[577,128]{1,0:T(8,128)S(1)}, u32[]{:S(2)}, u32[]{:S(2)}) collective-permute-start(f32[577,128]{1,0:T(8,128)} %get-tuple-element.34.refs_4_), channel_id=1, source_target_pairs={{0,16},{1,17},{2,18},{3,19},{4,20},{5,21},{6,22},{7,23},{8,24},{9,... | collective-permute-start | bytes 886280 | tf_op jit(solution)/shard_map/ppermute | solution.py:28
  12.6 2.8 %collective-permute-done.3.refs_5_ = f32[577,128]{1,0:T(8,128)S(1)} collective-permute-done((f32[577,128]{1,0:T(8,128)}, f32[577,128]{1,0:T(8,128)S(1)}, u32[]{:S(2)}, u32[]{:S(2)}) %collective-permute-start.3) | collective-permute-done | bytes 295456 | tf_op jit(solution)/shard_map/ppermute | solution.py:28
  15.4 1.5 %collective-permute-start.5 = (f32[577,128]{1,0:T(8,128)S(1)}, f32[577,128]{1,0:T(8,128)S(1)}, u32[]{:S(2)}, u32[]{:S(2)}) collective-permute-start(f32[577,128]{1,0:T(8,128)S(1)} %collective-permute-done.3.refs_5_), channel_id=1, source_target_pairs={{0,16},{1,17},{2,18},{3,19},{4,20},{5,21},{6,22},{7,23},{8,24},{9,... | collective-permute-start | bytes 886280 | tf_op jit(solution)/shard_map/ppermute | solution.py:28
  16.9 3.6 %collective-permute-done.block_ref.refs_1_ = f32[584,128]{1,0:T(8,128)S(1)} collective-permute-done((f32[584,128]{1,0:T(8,128)}, f32[584,128]{1,0:T(8,128)S(1)}, u32[]{:S(2)}, u32[]{:S(2)}) %collective-permute-start) | collective-permute-done | bytes 299040 | tf_op jit(solution)/shard_map/ppermute | solution.py:28
  22.0 2.4 %collective-permute-done.5.refs_7_ = f32[577,128]{1,0:T(8,128)S(1)} collective-permute-done((f32[577,128]{1,0:T(8,128)S(1)}, f32[577,128]{1,0:T(8,128)S(1)}, u32[]{:S(2)}, u32[]{:S(2)}) %collective-permute-start.5) | collective-permute-done | bytes 295456 | tf_op jit(solution)/shard_map/ppermute | solution.py:28
  24.4 1.6 %collective-permute-done.9.refs_11_ = f32[577,128]{1,0:T(8,128)S(1)} collective-permute-done((f32[577,128]{1,0:T(8,128)S(1)}, f32[577,128]{1,0:T(8,128)S(1)}, u32[]{:S(2)}, u32[]{:S(2)}) %collective-permute-start.9) | collective-permute-done | bytes 295456 | tf_op jit(solution)/shard_map/ppermute | solution.py:28
  26.0 3.8 %shard_map.95 = (bf16[512,1152]{1,0:T(8,128)(2,1)S(1)}, bf16[512,1152]{1,0:T(8,128)(2,1)S(1)}, f32[8,512]{1,0:T(8,128)S(1)}, f32[64,1152]{1,0:T(8,128)S(1)}, f32...) custom-call(f32[8,128]{1,0:T(8,128)S(1)} %shard_map.92.fixed_ref, ...), custom_call_target="tpu_custom_call" | custom-call | tf_op jit(solution)/shard_map/pallas_call | solution.py:215
  29.8 1.9 %shard_map.96 = (f32[64,1152]{1,0:T(8,128)S(1)}, f32[256,1152]{1,0:T(8,128)S(1)}, f32[256,1152]{1,0:T(8,128)S(1)}, f32[8,128]{1,0:T(8,128)S(1)}) custom-call(f32[8,128]{1,0:T(8,128)S(1)} %shard_map.92.fixed_ref, f32[584,128]{1,0:T(8,128)S(1)} %collective-permute-done.1.refs_0_, bf16[512,1152]{1,0:T(8,128)(2,1)S(1)} %get-tuple-element.37.refs_1_, ...), custom_call_target="tpu_custom_call" | custom-call | tf_op jit(solution)/shard_map/pallas_call | solution.py:215
  32.5 1.5 %collective-permute-start.13 = (f32[64,1152]{1,0:T(8,128)S(1)}, f32[64,1152]{1,0:T(8,128)S(1)}, u32[]{:S(2)}, u32[]{:S(2)}) collective-permute-start(f32[64,1152]{1,0:T(8,128)S(1)} %get-tuple-element.45), channel_id=1, source_target_pairs={{0,4},{1,5},{2,6},{3,7},{4,0},{5,1},{6,2},{7,3},{8,12},{9,13},{10,... | collective-permute-start | bytes 884744 | tf_op jit(solution)/shard_map/ppermute | solution.py:28
  33.9 1.6 %collective-permute-done.10.refs_1_ = f32[8,128]{1,0:T(8,128)S(1)} collective-permute-done((f32[8,128]{1,0:T(8,128)S(1)}, f32[8,128]{1,0:T(8,128)S(1)}, u32[]{:S(2)}, u32[]{:S(2)}) %collective-permute-start.10) | collective-permute-done | bytes 4128 | tf_op jit(solution)/shard_map/ppermute | solution.py:28
  35.8 1.6 %collective-permute-start.17 = (f32[64,1152]{1,0:T(8,128)S(1)}, f32[64,1152]{1,0:T(8,128)S(1)}, u32[]{:S(2)}, u32[]{:S(2)}) collective-permute-start(f32[64,1152]{1,0:T(8,128)S(1)} %get-tuple-element.60), channel_id=1, source_target_pairs={{0,16},{1,17},{2,18},{3,19},{4,20},{5,21},{6,22},{7,23},{8,24},{9,... | collective-permute-start | bytes 884744 | tf_op jit(solution)/shard_map/ppermute | solution.py:28
  37.3 1.2 %collective-permute-done.11 = f32[8,128]{1,0:T(8,128)S(1)} collective-permute-done((f32[8,128]{1,0:T(8,128)S(1)}, f32[8,128]{1,0:T(8,128)S(1)}, u32[]{:S(2)}, u32[]{:S(2)}) %collective-permute-start.11) | collective-permute-done | bytes 4128 | tf_op jit(solution)/shard_map/ppermute | solution.py:28
  38.5 2.1 %collective-permute-start.12 = (f32[8,128]{1,0:T(8,128)S(1)}, f32[8,128]{1,0:T(8,128)S(1)}, u32[]{:S(2)}, u32[]{:S(2)}) collective-permute-start(f32[8,128]{1,0:T(8,128)S(1)} %add.16.refs_0_), channel_id=1, source_target_pairs={{0,8},{1,9},{2,10},{3,11},{4,12},{5,13},{6,14},{7,15},{8,0},{9,1},... | collective-permute-start | bytes 12296 | tf_op jit(solution)/shard_map/ppermute | solution.py:28
  41.6 1.3 %collective-permute-start.20 = (f32[64,1152]{1,0:T(8,128)S(1)}, f32[64,1152]{1,0:T(8,128)S(1)}, u32[]{:S(2)}, u32[]{:S(2)}) collective-permute-start(f32[64,1152]{1,0:T(8,128)S(1)} %get-tuple-element.53), channel_id=1, source_target_pairs={{0,4},{1,5},{2,6},{3,7},{4,0},{5,1},{6,2},{7,3},{8,12},{9,13},{10,... | collective-permute-start | bytes 884744 | tf_op jit(solution)/shard_map/ppermute | solution.py:28
  42.9 2.3 %collective-permute-start.21 = (f32[64,1152]{1,0:T(8,128)S(1)}, f32[64,1152]{1,0:T(8,128)S(1)}, u32[]{:S(2)}, u32[]{:S(2)}) collective-permute-start(f32[64,1152]{1,0:T(8,128)S(1)} %shard_map.99), channel_id=1, source_target_pairs={{0,8},{1,9},{2,10},{3,11},{4,12},{5,13},{6,14},{7,15},{8,0},{9,1},... | collective-permute-start | bytes 884744 | tf_op jit(solution)/shard_map/ppermute | solution.py:28
  45.3 1.5 %collective-permute-start.19 = (f32[64,1152]{1,0:T(8,128)S(1)}, f32[64,1152]{1,0:T(8,128)S(1)}, u32[]{:S(2)}, u32[]{:S(2)}) collective-permute-start(f32[64,1152]{1,0:T(8,128)S(1)} %shard_map.100), channel_id=1, source_target_pairs={{0,2},{1,3},{2,0},{3,1},{4,6},{5,7},{6,4},{7,5},{8,10},{9,11},{10,... | collective-permute-start | bytes 884744 | tf_op jit(solution)/shard_map/ppermute | solution.py:28
  46.9 1.5 %collective-permute-start.18 = (f32[64,1152]{1,0:T(8,128)S(1)}, f32[64,1152]{1,0:T(8,128)S(1)}, u32[]{:S(2)}, u32[]{:S(2)}) collective-permute-start(f32[64,1152]{1,0:T(8,128)S(1)} %get-tuple-element.50), channel_id=1, source_target_pairs={{0,16},{1,17},{2,18},{3,19},{4,20},{5,21},{6,22},{7,23},{8,24},{9,... | collective-permute-start | bytes 884744 | tf_op jit(solution)/shard_map/ppermute | solution.py:28
  49.0 4.3 %collective-permute-done.14 = f32[8,128]{1,0:T(8,128)S(1)} collective-permute-done((f32[8,128]{1,0:T(8,128)S(1)}, f32[8,128]{1,0:T(8,128)S(1)}, u32[]{:S(2)}, u32[]{:S(2)}) %collective-permute-start.14) | collective-permute-done | bytes 4128 | tf_op jit(solution)/shard_map/ppermute | solution.py:28
  53.3 1.5 %collective-permute-start.15 = (f32[8,128]{1,0:T(8,128)S(1)}, f32[8,128]{1,0:T(8,128)S(1)}, u32[]{:S(2)}, u32[]{:S(2)}) collective-permute-start(f32[8,128]{1,0:T(8,128)S(1)} %add.17), channel_id=1, source_target_pairs={{0,16},{1,17},{2,18},{3,19},{4,20},{5,21},{6,22},{7,23},{8,24},{9,... | collective-permute-start | bytes 12296 | tf_op jit(solution)/shard_map/ppermute | solution.py:28
  54.7 2.1 %collective-permute-done.15 = f32[8,128]{1,0:T(8,128)S(1)} collective-permute-done((f32[8,128]{1,0:T(8,128)S(1)}, f32[8,128]{1,0:T(8,128)S(1)}, u32[]{:S(2)}, u32[]{:S(2)}) %collective-permute-start.15) | collective-permute-done | bytes 4128 | tf_op jit(solution)/shard_map/ppermute | solution.py:28
  (43 shorter events, 5.3 us)
Async XLA Ops:
  2.6 17.9 %collective-permute-start = (f32[584,128]{1,0:T(8,128)}, f32[584,128]{1,0:T(8,128)S(1)}, u32[]{:S(2)}, u32[]{:S(2)}) collective-permute-start(f32[584,128]{1,0:T(8,128)} %get-tuple-element.32.refs_0_), channel_id=1, source_target_pairs={{0,8},{1,9},{2,10},{3,11},{4,12},{5,13},{6,14},{7,15},{8,0},{9,1},... | collective-permute-start | bytes 897032 | tf_op jit(solution)/shard_map/ppermute | solution.py:28
  6.7 8.8 %collective-permute-start.3 = (f32[577,128]{1,0:T(8,128)}, f32[577,128]{1,0:T(8,128)S(1)}, u32[]{:S(2)}, u32[]{:S(2)}) collective-permute-start(f32[577,128]{1,0:T(8,128)} %get-tuple-element.34.refs_4_), channel_id=1, source_target_pairs={{0,2},{1,3},{2,0},{3,1},{4,6},{5,7},{6,4},{7,5},{8,10},{9,11},{10,... | collective-permute-start | bytes 886280 | tf_op jit(solution)/shard_map/ppermute | solution.py:28
  8.2 13.8 %collective-permute-start.2 = (f32[584,128]{1,0:T(8,128)}, f32[584,128]{1,0:T(8,128)S(1)}, u32[]{:S(2)}, u32[]{:S(2)}) collective-permute-start(f32[584,128]{1,0:T(8,128)} %get-tuple-element.32.refs_0_), channel_id=1, source_target_pairs={{0,4},{1,5},{2,6},{3,7},{4,0},{5,1},{6,2},{7,3},{8,12},{9,13},{10,... | collective-permute-start | bytes 897032 | tf_op jit(solution)/shard_map/ppermute | solution.py:28
  9.8 11.7 %collective-permute-start.4 = (f32[577,128]{1,0:T(8,128)}, f32[577,128]{1,0:T(8,128)S(1)}, u32[]{:S(2)}, u32[]{:S(2)}) collective-permute-start(f32[577,128]{1,0:T(8,128)} %get-tuple-element.34.refs_4_), channel_id=1, source_target_pairs={{0,16},{1,17},{2,18},{3,19},{4,20},{5,21},{6,22},{7,23},{8,24},{9,... | collective-permute-start | bytes 886280 | tf_op jit(solution)/shard_map/ppermute | solution.py:28
  12.6 13.4 %copy-start.3 = (f32[584,128]{1,0:T(8,128)S(1)}, f32[584,128]{1,0:T(8,128)}, u32[]{:S(2)}) copy-start(f32[584,128]{1,0:T(8,128)} %get-tuple-element.32.refs_0_) | copy-start | bytes 897028
  15.4 8.9 %collective-permute-start.5 = (f32[577,128]{1,0:T(8,128)S(1)}, f32[577,128]{1,0:T(8,128)S(1)}, u32[]{:S(2)}, u32[]{:S(2)}) collective-permute-start(f32[577,128]{1,0:T(8,128)S(1)} %collective-permute-done.3.refs_5_), channel_id=1, source_target_pairs={{0,16},{1,17},{2,18},{3,19},{4,20},{5,21},{6,22},{7,23},{8,24},{9,... | collective-permute-start | bytes 886280 | tf_op jit(solution)/shard_map/ppermute | solution.py:28
  20.6 9.2 %collective-permute-start.1 = (f32[584,128]{1,0:T(8,128)S(1)}, f32[584,128]{1,0:T(8,128)S(1)}, u32[]{:S(2)}, u32[]{:S(2)}) collective-permute-start(f32[584,128]{1,0:T(8,128)S(1)} %collective-permute-done.block_ref.refs_1_), channel_id=1, source_target_pairs={{0,4},{1,5},{2,6},{3,7},{4,0},{5,1},{6,2},{7,3},{8,12},{9,13},{10,... | collective-permute-start | bytes 897032 | tf_op jit(solution)/shard_map/ppermute | solution.py:28
  21.4 3.0 %collective-permute-start.6 = (f32[577,128]{1,0:T(8,128)S(1)}, f32[577,128]{1,0:T(8,128)S(1)}, u32[]{:S(2)}, u32[]{:S(2)}) collective-permute-start(f32[577,128]{1,0:T(8,128)S(1)} %copy-done.2), channel_id=1, source_target_pairs={{0,1},{1,0},{2,3},{3,2},{4,5},{5,4},{6,7},{7,6},{8,9},{9,8},{10,11... | collective-permute-start | bytes 886280 | tf_op jit(solution)/shard_map/ppermute | solution.py:28
  21.4 2.9 %collective-permute-start.7 = (f32[577,128]{1,0:T(8,128)S(1)}, f32[577,128]{1,0:T(8,128)S(1)}, u32[]{:S(2)}, u32[]{:S(2)}) collective-permute-start(f32[577,128]{1,0:T(8,128)S(1)} %collective-permute-done.3.refs_5_), channel_id=1, source_target_pairs={{0,1},{1,0},{2,3},{3,2},{4,5},{5,4},{6,7},{7,6},{8,9},{9,8},{10,11... | collective-permute-start | bytes 886280 | tf_op jit(solution)/shard_map/ppermute | solution.py:28
  22.0 2.4 %collective-permute-start.8 = (f32[577,128]{1,0:T(8,128)S(1)}, f32[577,128]{1,0:T(8,128)S(1)}, u32[]{:S(2)}, u32[]{:S(2)}) collective-permute-start(f32[577,128]{1,0:T(8,128)S(1)} %collective-permute-done.4.refs_6_), channel_id=1, source_target_pairs={{0,1},{1,0},{2,3},{3,2},{4,5},{5,4},{6,7},{7,6},{8,9},{9,8},{10,11... | collective-permute-start | bytes 886280 | tf_op jit(solution)/shard_map/ppermute | solution.py:28
  24.4 1.6 %collective-permute-start.9 = (f32[577,128]{1,0:T(8,128)S(1)}, f32[577,128]{1,0:T(8,128)S(1)}, u32[]{:S(2)}, u32[]{:S(2)}) collective-permute-start(f32[577,128]{1,0:T(8,128)S(1)} %collective-permute-done.5.refs_7_), channel_id=1, source_target_pairs={{0,1},{1,0},{2,3},{3,2},{4,5},{5,4},{6,7},{7,6},{8,9},{9,8},{10,11... | collective-permute-start | bytes 886280 | tf_op jit(solution)/shard_map/ppermute | solution.py:28
  31.7 3.9 %collective-permute-start.16 = (f32[256,1152]{1,0:T(8,128)S(1)}, f32[256,1152]{1,0:T(8,128)S(1)}, u32[]{:S(2)}, u32[]{:S(2)}) collective-permute-start(f32[256,1152]{1,0:T(8,128)S(1)} %get-tuple-element.48), channel_id=1, source_target_pairs={{0,1},{1,0},{2,3},{3,2},{4,5},{5,4},{6,7},{7,6},{8,9},{9,8},{10,11... | collective-permute-start | bytes 3538952 | tf_op jit(solution)/shard_map/ppermute | solution.py:28
  31.9 3.7 %collective-permute-start.10 = (f32[8,128]{1,0:T(8,128)S(1)}, f32[8,128]{1,0:T(8,128)S(1)}, u32[]{:S(2)}, u32[]{:S(2)}) collective-permute-start(f32[8,128]{1,0:T(8,128)S(1)} %get-tuple-element.43.refs_0_), channel_id=1, source_target_pairs={{0,4},{1,5},{2,6},{3,7},{4,0},{5,1},{6,2},{7,3},{8,12},{9,13},{10,... | collective-permute-start | bytes 12296 | tf_op jit(solution)/shard_map/ppermute | solution.py:28
  32.5 9.1 %collective-permute-start.13 = (f32[64,1152]{1,0:T(8,128)S(1)}, f32[64,1152]{1,0:T(8,128)S(1)}, u32[]{:S(2)}, u32[]{:S(2)}) collective-permute-start(f32[64,1152]{1,0:T(8,128)S(1)} %get-tuple-element.45), channel_id=1, source_target_pairs={{0,4},{1,5},{2,6},{3,7},{4,0},{5,1},{6,2},{7,3},{8,12},{9,13},{10,... | collective-permute-start | bytes 884744 | tf_op jit(solution)/shard_map/ppermute | solution.py:28
  35.8 9.5 %collective-permute-start.17 = (f32[64,1152]{1,0:T(8,128)S(1)}, f32[64,1152]{1,0:T(8,128)S(1)}, u32[]{:S(2)}, u32[]{:S(2)}) collective-permute-start(f32[64,1152]{1,0:T(8,128)S(1)} %get-tuple-element.60), channel_id=1, source_target_pairs={{0,16},{1,17},{2,18},{3,19},{4,20},{5,21},{6,22},{7,23},{8,24},{9,... | collective-permute-start | bytes 884744 | tf_op jit(solution)/shard_map/ppermute | solution.py:28
  37.3 1.2 %collective-permute-start.11 = (f32[8,128]{1,0:T(8,128)S(1)}, f32[8,128]{1,0:T(8,128)S(1)}, u32[]{:S(2)}, u32[]{:S(2)}) collective-permute-start(f32[8,128]{1,0:T(8,128)S(1)} %shard_map.97), channel_id=1, source_target_pairs={{0,1},{1,0},{2,3},{3,2},{4,5},{5,4},{6,7},{7,6},{8,9},{9,8},{10,11... | collective-permute-start | bytes 12296 | tf_op jit(solution)/shard_map/ppermute | solution.py:28
  38.5 9.9 %collective-permute-start.12 = (f32[8,128]{1,0:T(8,128)S(1)}, f32[8,128]{1,0:T(8,128)S(1)}, u32[]{:S(2)}, u32[]{:S(2)}) collective-permute-start(f32[8,128]{1,0:T(8,128)S(1)} %add.16.refs_0_), channel_id=1, source_target_pairs={{0,8},{1,9},{2,10},{3,11},{4,12},{5,13},{6,14},{7,15},{8,0},{9,1},... | collective-permute-start | bytes 12296 | tf_op jit(solution)/shard_map/ppermute | solution.py:28
  41.6 15.3 %collective-permute-start.20 = (f32[64,1152]{1,0:T(8,128)S(1)}, f32[64,1152]{1,0:T(8,128)S(1)}, u32[]{:S(2)}, u32[]{:S(2)}) collective-permute-start(f32[64,1152]{1,0:T(8,128)S(1)} %get-tuple-element.53), channel_id=1, source_target_pairs={{0,4},{1,5},{2,6},{3,7},{4,0},{5,1},{6,2},{7,3},{8,12},{9,13},{10,... | collective-permute-start | bytes 884744 | tf_op jit(solution)/shard_map/ppermute | solution.py:28
  42.9 13.9 %collective-permute-start.21 = (f32[64,1152]{1,0:T(8,128)S(1)}, f32[64,1152]{1,0:T(8,128)S(1)}, u32[]{:S(2)}, u32[]{:S(2)}) collective-permute-start(f32[64,1152]{1,0:T(8,128)S(1)} %shard_map.99), channel_id=1, source_target_pairs={{0,8},{1,9},{2,10},{3,11},{4,12},{5,13},{6,14},{7,15},{8,0},{9,1},... | collective-permute-start | bytes 884744 | tf_op jit(solution)/shard_map/ppermute | solution.py:28
  45.3 11.5 %collective-permute-start.19 = (f32[64,1152]{1,0:T(8,128)S(1)}, f32[64,1152]{1,0:T(8,128)S(1)}, u32[]{:S(2)}, u32[]{:S(2)}) collective-permute-start(f32[64,1152]{1,0:T(8,128)S(1)} %shard_map.100), channel_id=1, source_target_pairs={{0,2},{1,3},{2,0},{3,1},{4,6},{5,7},{6,4},{7,5},{8,10},{9,11},{10,... | collective-permute-start | bytes 884744 | tf_op jit(solution)/shard_map/ppermute | solution.py:28
  46.9 10.0 %copy-start.1 = (f32[64,1152]{1,0:T(8,128)S(1)}, f32[64,1152]{1,0:T(8,128)}, u32[]{:S(2)}) copy-start(f32[64,1152]{1,0:T(8,128)} %refs_4_.1) | copy-start | bytes 884740
  46.9 10.0 %collective-permute-start.18 = (f32[64,1152]{1,0:T(8,128)S(1)}, f32[64,1152]{1,0:T(8,128)S(1)}, u32[]{:S(2)}, u32[]{:S(2)}) collective-permute-start(f32[64,1152]{1,0:T(8,128)S(1)} %get-tuple-element.50), channel_id=1, source_target_pairs={{0,16},{1,17},{2,18},{3,19},{4,20},{5,21},{6,22},{7,23},{8,24},{9,... | collective-permute-start | bytes 884744 | tf_op jit(solution)/shard_map/ppermute | solution.py:28
  48.4 4.8 %collective-permute-start.14 = (f32[8,128]{1,0:T(8,128)S(1)}, f32[8,128]{1,0:T(8,128)S(1)}, u32[]{:S(2)}, u32[]{:S(2)}) collective-permute-start(f32[8,128]{1,0:T(8,128)S(1)} %shard_map.98), channel_id=1, source_target_pairs={{0,2},{1,3},{2,0},{3,1},{4,6},{5,7},{6,4},{7,5},{8,10},{9,11},{10,... | collective-permute-start | bytes 12296 | tf_op jit(solution)/shard_map/ppermute | solution.py:28
  53.3 3.6 %collective-permute-start.15 = (f32[8,128]{1,0:T(8,128)S(1)}, f32[8,128]{1,0:T(8,128)S(1)}, u32[]{:S(2)}, u32[]{:S(2)}) collective-permute-start(f32[8,128]{1,0:T(8,128)S(1)} %add.17), channel_id=1, source_target_pairs={{0,16},{1,17},{2,18},{3,19},{4,20},{5,21},{6,22},{7,23},{8,24},{9,... | collective-permute-start | bytes 12296 | tf_op jit(solution)/shard_map/ppermute | solution.py:28
  (2 other events, 18.9 us)

commit v6 on v5

--- a/solution.py
+++ b/solution.py
@@ -34,7 +34,8 @@
 
 def unit_rows(rows):
     norm = jnp.sqrt(jnp.sum(rows * rows, axis=1, keepdims=True) + EPSILON)
-    return rows / norm, norm
+    inverse = 1.0 / norm
+    return rows * inverse, inverse
 
 
 def halves(value):
@@ -114,9 +115,9 @@
         for piece in range(width // LANES):
             part = block[pl.ds(piece * rows, rows), :]
             squares += part * part
-        norm = jnp.sqrt(jnp.sum(squares, axis=1, keepdims=True) + EPSILON)
+        inverse = 1.0 / jnp.sqrt(jnp.sum(squares, axis=1, keepdims=True) + EPSILON)
         for piece in range(width // LANES):
-            high, low = halves(block[pl.ds(piece * rows, rows), :] / norm)
+            high, low = halves(block[pl.ds(piece * rows, rows), :] * inverse)
             high_ref[pl.ds(at * rows, rows), pl.ds(piece * LANES, LANES)] = high
             low_ref[pl.ds(at * rows, rows), pl.ds(piece * LANES, LANES)] = low
     lane = lax.broadcasted_iota(jnp.int32, (1, LANES), 1)
@@ -129,7 +130,7 @@
 def norm_kernel(block_ref, norm_ref):
     block = unpack(block_ref, norm_ref.shape[0])
     norm = jnp.sqrt(jnp.sum(block * block, axis=1, keepdims=True) + EPSILON)
-    norm_ref[...] = jnp.broadcast_to(norm, norm_ref.shape)
+    norm_ref[...] = jnp.broadcast_to(1.0 / norm, norm_ref.shape)
 
 
 def row_norms(block, rows):
@@ -164,7 +165,7 @@
     units = []
     for at in range(count):
         if at in norms:
-            units.append(halves(unpack(texts[at], rows) / norms[at][:, 0:1]))
+            units.append(halves(unpack(texts[at], rows) * norms[at][:, 0:1]))
         else:
             units.append(halves(unit_rows(unpack(texts[at], rows))[0]))
     high = jnp.concatenate([unit[0] for unit in units], axis=0)
@@ -261,8 +262,8 @@
     ):
         total = functools.reduce(jnp.add, [part[...] for part in parts])
         grad = scale * total
-        unit, norm = unit_rows(own_ref[...])
-        out_ref[...] = (grad - unit * jnp.sum(unit * grad, axis=1, keepdims=True)) / norm
+        unit, inverse = unit_rows(own_ref[...])
+        out_ref[...] = (grad - unit * jnp.sum(unit * grad, axis=1, keepdims=True)) * inverse
 
 
 def final(pairs, fixed, scalars, image, image_parts, text, text_parts):

time: 58.2 us -> 58.2 us (level)
  no operation moved by 1% of the time
where the time goes in v6:
time: 58.2 us; the launch traced here: 58 us
  starting transfers between devices  26.2 us (45%)
  waiting for transfers between devices  20.6 us (35%)
  Pallas kernels  8.91 us (15%)
  between operations  2.07 us (4%)
    ppermute x22, starting transfers between devices, exchange(): return lax.ppermute(value, AXES, [(i, i ^ step) for i in range(count)])  26.2 us
    ppermute x22, waiting for transfers between devices, exchange(): return lax.ppermute(value, AXES, [(i, i ^ step) for i in range(count)])  20.6 us
    pallas_call x2, Pallas kernels, tile(): pl.pallas_call(functools.partial(tile_kernel, places, normed, len(blocks)...  5.67 us
    pallas_call x1, Pallas kernels, pack(): pl.pallas_call(pack_kernel, out_shape=[jax.ShapeDtypeStruct((pieces + mor...  1.93 us
  transfers between devices with their start and end apart: 22, of which 9 were waited for; matrix products, arithmetic and copies ran while one was open for 0% of the time, Pallas kernels for 7%

profile of v6, /device:TPU:0, one launch (start us, length us, event | category | flops | bytes accessed | tf_op | source)
XLA Modules:
  0.0 58.0 jit_solution(3169692976445785921)
XLA Ops:
  0.6 1.9 %shard_map.93 = (f32[577,128]{1,0:T(8,128)}, f32[584,128]{1,0:T(8,128)}) custom-call(f32[64,1152]{1,0:T(8,128)} %refs_0_.1, f32[64,1152]{1,0:T(8,128)} %refs_4_.1, s32[1,64]{1,0:T(1,128)} %bitcast.2), custom_call_target="tpu_custom_call" | custom-call | tf_op jit(solution)/shard_map/pallas_call | solution.py:90
  2.6 4.1 %collective-permute-start = (f32[584,128]{1,0:T(8,128)}, f32[584,128]{1,0:T(8,128)S(1)}, u32[]{:S(2)}, u32[]{:S(2)}) collective-permute-start(f32[584,128]{1,0:T(8,128)} %get-tuple-element.32.refs_0_), channel_id=1, source_target_pairs={{0,8},{1,9},{2,10},{3,11},{4,12},{5,13},{6,14},{7,15},{8,0},{9,1},... | collective-permute-start | bytes 897032 | tf_op jit(solution)/shard_map/ppermute | solution.py:28
  6.7 1.5 %collective-permute-start.3 = (f32[577,128]{1,0:T(8,128)}, f32[577,128]{1,0:T(8,128)S(1)}, u32[]{:S(2)}, u32[]{:S(2)}) collective-permute-start(f32[577,128]{1,0:T(8,128)} %get-tuple-element.34.refs_4_), channel_id=1, source_target_pairs={{0,2},{1,3},{2,0},{3,1},{4,6},{5,7},{6,4},{7,5},{8,10},{9,11},{10,... | collective-permute-start | bytes 886280 | tf_op jit(solution)/shard_map/ppermute | solution.py:28
  8.2 1.6 %collective-permute-start.2 = (f32[584,128]{1,0:T(8,128)}, f32[584,128]{1,0:T(8,128)S(1)}, u32[]{:S(2)}, u32[]{:S(2)}) collective-permute-start(f32[584,128]{1,0:T(8,128)} %get-tuple-element.32.refs_0_), channel_id=1, source_target_pairs={{0,4},{1,5},{2,6},{3,7},{4,0},{5,1},{6,2},{7,3},{8,12},{9,13},{10,... | collective-permute-start | bytes 897032 | tf_op jit(solution)/shard_map/ppermute | solution.py:28
  9.8 1.5 %collective-permute-start.4 = (f32[577,128]{1,0:T(8,128)}, f32[577,128]{1,0:T(8,128)S(1)}, u32[]{:S(2)}, u32[]{:S(2)}) collective-permute-start(f32[577,128]{1,0:T(8,128)} %get-tuple-element.34.refs_4_), channel_id=1, source_target_pairs={{0,16},{1,17},{2,18},{3,19},{4,20},{5,21},{6,22},{7,23},{8,24},{9,... | collective-permute-start | bytes 886280 | tf_op jit(solution)/shard_map/ppermute | solution.py:28
  12.6 2.8 %collective-permute-done.3.refs_5_ = f32[577,128]{1,0:T(8,128)S(1)} collective-permute-done((f32[577,128]{1,0:T(8,128)}, f32[577,128]{1,0:T(8,128)S(1)}, u32[]{:S(2)}, u32[]{:S(2)}) %collective-permute-start.3) | collective-permute-done | bytes 295456 | tf_op jit(solution)/shard_map/ppermute | solution.py:28
  15.4 1.5 %collective-permute-start.5 = (f32[577,128]{1,0:T(8,128)S(1)}, f32[577,128]{1,0:T(8,128)S(1)}, u32[]{:S(2)}, u32[]{:S(2)}) collective-permute-start(f32[577,128]{1,0:T(8,128)S(1)} %collective-permute-done.3.refs_5_), channel_id=1, source_target_pairs={{0,16},{1,17},{2,18},{3,19},{4,20},{5,21},{6,22},{7,23},{8,24},{9,... | collective-permute-start | bytes 886280 | tf_op jit(solution)/shard_map/ppermute | solution.py:28
  16.9 3.6 %collective-permute-done.block_ref.refs_1_ = f32[584,128]{1,0:T(8,128)S(1)} collective-permute-done((f32[584,128]{1,0:T(8,128)}, f32[584,128]{1,0:T(8,128)S(1)}, u32[]{:S(2)}, u32[]{:S(2)}) %collective-permute-start) | collective-permute-done | bytes 299040 | tf_op jit(solution)/shard_map/ppermute | solution.py:28
  22.0 2.4 %collective-permute-done.5.refs_7_ = f32[577,128]{1,0:T(8,128)S(1)} collective-permute-done((f32[577,128]{1,0:T(8,128)S(1)}, f32[577,128]{1,0:T(8,128)S(1)}, u32[]{:S(2)}, u32[]{:S(2)}) %collective-permute-start.5) | collective-permute-done | bytes 295456 | tf_op jit(solution)/shard_map/ppermute | solution.py:28
  24.4 1.6 %collective-permute-done.9.refs_11_ = f32[577,128]{1,0:T(8,128)S(1)} collective-permute-done((f32[577,128]{1,0:T(8,128)S(1)}, f32[577,128]{1,0:T(8,128)S(1)}, u32[]{:S(2)}, u32[]{:S(2)}) %collective-permute-start.9) | collective-permute-done | bytes 295456 | tf_op jit(solution)/shard_map/ppermute | solution.py:28
  26.0 3.8 %shard_map.95 = (bf16[512,1152]{1,0:T(8,128)(2,1)S(1)}, bf16[512,1152]{1,0:T(8,128)(2,1)S(1)}, f32[8,512]{1,0:T(8,128)S(1)}, f32[64,1152]{1,0:T(8,128)S(1)}, f32...) custom-call(f32[8,128]{1,0:T(8,128)S(1)} %shard_map.92.fixed_ref, ...), custom_call_target="tpu_custom_call" | custom-call | tf_op jit(solution)/shard_map/pallas_call | solution.py:216
  29.8 1.9 %shard_map.96 = (f32[64,1152]{1,0:T(8,128)S(1)}, f32[256,1152]{1,0:T(8,128)S(1)}, f32[256,1152]{1,0:T(8,128)S(1)}, f32[8,128]{1,0:T(8,128)S(1)}) custom-call(f32[8,128]{1,0:T(8,128)S(1)} %shard_map.92.fixed_ref, f32[584,128]{1,0:T(8,128)S(1)} %collective-permute-done.1.refs_0_, bf16[512,1152]{1,0:T(8,128)(2,1)S(1)} %get-tuple-element.37.refs_1_, ...), custom_call_target="tpu_custom_call" | custom-call | tf_op jit(solution)/shard_map/pallas_call | solution.py:216
  32.5 1.4 %collective-permute-start.13 = (f32[64,1152]{1,0:T(8,128)S(1)}, f32[64,1152]{1,0:T(8,128)S(1)}, u32[]{:S(2)}, u32[]{:S(2)}) collective-permute-start(f32[64,1152]{1,0:T(8,128)S(1)} %get-tuple-element.45), channel_id=1, source_target_pairs={{0,4},{1,5},{2,6},{3,7},{4,0},{5,1},{6,2},{7,3},{8,12},{9,13},{10,... | collective-permute-start | bytes 884744 | tf_op jit(solution)/shard_map/ppermute | solution.py:28
  33.9 1.6 %collective-permute-done.10.refs_1_ = f32[8,128]{1,0:T(8,128)S(1)} collective-permute-done((f32[8,128]{1,0:T(8,128)S(1)}, f32[8,128]{1,0:T(8,128)S(1)}, u32[]{:S(2)}, u32[]{:S(2)}) %collective-permute-start.10) | collective-permute-done | bytes 4128 | tf_op jit(solution)/shard_map/ppermute | solution.py:28
  35.7 1.6 %collective-permute-start.17 = (f32[64,1152]{1,0:T(8,128)S(1)}, f32[64,1152]{1,0:T(8,128)S(1)}, u32[]{:S(2)}, u32[]{:S(2)}) collective-permute-start(f32[64,1152]{1,0:T(8,128)S(1)} %get-tuple-element.60), channel_id=1, source_target_pairs={{0,16},{1,17},{2,18},{3,19},{4,20},{5,21},{6,22},{7,23},{8,24},{9,... | collective-permute-start | bytes 884744 | tf_op jit(solution)/shard_map/ppermute | solution.py:28
  37.3 1.2 %collective-permute-done.11 = f32[8,128]{1,0:T(8,128)S(1)} collective-permute-done((f32[8,128]{1,0:T(8,128)S(1)}, f32[8,128]{1,0:T(8,128)S(1)}, u32[]{:S(2)}, u32[]{:S(2)}) %collective-permute-start.11) | collective-permute-done | bytes 4128 | tf_op jit(solution)/shard_map/ppermute | solution.py:28
  38.5 2.1 %collective-permute-start.12 = (f32[8,128]{1,0:T(8,128)S(1)}, f32[8,128]{1,0:T(8,128)S(1)}, u32[]{:S(2)}, u32[]{:S(2)}) collective-permute-start(f32[8,128]{1,0:T(8,128)S(1)} %add.16.refs_0_), channel_id=1, source_target_pairs={{0,8},{1,9},{2,10},{3,11},{4,12},{5,13},{6,14},{7,15},{8,0},{9,1},... | collective-permute-start | bytes 12296 | tf_op jit(solution)/shard_map/ppermute | solution.py:28
  41.6 1.3 %collective-permute-start.20 = (f32[64,1152]{1,0:T(8,128)S(1)}, f32[64,1152]{1,0:T(8,128)S(1)}, u32[]{:S(2)}, u32[]{:S(2)}) collective-permute-start(f32[64,1152]{1,0:T(8,128)S(1)} %get-tuple-element.53), channel_id=1, source_target_pairs={{0,4},{1,5},{2,6},{3,7},{4,0},{5,1},{6,2},{7,3},{8,12},{9,13},{10,... | collective-permute-start | bytes 884744 | tf_op jit(solution)/shard_map/ppermute | solution.py:28
  42.9 2.4 %collective-permute-start.21 = (f32[64,1152]{1,0:T(8,128)S(1)}, f32[64,1152]{1,0:T(8,128)S(1)}, u32[]{:S(2)}, u32[]{:S(2)}) collective-permute-start(f32[64,1152]{1,0:T(8,128)S(1)} %shard_map.99), channel_id=1, source_target_pairs={{0,8},{1,9},{2,10},{3,11},{4,12},{5,13},{6,14},{7,15},{8,0},{9,1},... | collective-permute-start | bytes 884744 | tf_op jit(solution)/shard_map/ppermute | solution.py:28
  45.3 1.6 %collective-permute-start.19 = (f32[64,1152]{1,0:T(8,128)S(1)}, f32[64,1152]{1,0:T(8,128)S(1)}, u32[]{:S(2)}, u32[]{:S(2)}) collective-permute-start(f32[64,1152]{1,0:T(8,128)S(1)} %shard_map.100), channel_id=1, source_target_pairs={{0,2},{1,3},{2,0},{3,1},{4,6},{5,7},{6,4},{7,5},{8,10},{9,11},{10,... | collective-permute-start | bytes 884744 | tf_op jit(solution)/shard_map/ppermute | solution.py:28
  46.9 1.5 %collective-permute-start.18 = (f32[64,1152]{1,0:T(8,128)S(1)}, f32[64,1152]{1,0:T(8,128)S(1)}, u32[]{:S(2)}, u32[]{:S(2)}) collective-permute-start(f32[64,1152]{1,0:T(8,128)S(1)} %get-tuple-element.50), channel_id=1, source_target_pairs={{0,16},{1,17},{2,18},{3,19},{4,20},{5,21},{6,22},{7,23},{8,24},{9,... | collective-permute-start | bytes 884744 | tf_op jit(solution)/shard_map/ppermute | solution.py:28
  49.0 4.3 %collective-permute-done.14 = f32[8,128]{1,0:T(8,128)S(1)} collective-permute-done((f32[8,128]{1,0:T(8,128)S(1)}, f32[8,128]{1,0:T(8,128)S(1)}, u32[]{:S(2)}, u32[]{:S(2)}) %collective-permute-start.14) | collective-permute-done | bytes 4128 | tf_op jit(solution)/shard_map/ppermute | solution.py:28
  53.3 1.5 %collective-permute-start.15 = (f32[8,128]{1,0:T(8,128)S(1)}, f32[8,128]{1,0:T(8,128)S(1)}, u32[]{:S(2)}, u32[]{:S(2)}) collective-permute-start(f32[8,128]{1,0:T(8,128)S(1)} %add.17), channel_id=1, source_target_pairs={{0,16},{1,17},{2,18},{3,19},{4,20},{5,21},{6,22},{7,23},{8,24},{9,... | collective-permute-start | bytes 12296 | tf_op jit(solution)/shard_map/ppermute | solution.py:28
  54.8 2.1 %collective-permute-done.15 = f32[8,128]{1,0:T(8,128)S(1)} collective-permute-done((f32[8,128]{1,0:T(8,128)S(1)}, f32[8,128]{1,0:T(8,128)S(1)}, u32[]{:S(2)}, u32[]{:S(2)}) %collective-permute-start.15) | collective-permute-done | bytes 4128 | tf_op jit(solution)/shard_map/ppermute | solution.py:28
  (43 shorter events, 5.4 us)
Async XLA Ops:
  2.6 17.9 %collective-permute-start = (f32[584,128]{1,0:T(8,128)}, f32[584,128]{1,0:T(8,128)S(1)}, u32[]{:S(2)}, u32[]{:S(2)}) collective-permute-start(f32[584,128]{1,0:T(8,128)} %get-tuple-element.32.refs_0_), channel_id=1, source_target_pairs={{0,8},{1,9},{2,10},{3,11},{4,12},{5,13},{6,14},{7,15},{8,0},{9,1},... | collective-permute-start | bytes 897032 | tf_op jit(solution)/shard_map/ppermute | solution.py:28
  6.7 8.8 %collective-permute-start.3 = (f32[577,128]{1,0:T(8,128)}, f32[577,128]{1,0:T(8,128)S(1)}, u32[]{:S(2)}, u32[]{:S(2)}) collective-permute-start(f32[577,128]{1,0:T(8,128)} %get-tuple-element.34.refs_4_), channel_id=1, source_target_pairs={{0,2},{1,3},{2,0},{3,1},{4,6},{5,7},{6,4},{7,5},{8,10},{9,11},{10,... | collective-permute-start | bytes 886280 | tf_op jit(solution)/shard_map/ppermute | solution.py:28
  8.2 13.8 %collective-permute-start.2 = (f32[584,128]{1,0:T(8,128)}, f32[584,128]{1,0:T(8,128)S(1)}, u32[]{:S(2)}, u32[]{:S(2)}) collective-permute-start(f32[584,128]{1,0:T(8,128)} %get-tuple-element.32.refs_0_), channel_id=1, source_target_pairs={{0,4},{1,5},{2,6},{3,7},{4,0},{5,1},{6,2},{7,3},{8,12},{9,13},{10,... | collective-permute-start | bytes 897032 | tf_op jit(solution)/shard_map/ppermute | solution.py:28
  9.8 11.7 %collective-permute-start.4 = (f32[577,128]{1,0:T(8,128)}, f32[577,128]{1,0:T(8,128)S(1)}, u32[]{:S(2)}, u32[]{:S(2)}) collective-permute-start(f32[577,128]{1,0:T(8,128)} %get-tuple-element.34.refs_4_), channel_id=1, source_target_pairs={{0,16},{1,17},{2,18},{3,19},{4,20},{5,21},{6,22},{7,23},{8,24},{9,... | collective-permute-start | bytes 886280 | tf_op jit(solution)/shard_map/ppermute | solution.py:28
  12.6 13.4 %copy-start.3 = (f32[584,128]{1,0:T(8,128)S(1)}, f32[584,128]{1,0:T(8,128)}, u32[]{:S(2)}) copy-start(f32[584,128]{1,0:T(8,128)} %get-tuple-element.32.refs_0_) | copy-start | bytes 897028
  15.4 8.9 %collective-permute-start.5 = (f32[577,128]{1,0:T(8,128)S(1)}, f32[577,128]{1,0:T(8,128)S(1)}, u32[]{:S(2)}, u32[]{:S(2)}) collective-permute-start(f32[577,128]{1,0:T(8,128)S(1)} %collective-permute-done.3.refs_5_), channel_id=1, source_target_pairs={{0,16},{1,17},{2,18},{3,19},{4,20},{5,21},{6,22},{7,23},{8,24},{9,... | collective-permute-start | bytes 886280 | tf_op jit(solution)/shard_map/ppermute | solution.py:28
  20.6 9.2 %collective-permute-start.1 = (f32[584,128]{1,0:T(8,128)S(1)}, f32[584,128]{1,0:T(8,128)S(1)}, u32[]{:S(2)}, u32[]{:S(2)}) collective-permute-start(f32[584,128]{1,0:T(8,128)S(1)} %collective-permute-done.block_ref.refs_1_), channel_id=1, source_target_pairs={{0,4},{1,5},{2,6},{3,7},{4,0},{5,1},{6,2},{7,3},{8,12},{9,13},{10,... | collective-permute-start | bytes 897032 | tf_op jit(solution)/shard_map/ppermute | solution.py:28
  21.4 2.9 %collective-permute-start.6 = (f32[577,128]{1,0:T(8,128)S(1)}, f32[577,128]{1,0:T(8,128)S(1)}, u32[]{:S(2)}, u32[]{:S(2)}) collective-permute-start(f32[577,128]{1,0:T(8,128)S(1)} %copy-done.2), channel_id=1, source_target_pairs={{0,1},{1,0},{2,3},{3,2},{4,5},{5,4},{6,7},{7,6},{8,9},{9,8},{10,11... | collective-permute-start | bytes 886280 | tf_op jit(solution)/shard_map/ppermute | solution.py:28
  21.4 2.9 %collective-permute-start.7 = (f32[577,128]{1,0:T(8,128)S(1)}, f32[577,128]{1,0:T(8,128)S(1)}, u32[]{:S(2)}, u32[]{:S(2)}) collective-permute-start(f32[577,128]{1,0:T(8,128)S(1)} %collective-permute-done.3.refs_5_), channel_id=1, source_target_pairs={{0,1},{1,0},{2,3},{3,2},{4,5},{5,4},{6,7},{7,6},{8,9},{9,8},{10,11... | collective-permute-start | bytes 886280 | tf_op jit(solution)/shard_map/ppermute | solution.py:28
  22.0 2.4 %collective-permute-start.8 = (f32[577,128]{1,0:T(8,128)S(1)}, f32[577,128]{1,0:T(8,128)S(1)}, u32[]{:S(2)}, u32[]{:S(2)}) collective-permute-start(f32[577,128]{1,0:T(8,128)S(1)} %collective-permute-done.4.refs_6_), channel_id=1, source_target_pairs={{0,1},{1,0},{2,3},{3,2},{4,5},{5,4},{6,7},{7,6},{8,9},{9,8},{10,11... | collective-permute-start | bytes 886280 | tf_op jit(solution)/shard_map/ppermute | solution.py:28
  24.4 1.6 %collective-permute-start.9 = (f32[577,128]{1,0:T(8,128)S(1)}, f32[577,128]{1,0:T(8,128)S(1)}, u32[]{:S(2)}, u32[]{:S(2)}) collective-permute-start(f32[577,128]{1,0:T(8,128)S(1)} %collective-permute-done.5.refs_7_), channel_id=1, source_target_pairs={{0,1},{1,0},{2,3},{3,2},{4,5},{5,4},{6,7},{7,6},{8,9},{9,8},{10,11... | collective-permute-start | bytes 886280 | tf_op jit(solution)/shard_map/ppermute | solution.py:28
  31.7 3.9 %collective-permute-start.16 = (f32[256,1152]{1,0:T(8,128)S(1)}, f32[256,1152]{1,0:T(8,128)S(1)}, u32[]{:S(2)}, u32[]{:S(2)}) collective-permute-start(f32[256,1152]{1,0:T(8,128)S(1)} %get-tuple-element.48), channel_id=1, source_target_pairs={{0,1},{1,0},{2,3},{3,2},{4,5},{5,4},{6,7},{7,6},{8,9},{9,8},{10,11... | collective-permute-start | bytes 3538952 | tf_op jit(solution)/shard_map/ppermute | solution.py:28
  31.9 3.7 %collective-permute-start.10 = (f32[8,128]{1,0:T(8,128)S(1)}, f32[8,128]{1,0:T(8,128)S(1)}, u32[]{:S(2)}, u32[]{:S(2)}) collective-permute-start(f32[8,128]{1,0:T(8,128)S(1)} %get-tuple-element.43.refs_0_), channel_id=1, source_target_pairs={{0,4},{1,5},{2,6},{3,7},{4,0},{5,1},{6,2},{7,3},{8,12},{9,13},{10,... | collective-permute-start | bytes 12296 | tf_op jit(solution)/shard_map/ppermute | solution.py:28
  32.5 9.1 %collective-permute-start.13 = (f32[64,1152]{1,0:T(8,128)S(1)}, f32[64,1152]{1,0:T(8,128)S(1)}, u32[]{:S(2)}, u32[]{:S(2)}) collective-permute-start(f32[64,1152]{1,0:T(8,128)S(1)} %get-tuple-element.45), channel_id=1, source_target_pairs={{0,4},{1,5},{2,6},{3,7},{4,0},{5,1},{6,2},{7,3},{8,12},{9,13},{10,... | collective-permute-start | bytes 884744 | tf_op jit(solution)/shard_map/ppermute | solution.py:28
  35.7 9.5 %collective-permute-start.17 = (f32[64,1152]{1,0:T(8,128)S(1)}, f32[64,1152]{1,0:T(8,128)S(1)}, u32[]{:S(2)}, u32[]{:S(2)}) collective-permute-start(f32[64,1152]{1,0:T(8,128)S(1)} %get-tuple-element.60), channel_id=1, source_target_pairs={{0,16},{1,17},{2,18},{3,19},{4,20},{5,21},{6,22},{7,23},{8,24},{9,... | collective-permute-start | bytes 884744 | tf_op jit(solution)/shard_map/ppermute | solution.py:28
  37.3 1.2 %collective-permute-start.11 = (f32[8,128]{1,0:T(8,128)S(1)}, f32[8,128]{1,0:T(8,128)S(1)}, u32[]{:S(2)}, u32[]{:S(2)}) collective-permute-start(f32[8,128]{1,0:T(8,128)S(1)} %shard_map.97), channel_id=1, source_target_pairs={{0,1},{1,0},{2,3},{3,2},{4,5},{5,4},{6,7},{7,6},{8,9},{9,8},{10,11... | collective-permute-start | bytes 12296 | tf_op jit(solution)/shard_map/ppermute | solution.py:28
  38.5 9.9 %collective-permute-start.12 = (f32[8,128]{1,0:T(8,128)S(1)}, f32[8,128]{1,0:T(8,128)S(1)}, u32[]{:S(2)}, u32[]{:S(2)}) collective-permute-start(f32[8,128]{1,0:T(8,128)S(1)} %add.16.refs_0_), channel_id=1, source_target_pairs={{0,8},{1,9},{2,10},{3,11},{4,12},{5,13},{6,14},{7,15},{8,0},{9,1},... | collective-permute-start | bytes 12296 | tf_op jit(solution)/shard_map/ppermute | solution.py:28
  41.6 15.3 %collective-permute-start.20 = (f32[64,1152]{1,0:T(8,128)S(1)}, f32[64,1152]{1,0:T(8,128)S(1)}, u32[]{:S(2)}, u32[]{:S(2)}) collective-permute-start(f32[64,1152]{1,0:T(8,128)S(1)} %get-tuple-element.53), channel_id=1, source_target_pairs={{0,4},{1,5},{2,6},{3,7},{4,0},{5,1},{6,2},{7,3},{8,12},{9,13},{10,... | collective-permute-start | bytes 884744 | tf_op jit(solution)/shard_map/ppermute | solution.py:28
  42.9 14.0 %collective-permute-start.21 = (f32[64,1152]{1,0:T(8,128)S(1)}, f32[64,1152]{1,0:T(8,128)S(1)}, u32[]{:S(2)}, u32[]{:S(2)}) collective-permute-start(f32[64,1152]{1,0:T(8,128)S(1)} %shard_map.99), channel_id=1, source_target_pairs={{0,8},{1,9},{2,10},{3,11},{4,12},{5,13},{6,14},{7,15},{8,0},{9,1},... | collective-permute-start | bytes 884744 | tf_op jit(solution)/shard_map/ppermute | solution.py:28
  45.3 11.6 %collective-permute-start.19 = (f32[64,1152]{1,0:T(8,128)S(1)}, f32[64,1152]{1,0:T(8,128)S(1)}, u32[]{:S(2)}, u32[]{:S(2)}) collective-permute-start(f32[64,1152]{1,0:T(8,128)S(1)} %shard_map.100), channel_id=1, source_target_pairs={{0,2},{1,3},{2,0},{3,1},{4,6},{5,7},{6,4},{7,5},{8,10},{9,11},{10,... | collective-permute-start | bytes 884744 | tf_op jit(solution)/shard_map/ppermute | solution.py:28
  46.9 10.0 %copy-start.1 = (f32[64,1152]{1,0:T(8,128)S(1)}, f32[64,1152]{1,0:T(8,128)}, u32[]{:S(2)}) copy-start(f32[64,1152]{1,0:T(8,128)} %refs_4_.1) | copy-start | bytes 884740
  46.9 10.0 %collective-permute-start.18 = (f32[64,1152]{1,0:T(8,128)S(1)}, f32[64,1152]{1,0:T(8,128)S(1)}, u32[]{:S(2)}, u32[]{:S(2)}) collective-permute-start(f32[64,1152]{1,0:T(8,128)S(1)} %get-tuple-element.50), channel_id=1, source_target_pairs={{0,16},{1,17},{2,18},{3,19},{4,20},{5,21},{6,22},{7,23},{8,24},{9,... | collective-permute-start | bytes 884744 | tf_op jit(solution)/shard_map/ppermute | solution.py:28
  48.4 4.9 %collective-permute-start.14 = (f32[8,128]{1,0:T(8,128)S(1)}, f32[8,128]{1,0:T(8,128)S(1)}, u32[]{:S(2)}, u32[]{:S(2)}) collective-permute-start(f32[8,128]{1,0:T(8,128)S(1)} %shard_map.98), channel_id=1, source_target_pairs={{0,2},{1,3},{2,0},{3,1},{4,6},{5,7},{6,4},{7,5},{8,10},{9,11},{10,... | collective-permute-start | bytes 12296 | tf_op jit(solution)/shard_map/ppermute | solution.py:28
  53.3 3.6 %collective-permute-start.15 = (f32[8,128]{1,0:T(8,128)S(1)}, f32[8,128]{1,0:T(8,128)S(1)}, u32[]{:S(2)}, u32[]{:S(2)}) collective-permute-start(f32[8,128]{1,0:T(8,128)S(1)} %add.17), channel_id=1, source_target_pairs={{0,16},{1,17},{2,18},{3,19},{4,20},{5,21},{6,22},{7,23},{8,24},{9,... | collective-permute-start | bytes 12296 | tf_op jit(solution)/shard_map/ppermute | solution.py:28
  (2 other events, 18.9 us)

commit v7 on v5

--- a/solution.py
+++ b/solution.py
@@ -21,7 +21,7 @@
     image, text = [], []
     for bit in range(1, count.bit_length() - 1):
         (text if bit in (2, 3) or bit > 4 and bit % 2 else image).append(1 << bit)
-    return image + [1], text[::-1]
+    return image[::-1] + [1], text[::-1]
 
 
 def exchange(value, step, count):

time: 58.2 us -> 58.2 us (level)
  no operation moved by 1% of the time
where the time goes in v7:
time: 58.2 us; the launch traced here: 58 us
  starting transfers between devices  26.4 us (45%)
  waiting for transfers between devices  20.5 us (35%)
  Pallas kernels  8.92 us (15%)
  between operations  2.07 us (4%)
    ppermute x22, starting transfers between devices, exchange(): return lax.ppermute(value, AXES, [(i, i ^ step) for i in range(count)])  26.4 us
    ppermute x22, waiting for transfers between devices, exchange(): return lax.ppermute(value, AXES, [(i, i ^ step) for i in range(count)])  20.5 us
    pallas_call x2, Pallas kernels, tile(): pl.pallas_call(functools.partial(tile_kernel, places, normed, len(blocks)...  5.68 us
    pallas_call x1, Pallas kernels, pack(): pl.pallas_call(pack_kernel, out_shape=[jax.ShapeDtypeStruct((pieces + mor...  1.93 us
  transfers between devices with their start and end apart: 22, of which 9 were waited for; matrix products, arithmetic and copies ran while one was open for 0% of the time, Pallas kernels for 7%

profile of v7, /device:TPU:0, one launch (start us, length us, event | category | flops | bytes accessed | tf_op | source)
XLA Modules:
  0.0 58.0 jit_solution(16767655911152764600)
XLA Ops:
  0.6 1.9 %shard_map.93 = (f32[577,128]{1,0:T(8,128)}, f32[584,128]{1,0:T(8,128)}) custom-call(f32[64,1152]{1,0:T(8,128)} %refs_0_.1, f32[64,1152]{1,0:T(8,128)} %refs_4_.1, s32[1,64]{1,0:T(1,128)} %bitcast.2), custom_call_target="tpu_custom_call" | custom-call | tf_op jit(solution)/shard_map/pallas_call | solution.py:89
  2.6 4.1 %collective-permute-start = (f32[584,128]{1,0:T(8,128)}, f32[584,128]{1,0:T(8,128)S(1)}, u32[]{:S(2)}, u32[]{:S(2)}) collective-permute-start(f32[584,128]{1,0:T(8,128)} %get-tuple-element.32.refs_0_), channel_id=1, source_target_pairs={{0,8},{1,9},{2,10},{3,11},{4,12},{5,13},{6,14},{7,15},{8,0},{9,1},... | collective-permute-start | bytes 897032 | tf_op jit(solution)/shard_map/ppermute | solution.py:28
  6.7 1.5 %collective-permute-start.3 = (f32[577,128]{1,0:T(8,128)}, f32[577,128]{1,0:T(8,128)S(1)}, u32[]{:S(2)}, u32[]{:S(2)}) collective-permute-start(f32[577,128]{1,0:T(8,128)} %get-tuple-element.34.refs_4_), channel_id=1, source_target_pairs={{0,16},{1,17},{2,18},{3,19},{4,20},{5,21},{6,22},{7,23},{8,24},{9,... | collective-permute-start | bytes 886280 | tf_op jit(solution)/shard_map/ppermute | solution.py:28
  8.2 1.6 %collective-permute-start.2 = (f32[584,128]{1,0:T(8,128)}, f32[584,128]{1,0:T(8,128)S(1)}, u32[]{:S(2)}, u32[]{:S(2)}) collective-permute-start(f32[584,128]{1,0:T(8,128)} %get-tuple-element.32.refs_0_), channel_id=1, source_target_pairs={{0,4},{1,5},{2,6},{3,7},{4,0},{5,1},{6,2},{7,3},{8,12},{9,13},{10,... | collective-permute-start | bytes 897032 | tf_op jit(solution)/shard_map/ppermute | solution.py:28
  9.7 1.5 %collective-permute-start.4 = (f32[577,128]{1,0:T(8,128)}, f32[577,128]{1,0:T(8,128)S(1)}, u32[]{:S(2)}, u32[]{:S(2)}) collective-permute-start(f32[577,128]{1,0:T(8,128)} %get-tuple-element.34.refs_4_), channel_id=1, source_target_pairs={{0,2},{1,3},{2,0},{3,1},{4,6},{5,7},{6,4},{7,5},{8,10},{9,11},{10,... | collective-permute-start | bytes 886280 | tf_op jit(solution)/shard_map/ppermute | solution.py:28
  12.6 2.8 %collective-permute-done.3.refs_5_ = f32[577,128]{1,0:T(8,128)S(1)} collective-permute-done((f32[577,128]{1,0:T(8,128)}, f32[577,128]{1,0:T(8,128)S(1)}, u32[]{:S(2)}, u32[]{:S(2)}) %collective-permute-start.3) | collective-permute-done | bytes 295456 | tf_op jit(solution)/shard_map/ppermute | solution.py:28
  15.4 1.5 %collective-permute-start.5 = (f32[577,128]{1,0:T(8,128)S(1)}, f32[577,128]{1,0:T(8,128)S(1)}, u32[]{:S(2)}, u32[]{:S(2)}) collective-permute-start(f32[577,128]{1,0:T(8,128)S(1)} %collective-permute-done.3.refs_5_), channel_id=1, source_target_pairs={{0,2},{1,3},{2,0},{3,1},{4,6},{5,7},{6,4},{7,5},{8,10},{9,11},{10,... | collective-permute-start | bytes 886280 | tf_op jit(solution)/shard_map/ppermute | solution.py:28
  17.0 3.5 %collective-permute-done.block_ref.refs_1_ = f32[584,128]{1,0:T(8,128)S(1)} collective-permute-done((f32[584,128]{1,0:T(8,128)}, f32[584,128]{1,0:T(8,128)S(1)}, u32[]{:S(2)}, u32[]{:S(2)}) %collective-permute-start) | collective-permute-done | bytes 299040 | tf_op jit(solution)/shard_map/ppermute | solution.py:28
  22.0 2.3 %collective-permute-done.5.refs_7_ = f32[577,128]{1,0:T(8,128)S(1)} collective-permute-done((f32[577,128]{1,0:T(8,128)S(1)}, f32[577,128]{1,0:T(8,128)S(1)}, u32[]{:S(2)}, u32[]{:S(2)}) %collective-permute-start.5) | collective-permute-done | bytes 295456 | tf_op jit(solution)/shard_map/ppermute | solution.py:28
  24.4 1.6 %collective-permute-done.9.refs_11_ = f32[577,128]{1,0:T(8,128)S(1)} collective-permute-done((f32[577,128]{1,0:T(8,128)S(1)}, f32[577,128]{1,0:T(8,128)S(1)}, u32[]{:S(2)}, u32[]{:S(2)}) %collective-permute-start.9) | collective-permute-done | bytes 295456 | tf_op jit(solution)/shard_map/ppermute | solution.py:28
  25.9 3.8 %shard_map.95 = (bf16[512,1152]{1,0:T(8,128)(2,1)S(1)}, bf16[512,1152]{1,0:T(8,128)(2,1)S(1)}, f32[8,512]{1,0:T(8,128)S(1)}, f32[64,1152]{1,0:T(8,128)S(1)}, f32...) custom-call(f32[8,128]{1,0:T(8,128)S(1)} %shard_map.92.fixed_ref, ...), custom_call_target="tpu_custom_call" | custom-call | tf_op jit(solution)/shard_map/pallas_call | solution.py:215
  29.8 1.9 %shard_map.96 = (f32[64,1152]{1,0:T(8,128)S(1)}, f32[256,1152]{1,0:T(8,128)S(1)}, f32[256,1152]{1,0:T(8,128)S(1)}, f32[8,128]{1,0:T(8,128)S(1)}) custom-call(f32[8,128]{1,0:T(8,128)S(1)} %shard_map.92.fixed_ref, f32[584,128]{1,0:T(8,128)S(1)} %collective-permute-done.1.refs_0_, bf16[512,1152]{1,0:T(8,128)(2,1)S(1)} %get-tuple-element.37.refs_1_, ...), custom_call_target="tpu_custom_call" | custom-call | tf_op jit(solution)/shard_map/pallas_call | solution.py:215
  32.5 1.4 %collective-permute-start.13 = (f32[64,1152]{1,0:T(8,128)S(1)}, f32[64,1152]{1,0:T(8,128)S(1)}, u32[]{:S(2)}, u32[]{:S(2)}) collective-permute-start(f32[64,1152]{1,0:T(8,128)S(1)} %get-tuple-element.45), channel_id=1, source_target_pairs={{0,4},{1,5},{2,6},{3,7},{4,0},{5,1},{6,2},{7,3},{8,12},{9,13},{10,... | collective-permute-start | bytes 884744 | tf_op jit(solution)/shard_map/ppermute | solution.py:28
  33.9 1.6 %collective-permute-done.10.refs_1_ = f32[8,128]{1,0:T(8,128)S(1)} collective-permute-done((f32[8,128]{1,0:T(8,128)S(1)}, f32[8,128]{1,0:T(8,128)S(1)}, u32[]{:S(2)}, u32[]{:S(2)}) %collective-permute-start.10) | collective-permute-done | bytes 4128 | tf_op jit(solution)/shard_map/ppermute | solution.py:28
  35.7 1.6 %collective-permute-start.17 = (f32[64,1152]{1,0:T(8,128)S(1)}, f32[64,1152]{1,0:T(8,128)S(1)}, u32[]{:S(2)}, u32[]{:S(2)}) collective-permute-start(f32[64,1152]{1,0:T(8,128)S(1)} %get-tuple-element.60), channel_id=1, source_target_pairs={{0,2},{1,3},{2,0},{3,1},{4,6},{5,7},{6,4},{7,5},{8,10},{9,11},{10,... | collective-permute-start | bytes 884744 | tf_op jit(solution)/shard_map/ppermute | solution.py:28
  37.3 1.2 %collective-permute-done.11 = f32[8,128]{1,0:T(8,128)S(1)} collective-permute-done((f32[8,128]{1,0:T(8,128)S(1)}, f32[8,128]{1,0:T(8,128)S(1)}, u32[]{:S(2)}, u32[]{:S(2)}) %collective-permute-start.11) | collective-permute-done | bytes 4128 | tf_op jit(solution)/shard_map/ppermute | solution.py:28
  38.5 2.1 %collective-permute-start.12 = (f32[8,128]{1,0:T(8,128)S(1)}, f32[8,128]{1,0:T(8,128)S(1)}, u32[]{:S(2)}, u32[]{:S(2)}) collective-permute-start(f32[8,128]{1,0:T(8,128)S(1)} %add.16.refs_0_), channel_id=1, source_target_pairs={{0,8},{1,9},{2,10},{3,11},{4,12},{5,13},{6,14},{7,15},{8,0},{9,1},... | collective-permute-start | bytes 12296 | tf_op jit(solution)/shard_map/ppermute | solution.py:28
  41.6 1.3 %collective-permute-start.20 = (f32[64,1152]{1,0:T(8,128)S(1)}, f32[64,1152]{1,0:T(8,128)S(1)}, u32[]{:S(2)}, u32[]{:S(2)}) collective-permute-start(f32[64,1152]{1,0:T(8,128)S(1)} %get-tuple-element.53), channel_id=1, source_target_pairs={{0,4},{1,5},{2,6},{3,7},{4,0},{5,1},{6,2},{7,3},{8,12},{9,13},{10,... | collective-permute-start | bytes 884744 | tf_op jit(solution)/shard_map/ppermute | solution.py:28
  42.9 2.4 %collective-permute-start.21 = (f32[64,1152]{1,0:T(8,128)S(1)}, f32[64,1152]{1,0:T(8,128)S(1)}, u32[]{:S(2)}, u32[]{:S(2)}) collective-permute-start(f32[64,1152]{1,0:T(8,128)S(1)} %shard_map.99), channel_id=1, source_target_pairs={{0,8},{1,9},{2,10},{3,11},{4,12},{5,13},{6,14},{7,15},{8,0},{9,1},... | collective-permute-start | bytes 884744 | tf_op jit(solution)/shard_map/ppermute | solution.py:28
  45.3 1.5 %collective-permute-start.19 = (f32[64,1152]{1,0:T(8,128)S(1)}, f32[64,1152]{1,0:T(8,128)S(1)}, u32[]{:S(2)}, u32[]{:S(2)}) collective-permute-start(f32[64,1152]{1,0:T(8,128)S(1)} %shard_map.100), channel_id=1, source_target_pairs={{0,16},{1,17},{2,18},{3,19},{4,20},{5,21},{6,22},{7,23},{8,24},{9,... | collective-permute-start | bytes 884744 | tf_op jit(solution)/shard_map/ppermute | solution.py:28
  46.8 1.6 %collective-permute-start.18 = (f32[64,1152]{1,0:T(8,128)S(1)}, f32[64,1152]{1,0:T(8,128)S(1)}, u32[]{:S(2)}, u32[]{:S(2)}) collective-permute-start(f32[64,1152]{1,0:T(8,128)S(1)} %get-tuple-element.50), channel_id=1, source_target_pairs={{0,2},{1,3},{2,0},{3,1},{4,6},{5,7},{6,4},{7,5},{8,10},{9,11},{10,... | collective-permute-start | bytes 884744 | tf_op jit(solution)/shard_map/ppermute | solution.py:28
  49.0 4.3 %collective-permute-done.14 = f32[8,128]{1,0:T(8,128)S(1)} collective-permute-done((f32[8,128]{1,0:T(8,128)S(1)}, f32[8,128]{1,0:T(8,128)S(1)}, u32[]{:S(2)}, u32[]{:S(2)}) %collective-permute-start.14) | collective-permute-done | bytes 4128 | tf_op jit(solution)/shard_map/ppermute | solution.py:28
  53.3 1.5 %collective-permute-start.15 = (f32[8,128]{1,0:T(8,128)S(1)}, f32[8,128]{1,0:T(8,128)S(1)}, u32[]{:S(2)}, u32[]{:S(2)}) collective-permute-start(f32[8,128]{1,0:T(8,128)S(1)} %add.17), channel_id=1, source_target_pairs={{0,2},{1,3},{2,0},{3,1},{4,6},{5,7},{6,4},{7,5},{8,10},{9,11},{10,... | collective-permute-start | bytes 12296 | tf_op jit(solution)/shard_map/ppermute | solution.py:28
  54.8 2.1 %collective-permute-done.15 = f32[8,128]{1,0:T(8,128)S(1)} collective-permute-done((f32[8,128]{1,0:T(8,128)S(1)}, f32[8,128]{1,0:T(8,128)S(1)}, u32[]{:S(2)}, u32[]{:S(2)}) %collective-permute-start.15) | collective-permute-done | bytes 4128 | tf_op jit(solution)/shard_map/ppermute | solution.py:28
  (43 shorter events, 5.4 us)
Async XLA Ops:
  2.6 17.9 %collective-permute-start = (f32[584,128]{1,0:T(8,128)}, f32[584,128]{1,0:T(8,128)S(1)}, u32[]{:S(2)}, u32[]{:S(2)}) collective-permute-start(f32[584,128]{1,0:T(8,128)} %get-tuple-element.32.refs_0_), channel_id=1, source_target_pairs={{0,8},{1,9},{2,10},{3,11},{4,12},{5,13},{6,14},{7,15},{8,0},{9,1},... | collective-permute-start | bytes 897032 | tf_op jit(solution)/shard_map/ppermute | solution.py:28
  6.7 8.8 %collective-permute-start.3 = (f32[577,128]{1,0:T(8,128)}, f32[577,128]{1,0:T(8,128)S(1)}, u32[]{:S(2)}, u32[]{:S(2)}) collective-permute-start(f32[577,128]{1,0:T(8,128)} %get-tuple-element.34.refs_4_), channel_id=1, source_target_pairs={{0,16},{1,17},{2,18},{3,19},{4,20},{5,21},{6,22},{7,23},{8,24},{9,... | collective-permute-start | bytes 886280 | tf_op jit(solution)/shard_map/ppermute | solution.py:28
  8.2 13.8 %collective-permute-start.2 = (f32[584,128]{1,0:T(8,128)}, f32[584,128]{1,0:T(8,128)S(1)}, u32[]{:S(2)}, u32[]{:S(2)}) collective-permute-start(f32[584,128]{1,0:T(8,128)} %get-tuple-element.32.refs_0_), channel_id=1, source_target_pairs={{0,4},{1,5},{2,6},{3,7},{4,0},{5,1},{6,2},{7,3},{8,12},{9,13},{10,... | collective-permute-start | bytes 897032 | tf_op jit(solution)/shard_map/ppermute | solution.py:28
  9.7 11.7 %collective-permute-start.4 = (f32[577,128]{1,0:T(8,128)}, f32[577,128]{1,0:T(8,128)S(1)}, u32[]{:S(2)}, u32[]{:S(2)}) collective-permute-start(f32[577,128]{1,0:T(8,128)} %get-tuple-element.34.refs_4_), channel_id=1, source_target_pairs={{0,2},{1,3},{2,0},{3,1},{4,6},{5,7},{6,4},{7,5},{8,10},{9,11},{10,... | collective-permute-start | bytes 886280 | tf_op jit(solution)/shard_map/ppermute | solution.py:28
  12.6 13.4 %copy-start.3 = (f32[584,128]{1,0:T(8,128)S(1)}, f32[584,128]{1,0:T(8,128)}, u32[]{:S(2)}) copy-start(f32[584,128]{1,0:T(8,128)} %get-tuple-element.32.refs_0_) | copy-start | bytes 897028
  15.4 8.9 %collective-permute-start.5 = (f32[577,128]{1,0:T(8,128)S(1)}, f32[577,128]{1,0:T(8,128)S(1)}, u32[]{:S(2)}, u32[]{:S(2)}) collective-permute-start(f32[577,128]{1,0:T(8,128)S(1)} %collective-permute-done.3.refs_5_), channel_id=1, source_target_pairs={{0,2},{1,3},{2,0},{3,1},{4,6},{5,7},{6,4},{7,5},{8,10},{9,11},{10,... | collective-permute-start | bytes 886280 | tf_op jit(solution)/shard_map/ppermute | solution.py:28
  20.6 9.2 %collective-permute-start.1 = (f32[584,128]{1,0:T(8,128)S(1)}, f32[584,128]{1,0:T(8,128)S(1)}, u32[]{:S(2)}, u32[]{:S(2)}) collective-permute-start(f32[584,128]{1,0:T(8,128)S(1)} %collective-permute-done.block_ref.refs_1_), channel_id=1, source_target_pairs={{0,4},{1,5},{2,6},{3,7},{4,0},{5,1},{6,2},{7,3},{8,12},{9,13},{10,... | collective-permute-start | bytes 897032 | tf_op jit(solution)/shard_map/ppermute | solution.py:28
  21.4 2.9 %collective-permute-start.6 = (f32[577,128]{1,0:T(8,128)S(1)}, f32[577,128]{1,0:T(8,128)S(1)}, u32[]{:S(2)}, u32[]{:S(2)}) collective-permute-start(f32[577,128]{1,0:T(8,128)S(1)} %copy-done.2), channel_id=1, source_target_pairs={{0,1},{1,0},{2,3},{3,2},{4,5},{5,4},{6,7},{7,6},{8,9},{9,8},{10,11... | collective-permute-start | bytes 886280 | tf_op jit(solution)/shard_map/ppermute | solution.py:28
  21.4 2.9 %collective-permute-start.7 = (f32[577,128]{1,0:T(8,128)S(1)}, f32[577,128]{1,0:T(8,128)S(1)}, u32[]{:S(2)}, u32[]{:S(2)}) collective-permute-start(f32[577,128]{1,0:T(8,128)S(1)} %collective-permute-done.3.refs_5_), channel_id=1, source_target_pairs={{0,1},{1,0},{2,3},{3,2},{4,5},{5,4},{6,7},{7,6},{8,9},{9,8},{10,11... | collective-permute-start | bytes 886280 | tf_op jit(solution)/shard_map/ppermute | solution.py:28
  22.0 2.4 %collective-permute-start.8 = (f32[577,128]{1,0:T(8,128)S(1)}, f32[577,128]{1,0:T(8,128)S(1)}, u32[]{:S(2)}, u32[]{:S(2)}) collective-permute-start(f32[577,128]{1,0:T(8,128)S(1)} %collective-permute-done.4.refs_6_), channel_id=1, source_target_pairs={{0,1},{1,0},{2,3},{3,2},{4,5},{5,4},{6,7},{7,6},{8,9},{9,8},{10,11... | collective-permute-start | bytes 886280 | tf_op jit(solution)/shard_map/ppermute | solution.py:28
  24.4 1.6 %collective-permute-start.9 = (f32[577,128]{1,0:T(8,128)S(1)}, f32[577,128]{1,0:T(8,128)S(1)}, u32[]{:S(2)}, u32[]{:S(2)}) collective-permute-start(f32[577,128]{1,0:T(8,128)S(1)} %collective-permute-done.5.refs_7_), channel_id=1, source_target_pairs={{0,1},{1,0},{2,3},{3,2},{4,5},{5,4},{6,7},{7,6},{8,9},{9,8},{10,11... | collective-permute-start | bytes 886280 | tf_op jit(solution)/shard_map/ppermute | solution.py:28
  31.7 3.9 %collective-permute-start.16 = (f32[256,1152]{1,0:T(8,128)S(1)}, f32[256,1152]{1,0:T(8,128)S(1)}, u32[]{:S(2)}, u32[]{:S(2)}) collective-permute-start(f32[256,1152]{1,0:T(8,128)S(1)} %get-tuple-element.48), channel_id=1, source_target_pairs={{0,1},{1,0},{2,3},{3,2},{4,5},{5,4},{6,7},{7,6},{8,9},{9,8},{10,11... | collective-permute-start | bytes 3538952 | tf_op jit(solution)/shard_map/ppermute | solution.py:28
  31.9 3.7 %collective-permute-start.10 = (f32[8,128]{1,0:T(8,128)S(1)}, f32[8,128]{1,0:T(8,128)S(1)}, u32[]{:S(2)}, u32[]{:S(2)}) collective-permute-start(f32[8,128]{1,0:T(8,128)S(1)} %get-tuple-element.43.refs_0_), channel_id=1, source_target_pairs={{0,4},{1,5},{2,6},{3,7},{4,0},{5,1},{6,2},{7,3},{8,12},{9,13},{10,... | collective-permute-start | bytes 12296 | tf_op jit(solution)/shard_map/ppermute | solution.py:28
  32.5 9.1 %collective-permute-start.13 = (f32[64,1152]{1,0:T(8,128)S(1)}, f32[64,1152]{1,0:T(8,128)S(1)}, u32[]{:S(2)}, u32[]{:S(2)}) collective-permute-start(f32[64,1152]{1,0:T(8,128)S(1)} %get-tuple-element.45), channel_id=1, source_target_pairs={{0,4},{1,5},{2,6},{3,7},{4,0},{5,1},{6,2},{7,3},{8,12},{9,13},{10,... | collective-permute-start | bytes 884744 | tf_op jit(solution)/shard_map/ppermute | solution.py:28
  35.7 9.6 %collective-permute-start.17 = (f32[64,1152]{1,0:T(8,128)S(1)}, f32[64,1152]{1,0:T(8,128)S(1)}, u32[]{:S(2)}, u32[]{:S(2)}) collective-permute-start(f32[64,1152]{1,0:T(8,128)S(1)} %get-tuple-element.60), channel_id=1, source_target_pairs={{0,2},{1,3},{2,0},{3,1},{4,6},{5,7},{6,4},{7,5},{8,10},{9,11},{10,... | collective-permute-start | bytes 884744 | tf_op jit(solution)/shard_map/ppermute | solution.py:28
  37.3 1.2 %collective-permute-start.11 = (f32[8,128]{1,0:T(8,128)S(1)}, f32[8,128]{1,0:T(8,128)S(1)}, u32[]{:S(2)}, u32[]{:S(2)}) collective-permute-start(f32[8,128]{1,0:T(8,128)S(1)} %shard_map.97), channel_id=1, source_target_pairs={{0,1},{1,0},{2,3},{3,2},{4,5},{5,4},{6,7},{7,6},{8,9},{9,8},{10,11... | collective-permute-start | bytes 12296 | tf_op jit(solution)/shard_map/ppermute | solution.py:28
  38.5 9.9 %collective-permute-start.12 = (f32[8,128]{1,0:T(8,128)S(1)}, f32[8,128]{1,0:T(8,128)S(1)}, u32[]{:S(2)}, u32[]{:S(2)}) collective-permute-start(f32[8,128]{1,0:T(8,128)S(1)} %add.16.refs_0_), channel_id=1, source_target_pairs={{0,8},{1,9},{2,10},{3,11},{4,12},{5,13},{6,14},{7,15},{8,0},{9,1},... | collective-permute-start | bytes 12296 | tf_op jit(solution)/shard_map/ppermute | solution.py:28
  41.6 15.3 %collective-permute-start.20 = (f32[64,1152]{1,0:T(8,128)S(1)}, f32[64,1152]{1,0:T(8,128)S(1)}, u32[]{:S(2)}, u32[]{:S(2)}) collective-permute-start(f32[64,1152]{1,0:T(8,128)S(1)} %get-tuple-element.53), channel_id=1, source_target_pairs={{0,4},{1,5},{2,6},{3,7},{4,0},{5,1},{6,2},{7,3},{8,12},{9,13},{10,... | collective-permute-start | bytes 884744 | tf_op jit(solution)/shard_map/ppermute | solution.py:28
  42.9 14.0 %collective-permute-start.21 = (f32[64,1152]{1,0:T(8,128)S(1)}, f32[64,1152]{1,0:T(8,128)S(1)}, u32[]{:S(2)}, u32[]{:S(2)}) collective-permute-start(f32[64,1152]{1,0:T(8,128)S(1)} %shard_map.99), channel_id=1, source_target_pairs={{0,8},{1,9},{2,10},{3,11},{4,12},{5,13},{6,14},{7,15},{8,0},{9,1},... | collective-permute-start | bytes 884744 | tf_op jit(solution)/shard_map/ppermute | solution.py:28
  45.3 11.6 %collective-permute-start.19 = (f32[64,1152]{1,0:T(8,128)S(1)}, f32[64,1152]{1,0:T(8,128)S(1)}, u32[]{:S(2)}, u32[]{:S(2)}) collective-permute-start(f32[64,1152]{1,0:T(8,128)S(1)} %shard_map.100), channel_id=1, source_target_pairs={{0,16},{1,17},{2,18},{3,19},{4,20},{5,21},{6,22},{7,23},{8,24},{9,... | collective-permute-start | bytes 884744 | tf_op jit(solution)/shard_map/ppermute | solution.py:28
  46.8 10.1 %copy-start.1 = (f32[64,1152]{1,0:T(8,128)S(1)}, f32[64,1152]{1,0:T(8,128)}, u32[]{:S(2)}) copy-start(f32[64,1152]{1,0:T(8,128)} %refs_4_.1) | copy-start | bytes 884740
  46.8 10.0 %collective-permute-start.18 = (f32[64,1152]{1,0:T(8,128)S(1)}, f32[64,1152]{1,0:T(8,128)S(1)}, u32[]{:S(2)}, u32[]{:S(2)}) collective-permute-start(f32[64,1152]{1,0:T(8,128)S(1)} %get-tuple-element.50), channel_id=1, source_target_pairs={{0,2},{1,3},{2,0},{3,1},{4,6},{5,7},{6,4},{7,5},{8,10},{9,11},{10,... | collective-permute-start | bytes 884744 | tf_op jit(solution)/shard_map/ppermute | solution.py:28
  48.4 4.8 %collective-permute-start.14 = (f32[8,128]{1,0:T(8,128)S(1)}, f32[8,128]{1,0:T(8,128)S(1)}, u32[]{:S(2)}, u32[]{:S(2)}) collective-permute-start(f32[8,128]{1,0:T(8,128)S(1)} %shard_map.98), channel_id=1, source_target_pairs={{0,16},{1,17},{2,18},{3,19},{4,20},{5,21},{6,22},{7,23},{8,24},{9,... | collective-permute-start | bytes 12296 | tf_op jit(solution)/shard_map/ppermute | solution.py:28
  53.3 3.6 %collective-permute-start.15 = (f32[8,128]{1,0:T(8,128)S(1)}, f32[8,128]{1,0:T(8,128)S(1)}, u32[]{:S(2)}, u32[]{:S(2)}) collective-permute-start(f32[8,128]{1,0:T(8,128)S(1)} %add.17), channel_id=1, source_target_pairs={{0,2},{1,3},{2,0},{3,1},{4,6},{5,7},{6,4},{7,5},{8,10},{9,11},{10,... | collective-permute-start | bytes 12296 | tf_op jit(solution)/shard_map/ppermute | solution.py:28
  (2 other events, 18.9 us)
